TPU v7x, 256 devices: a whole 4x4x8 slice. The times are simulated.
256 devices in a mesh: blk: 32 (over x_hi, z, core), col: 8 (over x_lo, y).
Axes of the slice: x: 4 (x_hi: 2, x_lo: 2; x = x_hi * 2 + x_lo), y: 4, z: 8, core: 2. Of those that a mesh axis runs over, the one named last changes fastest.
Arguments:
- amplitudes: bfloat16 [1024, 32768], P('blk', 'col'), may hold values from -6 to 6
- integrals: bfloat16 [32768, 32768], P('blk', 'col'), may hold values from -0.03125 to 0.03125
- amp_mask: int32 [1024, 256], P('blk', 'col'), may hold values 0 or 1
- int_mask: int32 [256, 256], P('blk', 'col'), may hold values 0 or 1
Outputs:
- ladder: bfloat16 [1024, 32768], P('col', 'blk')
All inputs are finite; a program needn't handle non-finite values. No bound on the sum of `amp_mask` or of `int_mask` on one device may be relied on, other than what follows from the above.
Results may differ from a plain program's by a relative error of at most 0.001.
Values may be sent and summed in bfloat16 or wider, within the bound.
No kernel may reach another device: no remote copies, remote signals or barrier semaphores. Data moves between devices by JAX's collectives and lax.ppermute only.
A program may use at most 64 MiB of HBM per device.

v0:
```python
import jax
import jax.numpy as jnp
from jax import lax
from jax.sharding import PartitionSpec as P

TILE = 128


def local(amplitudes, integrals, amp_mask, int_mask):
    row_count, col_count = integrals.shape
    kept_ints = (
        integrals.reshape(row_count // TILE, TILE, col_count // TILE, TILE)
        * int_mask.astype(jnp.bfloat16)[:, None, :, None]
    ).reshape(row_count, col_count)
    pair_local = amplitudes.shape[0]
    kept_amps = (
        amplitudes.reshape(pair_local, col_count // TILE, TILE)
        * amp_mask.astype(jnp.bfloat16)[:, :, None]
    ).reshape(pair_local, col_count)
    partial_value = lax.dot_general(
        lax.all_gather(kept_amps, "blk", axis=0, tiled=True),
        kept_ints,
        (((1,), (1,)), ((), ())),
        preferred_element_type=jnp.float32,
    )
    summed = lax.psum_scatter(partial_value, "col", scatter_dimension=0, tiled=True)
    return summed.astype(jnp.bfloat16)


def solution(mesh):
    in_specs = (P("blk", "col"), P("blk", "col"), P("blk", "col"), P("blk", "col"))
    out_specs = P("col", "blk")
    return jax.shard_map(local, mesh=mesh, in_specs=in_specs, out_specs=out_specs, check_vma=False)
```

profile of v0, /device:TPU:24, one launch (start us, length us, event | category | flops | bytes accessed | tf_op | source)
XLA Modules:
  0.0 194.3 jit_solution(4409363255665506363)
XLA Ops:
  6.5 0.0 all-gather.2.cloned.1.call-start
  6.5 0.7 convert_element_type.9
  7.3 0.2 mul.22
  7.5 1.8 bitcast_multiply_fusion.2
  9.2 0.0 all-gather.2.cloned.1.call-update
  9.3 0.0 reduce-scatter.2.cloned.1.call-start
  9.3 0.7 convert_element_type.10
  10.0 104.3 %all-gather.2.cloned.1.call-done = bf16[1024,4096]{1,0:T(8,128)(2,1)} async-done(((bf16[32,4096]{1,0:T(8,128)(2,1)}), bf16[1024,4096]{1,0:T(8,128)(2,1)}) %all-gather.2.cloned.1.call-update) | async-done | bytes 8388624 | tf_op jit(solution)/shard_map/all_gather | solution.py:21
  114.3 1.1 mul.25
  115.4 20.1 %fusion = f32[1024,1024]{1,0:T(8,128)} fusion(bf16[1024,4096]{1,0:T(8,128)(2,1)} %all-gather.2.cloned.1.call-done, bf16[1024,4096]{1,0:T(8,128)(2,1)} %param.5, bf16[128,8,32,128]{3,2,1,0:T(8,128)(2,1)S(1)} %bitcast.9), kind=kOutput, calls=%fused_computation.1 | convolution fusion | flops 8594128896 | bytes 29360128 | tf_op jit(solution)/shard_map/dot_general | solution.py:20
  135.6 0.0 reduce-scatter.2.cloned.1.call-update
  135.6 50.1 %reduce-scatter.2.cloned.1.call-done = f32[128,1024]{1,0:T(8,128)} async-done(((f32[1024,1024]{1,0:T(8,128)}), f32[128,1024]{1,0:T(8,128)}) %reduce-scatter.2.cloned.1.call-update) | async-done | bytes 524304 | tf_op jit(solution)/shard_map/reduce_scatter | solution.py:26
  185.7 1.8 convert_element_type.11
Async XLA Ops:
  6.5 107.8 %all-gather.2.cloned.1.call-start = ((), (), s32[]{:S(2)}) async-start(), calls=%async_computation.1 | async-start | bytes 8650752 | tf_op jit(solution)/shard_map/all_gather | solution.py:21
  9.3 176.4 %reduce-scatter.2.cloned.1.call-start = ((), (), s32[]{:S(2)}) async-start(), calls=%async_computation.2 | async-start | bytes 4718592 | tf_op jit(solution)/shard_map/reduce_scatter | solution.py:26
Sparse Core Ops, SparseCore 0:
  10.1 104.1 all-gather.1
  135.7 49.9 reduce-scatter.1
where the time goes:
time: 198 us; the launch traced here: 194 us
  waiting for transfers between devices  154 us (78%)
  matrix products  20.1 us (10%)
  between operations  13.4 us (7%)
  other arithmetic  4.96 us (3%)
    all_gather x1, waiting for transfers between devices, local(): lax.all_gather(kept_amps, 'blk', axis=0, tiled=True)  104 us
    reduce_scatter x1, waiting for transfers between devices, local(): lax.psum_scatter(partial_value, 'col', scatter_dimension=0, tiled=True)  50.1 us
    dot_general x1, matrix products, local(): lax.dot_general(lax.all_gather(kept_amps, 'blk', axis=0, tiled=True), kep...  20.1 us
  transfers between devices with their start and end apart: 2, of which 2 were waited for; matrix products, arithmetic and copies ran while one was open for 0% of the time, Pallas kernels for 0%

commit v1 on v0

v1 whole, which is shorter than its diff:
```python
import jax
import jax.numpy as jnp
from jax import lax
from jax.experimental import pallas as pl
from jax.experimental.pallas import tpu as pltpu
from jax.sharding import Mesh, PartitionSpec as P

TILE = 128
OWN = 32
TILES = 32
GROUP = 8
WIN = 256
LOW = (0, 80, 240, 320)
ROWS = 576
MSG = ROWS + OWN
F32 = jnp.float32
BF16 = jnp.bfloat16


def swap(x, axis):
    return lax.ppermute(x, axis, [(0, 1), (1, 0)])


def pack_kernel(amps_ref, mask_ref, msg_ref, kept_ref, over_ref, acc):
    mask = mask_ref[...].astype(F32)
    row = lax.broadcasted_iota(jnp.int32, (OWN, OWN), 0)
    col = lax.broadcasted_iota(jnp.int32, (OWN, OWN), 1)
    below = (col < row).astype(BF16)
    mask16 = mask.astype(BF16)
    in_tile = jnp.dot(below, mask16, preferred_element_type=F32)
    count = jnp.dot(jnp.ones((OWN, OWN), BF16), mask16, preferred_element_type=F32)
    same = row // GROUP == col // GROUP
    before = jnp.dot(count.astype(BF16), ((row < col) & same).astype(BF16), preferred_element_type=F32)
    in_group = in_tile + before
    lane = lax.broadcasted_iota(jnp.int32, (OWN, TILES), 1) // GROUP
    total = [
        jnp.sum(jnp.where(lane == g, count, 0.0), axis=1, keepdims=True) for g in range(4)
    ]
    start1 = jnp.maximum(total[0], float(LOW[1]))
    end1 = start1 + total[1]
    start3 = ROWS - total[3]
    start2 = jnp.minimum(start3, float(LOW[2] + WIN)) - total[2]
    over = (end1 > LOW[1] + WIN) | (start2 < LOW[2]) | (end1 > start2)
    over_ref[...] = jnp.broadcast_to(jnp.where(over, 1, 0)[:8], (8, TILE)).astype(jnp.int32)
    offset = jnp.where(
        lane == 0,
        0.0,
        jnp.where(lane == 1, start1 - LOW[1], jnp.where(lane == 2, start2 - LOW[2], start3 - LOW[3])),
    )
    place = jnp.where(mask > 0.0, in_group + offset, -1.0)
    msg_ref[ROWS:MSG, :] = jnp.concatenate([place, jnp.zeros((OWN, TILE - TILES), F32)], axis=1).astype(BF16)
    acc[...] = jnp.zeros_like(acc)
    spots = lax.broadcasted_iota(jnp.int32, (OWN, WIN), 1).astype(F32)
    for g in range(4):
        hot, val = [], []
        for t in range(g * GROUP, (g + 1) * GROUP):
            tile = amps_ref[:, t * TILE : (t + 1) * TILE]
            kept_ref[:, t * TILE : (t + 1) * TILE] = tile * mask16[:, t : t + 1]
            hot.append((place[:, t : t + 1] == spots).astype(BF16))
            val.append(tile)
        hot = jnp.concatenate(hot, axis=0)
        val = jnp.concatenate(val, axis=0)
        acc[LOW[g] : LOW[g] + WIN, :] += lax.dot_general(
            hot, val, (((0,), (0,)), ((), ())), preferred_element_type=F32
        )
    msg_ref[:ROWS, :] = acc[...].astype(BF16)


def pack(amps, mask):
    return pl.pallas_call(
        pack_kernel,
        out_shape=(
            jax.ShapeDtypeStruct((MSG, TILE), BF16),
            jax.ShapeDtypeStruct(amps.shape, BF16),
            jax.ShapeDtypeStruct((8, TILE), jnp.int32),
        ),
        scratch_shapes=[pltpu.VMEM((ROWS, TILE), F32)],
        compiler_params=pltpu.CompilerParams(vmem_limit_bytes=16 << 20),
    )(amps, mask)


def unpack_kernel(core_ref, own_ref, other_ref, out_ref):
    core = core_ref[0]
    spots = lax.broadcasted_iota(jnp.int32, (OWN, WIN), 1).astype(F32)
    for ref, which in ((own_ref, core), (other_ref, 1 - core)):
        rows = pl.ds(pl.multiple_of(which * OWN, OWN), OWN)
        place = ref[0, ROWS:MSG, :].astype(F32)
        for g in range(4):
            hot = jnp.concatenate(
                [(place[:, t : t + 1] == spots).astype(BF16) for t in range(g * GROUP, (g + 1) * GROUP)],
                axis=0,
            )
            got = jnp.dot(hot, ref[0, LOW[g] : LOW[g] + WIN, :], preferred_element_type=F32).astype(BF16)
            for i in range(GROUP):
                t = g * GROUP + i
                out_ref[rows, t * TILE : (t + 1) * TILE] = got[i * OWN : (i + 1) * OWN, :]


def unpack(core, own, other):
    n = own.shape[0]
    return pl.pallas_call(
        unpack_kernel,
        grid=(n,),
        in_specs=[
            pl.BlockSpec(memory_space=pltpu.SMEM),
            pl.BlockSpec((1, MSG, TILE), lambda i: (i, 0, 0)),
            pl.BlockSpec((1, MSG, TILE), lambda i: (i, 0, 0)),
        ],
        out_specs=pl.BlockSpec((2 * OWN, TILES * TILE), lambda i: (i, 0)),
        out_shape=jax.ShapeDtypeStruct((n * 2 * OWN, TILES * TILE), BF16),
        compiler_params=pltpu.CompilerParams(vmem_limit_bytes=16 << 20),
        cost_estimate=pl.CostEstimate(flops=4_000_000_000, bytes_accessed=6 << 20, transcendentals=0),
    )(core, own, other)


def local(amplitudes, integrals, amp_mask, int_mask):
    row_count, col_count = integrals.shape
    msg, kept_amps, over = pack(amplitudes, amp_mask)

    far = swap(msg, "xh")
    gathered = [lax.all_gather(m, "z", axis=0) for m in (msg, far)]

    for axis, size in (("z", 8), ("y", 4)):
        hop = 1
        while hop < size:
            over = jnp.maximum(over, lax.ppermute(over, axis, [(i, (i + hop) % size) for i in range(size)]))
            hop *= 2
    for axis in ("core", "xh", "xl"):
        over = jnp.maximum(over, swap(over, axis))
    full = over[0, 0] > 0

    kept_ints = (
        integrals.reshape(row_count // TILE, TILE, col_count // TILE, TILE)
        * int_mask.astype(BF16)[:, None, :, None]
    ).reshape(row_count, col_count)
    kept_ints = lax.optimization_barrier(kept_ints)

    core = lax.axis_index("core").reshape(1)
    sums = []
    for chunk in range(2):
        own = gathered[chunk]
        other = swap(own, "core")

        def slow(kept, own, other):
            kept = kept if chunk == 0 else swap(kept, "xh")
            return lax.all_gather(kept, ("z", "core"), axis=0, tiled=True)

        amps = lax.cond(full, slow, lambda kept, own, other: unpack(core, own, other), kept_amps, own, other)
        partial_value = lax.dot_general(amps, kept_ints, (((1,), (1,)), ((), ())), preferred_element_type=F32)
        parts = lax.all_to_all(partial_value.reshape(4, -1, row_count), "y", 0, 0)
        sums.append(jnp.sum(parts, axis=0))
    near = lax.axis_index("xl") == lax.axis_index("xh")
    mine = jnp.where(near, sums[0], sums[1])
    sent = jnp.where(near, sums[1], sums[0])
    return (mine + swap(sent, "xl")).astype(BF16)


def solution(mesh):
    fine = Mesh(mesh.devices.reshape(2, 8, 2, 2, 4), ("xh", "z", "core", "xl", "y"))
    blk, col = ("xh", "z", "core"), ("xl", "y")
    return jax.shard_map(
        local, mesh=fine, in_specs=(P(blk, col),) * 4, out_specs=P(col, blk), check_vma=False
    )
```

time: 198 us -> 192 us (0.970)
  waiting for transfers between devices: 154 us -> 96.2 us
  starting transfers between devices: 0.04 us -> 28.6 us
  Pallas kernels: 0 us -> 15.5 us
  local copies, waits for them, and re-layouts: 1.34 us -> 6.29 us
  other arithmetic: 4.96 us -> 8.41 us
    all_gather x1 -> x2, waiting for transfers between devices: 104 us -> 26.4 us  [local(): gathered = [lax.all_gather(m, 'z', axis=0) for m in (msg, far)]]
    reduce_scatter x1 -> x0, waiting for transfers between devices: 50.1 us -> none  [local(): lax.psum_scatter(partial_value, 'col', scatter_dimension=0, tiled=True)]
    ppermute x0 -> x12, waiting for transfers between devices: none -> 39.4 us  [the longest x5 21.5 us: local(): lax.ppermute(over, axis, [(i, (i + hop) % size) for i in range(size)])]
    all_to_all x0 -> x2, waiting for transfers between devices: none -> 30.4 us  [local(): parts = lax.all_to_all(partial_value.reshape(4, -1, row_count), 'y', 0, 0)]
    ppermute x0 -> x12, starting transfers between devices: none -> 17.2 us  [the longest x7 9.09 us: swap(): return lax.ppermute(x, axis, [(0, 1), (1, 0)])]
    pallas_call x0 -> x3, Pallas kernels: none -> 15.5 us  [the longest x2 13.9 us: unpack(): pl.pallas_call(unpack_kernel, grid=(n,), in_specs=[pl.BlockSpec(memory_sp...]
    all_to_all x0 -> x2, starting transfers between devices: none -> 11.4 us  [local(): parts = lax.all_to_all(partial_value.reshape(4, -1, row_count), 'y', 0, 0)]
    unnamed x0 -> x14, local copies, waits for them, and re-layouts: none -> 4.58 us
  transfers between devices with their start and end apart: 2 -> 16, of which waited for: 2 -> 12; matrix products, arithmetic and copies ran while one was open for 0% -> 15% of each run, Pallas kernels for 0% -> 7%
where the time goes in v1:
time: 192 us; the launch traced here: 190 us
  waiting for transfers between devices  96.2 us (50%)
  starting transfers between devices  28.6 us (15%)
  matrix products  21 us (11%)
  Pallas kernels  15.5 us (8%)
  between operations  14.1 us (7%)
  other arithmetic  8.41 us (4%)
  local copies, waits for them, and re-layouts  6.29 us (3%)
    all_to_all x2, waiting for transfers between devices, local(): parts = lax.all_to_all(partial_value.reshape(4, -1, row_count), 'y', 0, 0)  30.4 us
    all_gather x2, waiting for transfers between devices, local(): gathered = [lax.all_gather(m, 'z', axis=0) for m in (msg, far)]  26.4 us
    ppermute x5, waiting for transfers between devices, local(): lax.ppermute(over, axis, [(i, (i + hop) % size) for i in range(size)])  21.5 us
    dot_general x2, matrix products, local(): lax.dot_general(amps, kept_ints, (((1,), (1,)), ((), ())), preferred_elem...  21 us
    ppermute x7, waiting for transfers between devices, swap(): return lax.ppermute(x, axis, [(0, 1), (1, 0)])  17.9 us
    pallas_call x2, Pallas kernels, unpack(): pl.pallas_call(unpack_kernel, grid=(n,), in_specs=[pl.BlockSpec(memory_sp...  13.9 us
    all_to_all x2, starting transfers between devices, local(): parts = lax.all_to_all(partial_value.reshape(4, -1, row_count), 'y', 0, 0)  11.4 us
    ppermute x7, starting transfers between devices, swap(): return lax.ppermute(x, axis, [(0, 1), (1, 0)])  9.09 us
  transfers between devices with their start and end apart: 16, of which 12 were waited for; matrix products, arithmetic and copies ran while one was open for 15% of the time, Pallas kernels for 7%

profile of v1, /device:TPU:24, one launch (start us, length us, event | category | flops | bytes accessed | tf_op | source)
XLA Modules:
  0.0 190.0 jit_solution(17838992647452056083)
XLA Ops:
  8.2 1.5 shard_map.46
  9.8 3.1 %collective-permute-start.10 = (bf16[608,128]{1,0:T(8,128)(2,1)}, bf16[608,128]{1,0:T(8,128)(2,1)S(1)}, u32[]{:S(2)}, u32[]{:S(2)}) collective-permute-start(bf16[608,128]{1,0:T(8,128)(2,1)} %get-tuple-element.35), channel_id=1, source_target_pairs={{0,128},{128,0},{1,129},{129,1},{2,130},{130,2},{3,131},{131,3},{4... | collective-permute-start | bytes 466952 | tf_op jit(solution)/shard_map/ppermute | solution.py:21
  12.9 4.5 %collective-permute-done.10 = bf16[608,128]{1,0:T(8,128)(2,1)S(1)} collective-permute-done((bf16[608,128]{1,0:T(8,128)(2,1)}, bf16[608,128]{1,0:T(8,128)(2,1)S(1)}, u32[]{:S(2)}, u32[]{:S(2)}) %collective-permute-start.10) | collective-permute-done | bytes 155680 | tf_op jit(solution)/shard_map/ppermute | solution.py:21
  18.1 2.0 %collective-permute-start.1 = (s32[8,128]{1,0:T(8,128)S(1)}, s32[8,128]{1,0:T(8,128)S(1)}, u32[]{:S(2)}, u32[]{:S(2)}) collective-permute-start(s32[8,128]{1,0:T(8,128)S(1)} %get-tuple-element.34), channel_id=1, source_target_pairs={{0,16},{16,32},{32,48},{48,64},{64,80},{80,96},{96,112},{112,0},{1... | collective-permute-start | bytes 12296 | tf_op jit(solution)/shard_map/ppermute | solution.py:126
  20.1 5.5 %collective-permute-done.1 = s32[8,128]{1,0:T(8,128)S(1)} collective-permute-done((s32[8,128]{1,0:T(8,128)S(1)}, s32[8,128]{1,0:T(8,128)S(1)}, u32[]{:S(2)}, u32[]{:S(2)}) %collective-permute-start.1) | collective-permute-done | bytes 4128 | tf_op jit(solution)/shard_map/ppermute | solution.py:126
  25.6 5.7 %collective-permute-done.2 = s32[8,128]{1,0:T(8,128)S(1)} collective-permute-done((s32[8,128]{1,0:T(8,128)S(1)}, s32[8,128]{1,0:T(8,128)S(1)}, u32[]{:S(2)}, u32[]{:S(2)}) %collective-permute-start.2) | collective-permute-done | bytes 4128 | tf_op jit(solution)/shard_map/ppermute | solution.py:126
  31.3 4.6 %collective-permute-start.3 = (s32[8,128]{1,0:T(8,128)S(1)}, s32[8,128]{1,0:T(8,128)S(1)}, u32[]{:S(2)}, u32[]{:S(2)}) collective-permute-start(s32[8,128]{1,0:T(8,128)S(1)} %max.25), channel_id=1, source_target_pairs={{0,64},{16,80},{32,96},{48,112},{64,0},{80,16},{96,32},{112,48},{1... | collective-permute-start | bytes 12296 | tf_op jit(solution)/shard_map/ppermute | solution.py:126
  36.0 3.0 %collective-permute-done.3 = s32[8,128]{1,0:T(8,128)S(1)} collective-permute-done((s32[8,128]{1,0:T(8,128)S(1)}, s32[8,128]{1,0:T(8,128)S(1)}, u32[]{:S(2)}, u32[]{:S(2)}) %collective-permute-start.3) | collective-permute-done | bytes 4128 | tf_op jit(solution)/shard_map/ppermute | solution.py:126
  39.2 3.4 %collective-permute-done.4 = s32[8,128]{1,0:T(8,128)S(1)} collective-permute-done((s32[8,128]{1,0:T(8,128)S(1)}, s32[8,128]{1,0:T(8,128)S(1)}, u32[]{:S(2)}, u32[]{:S(2)}) %collective-permute-start.4) | collective-permute-done | bytes 4128 | tf_op jit(solution)/shard_map/ppermute | solution.py:126
  42.6 1.2 collective-permute-start.5
  43.8 3.9 %collective-permute-done.5 = s32[8,128]{1,0:T(8,128)S(1)} collective-permute-done((s32[8,128]{1,0:T(8,128)S(1)}, s32[8,128]{1,0:T(8,128)S(1)}, u32[]{:S(2)}, u32[]{:S(2)}) %collective-permute-start.5) | collective-permute-done | bytes 4128 | tf_op jit(solution)/shard_map/ppermute | solution.py:126
  47.7 1.2 collective-permute-done.6
  48.9 3.0 %collective-permute-start.7 = (s32[8,128]{1,0:T(8,128)S(1)}, s32[8,128]{1,0:T(8,128)S(1)}, u32[]{:S(2)}, u32[]{:S(2)}) collective-permute-start(s32[8,128]{1,0:T(8,128)S(1)} %max.29), channel_id=1, source_target_pairs={{0,128},{128,0},{1,129},{129,1},{2,130},{130,2},{3,131},{131,3},{4... | collective-permute-start | bytes 12296 | tf_op jit(solution)/shard_map/ppermute | solution.py:21
  52.5 1.4 collective-permute-done.7
  54.0 1.4 collective-permute-start.8
  55.4 1.1 mul.11
  56.6 2.2 %copy-done.2 = bf16[1024,4096]{1,0:T(8,128)(2,1)S(1)} copy-done((bf16[1024,4096]{1,0:T(8,128)(2,1)S(1)}, bf16[1024,4096]{1,0:T(8,128)(2,1)}, u32[]{:S(2)}) %copy-start.2) | copy-done | bytes 8388632
  58.8 4.8 %bitcast_multiply_fusion = bf16[1024,4096]{1,0:T(8,128)(2,1)} fusion(bf16[1024,4096]{1,0:T(8,128)(2,1)S(1)} %copy-done.2, bf16[128,8,32,128]{3,2,1,0:T(8,128)(2,1)S(1)} %bitcast.14), kind=kLoop, calls=%fused_computation | loop fusion | flops 4194304 | bytes 25165824 | tf_op jit(solution)/shard_map/mul | solution.py:133
  64.9 26.4 %all-gather.13.cloned.1.call-done = bf16[4864,128]{1,0:T(8,128)(2,1)} async-done(((bf16[608,128]{1,0:T(8,128)(2,1)}), bf16[4864,128]{1,0:T(8,128)(2,1)}) %all-gather.13.cloned.1.call-update) | async-done | bytes 1245200 | tf_op jit(solution)/shard_map/all_gather | solution.py:121
  91.3 5.8 %conditional.2 = (bf16[512,4096]{1,0:T(8,128)(2,1)}) conditional(s32[]{:T(128)} %bitcast, (s32[1]{0:T(128)}, bf16[8,608,128]{2,1,0:T(8,128)(2,1)S(1)}, bf16[8,608,128]{2,1,0:T(8,128)(2,1)S(1)}) %tuple.32, bf16[32,4096]{1,0:T(8,128)(2,1)S(1)} %get-tuple-element.36), branch_computations={%region_0.0_spmd, %region_1.0_spmd} | conditional | flops 4000000000 | bytes 14417996 | solution.py:148
  91.3 5.8 %branch_0_fun.2 = bf16[512,4096]{1,0:T(8,128)(2,1)} custom-call(s32[1]{0:T(128)} %get-tuple-element.25.core_ref, bf16[8,608,128]{2,1,0:T(8,128)(2,1)S(1)} %get-tuple-element.26.own_ref, bf16[8,608,128]{2,1,0:T(8,128)(2,1)S(1)} %get-tuple-element.27.other_ref), custom_call_target="tpu_custom_call" | custom-call | flops 4000000000 | bytes 6291456 | tf_op jit(solution)/shard_map/cond/branch_0_fun/pallas_call | solution.py:101
  97.1 10.5 %fusion = f32[512,1024]{1,0:T(8,128)} fusion(bf16[512,4096]{1,0:T(8,128)(2,1)} %get-tuple-element.37, bf16[1024,4096]{1,0:T(8,128)(2,1)} %bitcast_multiply_fusion), kind=kOutput, calls=%fused_computation.3 | convolution fusion | flops 4294967296 | bytes 14680064 | tf_op jit(solution)/shard_map/dot_general | solution.py:149
  107.6 4.9 %all-to-all-start = ((f32[4,128,1024]{2,1,0:T(8,128)}), f32[4,128,1024]{2,1,0:T(8,128)S(1)}, u32[]{:S(2)}, u32[]{:S(2)}) async-start(f32[4,128,1024]{2,1,0:T(8,128)} %bitcast.15), calls=%async_computation | async-start | bytes 4194304 | tf_op jit(solution)/shard_map/all_to_all | solution.py:150
  112.5 8.1 %conditional.3 = (bf16[512,4096]{1,0:T(8,128)(2,1)}) conditional(s32[]{:T(128)} %bitcast, (s32[1]{0:T(128)}, bf16[8,608,128]{2,1,0:T(8,128)(2,1)}, bf16[8,608,128]{2,1,0:T(8,128)(2,1)}) %tuple.31, bf16[32,4096]{1,0:T(8,128)(2,1)S(1)} %copy-done.4), branch_computations={%region_3.0_spmd, %region_4.0_spmd} | conditional | flops 4000000000 | bytes 15466612 | solution.py:148
  112.5 8.1 %branch_0_fun.3 = bf16[512,4096]{1,0:T(8,128)(2,1)} custom-call(s32[1]{0:T(128)} %get-tuple-element.28.core_ref, bf16[8,608,128]{2,1,0:T(8,128)(2,1)} %get-tuple-element.29.own_ref, bf16[8,608,128]{2,1,0:T(8,128)(2,1)} %get-tuple-element.30.other_ref), custom_call_target="tpu_custom_call" | custom-call | flops 4000000000 | bytes 6291456 | tf_op jit(solution)/shard_map/cond/branch_0_fun/pallas_call | solution.py:101
  120.6 10.5 %fusion.1 = f32[512,1024]{1,0:T(8,128)} fusion(bf16[512,4096]{1,0:T(8,128)(2,1)} %get-tuple-element.38, bf16[1024,4096]{1,0:T(8,128)(2,1)} %bitcast_multiply_fusion), kind=kOutput, calls=%fused_computation.4 | convolution fusion | flops 4294967296 | bytes 14680064 | tf_op jit(solution)/shard_map/dot_general | solution.py:149
  131.1 6.3 %all-to-all-done = f32[4,128,1024]{2,1,0:T(8,128)S(1)} async-done(((f32[4,128,1024]{2,1,0:T(8,128)}), f32[4,128,1024]{2,1,0:T(8,128)S(1)}, u32[]{:S(2)}, u32[]{:S(2)}) %all-to-all-start) | async-done | bytes 2097184 | tf_op jit(solution)/shard_map/all_to_all | solution.py:150
  137.4 6.5 %all-to-all-start.1 = ((f32[4,128,1024]{2,1,0:T(8,128)}), f32[4,128,1024]{2,1,0:T(8,128)}, u32[]{:S(2)}, u32[]{:S(2)}) async-start(f32[4,128,1024]{2,1,0:T(8,128)} %bitcast.16), calls=%async_computation.1 | async-start | bytes 4194304 | tf_op jit(solution)/shard_map/all_to_all | solution.py:150
  144.1 24.0 %all-to-all-done.1 = f32[4,128,1024]{2,1,0:T(8,128)} async-done(((f32[4,128,1024]{2,1,0:T(8,128)}), f32[4,128,1024]{2,1,0:T(8,128)}, u32[]{:S(2)}, u32[]{:S(2)}) %all-to-all-start.1) | async-done | bytes 2097184 | tf_op jit(solution)/shard_map/all_to_all | solution.py:150
  168.1 1.8 reduce_sum.19
  170.0 1.6 collective-permute-start.12
  171.6 10.8 %collective-permute-done.12 = f32[128,1024]{1,0:T(8,128)S(1)} collective-permute-done((f32[128,1024]{1,0:T(8,128)S(1)}, f32[128,1024]{1,0:T(8,128)S(1)}, u32[]{:S(2)}, u32[]{:S(2)}) %collective-permute-start.12) | collective-permute-done | bytes 524320 | tf_op jit(solution)/shard_map/ppermute | solution.py:21
  (39 shorter events, 5.0 us)
Async XLA Ops:
  6.5 48.9 %all-gather.11.cloned.1.call-start = ((), (), s32[]{:S(2)}) async-start(), calls=%async_computation.4 | async-start | bytes 1400832 | tf_op jit(solution)/shard_map/all_gather | solution.py:121
  6.5 0.9 copy-start
  7.5 0.7 copy-start.1
  9.8 81.5 %copy-start.3 = (bf16[32,4096]{1,0:T(8,128)(2,1)}, bf16[32,4096]{1,0:T(8,128)(2,1)S(1)}, u32[]{:S(2)}) copy-start(bf16[32,4096]{1,0:T(8,128)(2,1)S(1)} %get-tuple-element.36) | copy-start | bytes 786436
  9.8 81.5 %all-gather.13.cloned.1.call-start = ((), (), s32[]{:S(2)}) async-start(), calls=%async_computation.5 | async-start | bytes 1400832 | tf_op jit(solution)/shard_map/all_gather | solution.py:121
  9.8 7.6 %collective-permute-start.10 = (bf16[608,128]{1,0:T(8,128)(2,1)}, bf16[608,128]{1,0:T(8,128)(2,1)S(1)}, u32[]{:S(2)}, u32[]{:S(2)}) collective-permute-start(bf16[608,128]{1,0:T(8,128)(2,1)} %get-tuple-element.35), channel_id=1, source_target_pairs={{0,128},{128,0},{1,129},{129,1},{2,130},{130,2},{3,131},{131,3},{4... | collective-permute-start | bytes 466952 | tf_op jit(solution)/shard_map/ppermute | solution.py:21
  17.4 0.7 copy-start.7
  18.1 7.5 %collective-permute-start.1 = (s32[8,128]{1,0:T(8,128)S(1)}, s32[8,128]{1,0:T(8,128)S(1)}, u32[]{:S(2)}, u32[]{:S(2)}) collective-permute-start(s32[8,128]{1,0:T(8,128)S(1)} %get-tuple-element.34), channel_id=1, source_target_pairs={{0,16},{16,32},{32,48},{48,64},{64,80},{80,96},{96,112},{112,0},{1... | collective-permute-start | bytes 12296 | tf_op jit(solution)/shard_map/ppermute | solution.py:126
  25.6 5.7 %collective-permute-start.2 = (s32[8,128]{1,0:T(8,128)S(1)}, s32[8,128]{1,0:T(8,128)S(1)}, u32[]{:S(2)}, u32[]{:S(2)}) collective-permute-start(s32[8,128]{1,0:T(8,128)S(1)} %max.24), channel_id=1, source_target_pairs={{0,32},{16,48},{32,64},{48,80},{64,96},{80,112},{96,0},{112,16},{1... | collective-permute-start | bytes 12296 | tf_op jit(solution)/shard_map/ppermute | solution.py:126
  31.3 7.6 %collective-permute-start.3 = (s32[8,128]{1,0:T(8,128)S(1)}, s32[8,128]{1,0:T(8,128)S(1)}, u32[]{:S(2)}, u32[]{:S(2)}) collective-permute-start(s32[8,128]{1,0:T(8,128)S(1)} %max.25), channel_id=1, source_target_pairs={{0,64},{16,80},{32,96},{48,112},{64,0},{80,16},{96,32},{112,48},{1... | collective-permute-start | bytes 12296 | tf_op jit(solution)/shard_map/ppermute | solution.py:126
  39.0 3.6 %collective-permute-start.4 = (s32[8,128]{1,0:T(8,128)S(1)}, s32[8,128]{1,0:T(8,128)S(1)}, u32[]{:S(2)}, u32[]{:S(2)}) collective-permute-start(s32[8,128]{1,0:T(8,128)S(1)} %max.26), channel_id=1, source_target_pairs={{0,1},{1,2},{2,3},{3,0},{4,5},{5,6},{6,7},{7,4},{8,9},{9,10},{10,1... | collective-permute-start | bytes 12296 | tf_op jit(solution)/shard_map/ppermute | solution.py:126
  42.6 5.1 %collective-permute-start.5 = (s32[8,128]{1,0:T(8,128)S(1)}, s32[8,128]{1,0:T(8,128)S(1)}, u32[]{:S(2)}, u32[]{:S(2)}) collective-permute-start(s32[8,128]{1,0:T(8,128)S(1)} %max.27), channel_id=1, source_target_pairs={{0,2},{1,3},{2,0},{3,1},{4,6},{5,7},{6,4},{7,5},{8,10},{9,11},{10,... | collective-permute-start | bytes 12296 | tf_op jit(solution)/shard_map/ppermute | solution.py:126
  47.7 1.2 collective-permute-start.6
  48.9 5.1 %collective-permute-start.7 = (s32[8,128]{1,0:T(8,128)S(1)}, s32[8,128]{1,0:T(8,128)S(1)}, u32[]{:S(2)}, u32[]{:S(2)}) collective-permute-start(s32[8,128]{1,0:T(8,128)S(1)} %max.29), channel_id=1, source_target_pairs={{0,128},{128,0},{1,129},{129,1},{2,130},{130,2},{3,131},{131,3},{4... | collective-permute-start | bytes 12296 | tf_op jit(solution)/shard_map/ppermute | solution.py:21
  54.0 9.7 %collective-permute-start.8 = (s32[8,128]{1,0:T(8,128)S(1)}, s32[8,128]{1,0:T(8,128)S(1)}, u32[]{:S(2)}, u32[]{:S(2)}) collective-permute-start(s32[8,128]{1,0:T(8,128)S(1)} %max.30), channel_id=1, source_target_pairs={{0,4},{4,0},{1,5},{5,1},{2,6},{6,2},{3,7},{7,3},{8,12},{12,8},{9,1... | collective-permute-start | bytes 12296 | tf_op jit(solution)/shard_map/ppermute | solution.py:21
  55.4 3.4 %copy-start.2 = (bf16[1024,4096]{1,0:T(8,128)(2,1)S(1)}, bf16[1024,4096]{1,0:T(8,128)(2,1)}, u32[]{:S(2)}) copy-start(bf16[1024,4096]{1,0:T(8,128)(2,1)} %param.9) | copy-start | bytes 25165828
  55.4 35.8 %collective-permute-start.9 = (bf16[8,608,128]{2,1,0:T(8,128)(2,1)}, bf16[8,608,128]{2,1,0:T(8,128)(2,1)S(1)}, u32[]{:S(2)}, u32[]{:S(2)}) collective-permute-start(bf16[8,608,128]{2,1,0:T(8,128)(2,1)} %bitcast.19), channel_id=1, source_target_pairs={{0,8},{8,0},{1,9},{9,1},{2,10},{10,2},{3,11},{11,3},{4,12},{12,4},... | collective-permute-start | bytes 3735560 | tf_op jit(solution)/shard_map/ppermute | solution.py:21
  58.8 32.5 %copy-start.8 = (bf16[4864,128]{1,0:T(8,128)(2,1)S(1)}, bf16[4864,128]{1,0:T(8,128)(2,1)}, u32[]{:S(2)}) copy-start(bf16[4864,128]{1,0:T(8,128)(2,1)} %all-gather.11.cloned.1.call-done) | copy-start | bytes 3735556
  91.3 21.2 %collective-permute-start.11 = (bf16[8,608,128]{2,1,0:T(8,128)(2,1)}, bf16[8,608,128]{2,1,0:T(8,128)(2,1)}, u32[]{:S(2)}, u32[]{:S(2)}) collective-permute-start(bf16[8,608,128]{2,1,0:T(8,128)(2,1)} %bitcast.17), channel_id=1, source_target_pairs={{0,8},{8,0},{1,9},{9,1},{2,10},{10,2},{3,11},{11,3},{4,12},{12,4},... | collective-permute-start | bytes 3735560 | tf_op jit(solution)/shard_map/ppermute | solution.py:21
  107.6 4.9 %copy-start.4 = (bf16[32,4096]{1,0:T(8,128)(2,1)S(1)}, bf16[32,4096]{1,0:T(8,128)(2,1)}, u32[]{:S(2)}) copy-start(bf16[32,4096]{1,0:T(8,128)(2,1)} %copy-done.3) | copy-start | bytes 786436
  107.6 29.8 %all-to-all-start = ((f32[4,128,1024]{2,1,0:T(8,128)}), f32[4,128,1024]{2,1,0:T(8,128)S(1)}, u32[]{:S(2)}, u32[]{:S(2)}) async-start(f32[4,128,1024]{2,1,0:T(8,128)} %bitcast.15), calls=%async_computation | async-start | bytes 4194304 | tf_op jit(solution)/shard_map/all_to_all | solution.py:150
  137.4 30.7 %all-to-all-start.1 = ((f32[4,128,1024]{2,1,0:T(8,128)}), f32[4,128,1024]{2,1,0:T(8,128)}, u32[]{:S(2)}, u32[]{:S(2)}) async-start(f32[4,128,1024]{2,1,0:T(8,128)} %bitcast.16), calls=%async_computation.1 | async-start | bytes 4194304 | tf_op jit(solution)/shard_map/all_to_all | solution.py:150
  170.0 12.4 %collective-permute-start.12 = (f32[128,1024]{1,0:T(8,128)S(1)}, f32[128,1024]{1,0:T(8,128)S(1)}, u32[]{:S(2)}, u32[]{:S(2)}) collective-permute-start(f32[128,1024]{1,0:T(8,128)S(1)} %broadcast_select_fusion), channel_id=1, source_target_pairs={{0,4},{4,0},{1,5},{5,1},{2,6},{6,2},{3,7},{7,3},{8,12},{12,8},{9,1... | collective-permute-start | bytes 1572872 | tf_op jit(solution)/shard_map/ppermute | solution.py:21
Sparse Core Ops, SparseCore 0:
  9.9 41.8 all-gather.10
  53.6 37.6 all-gather.12

commit v2 on v0

v2 whole, which is shorter than its diff:
```python
import jax
import jax.numpy as jnp
from jax import lax
from jax.experimental import pallas as pl
from jax.experimental.pallas import tpu as pltpu
from jax.sharding import Mesh, PartitionSpec as P

TILE = 128
OWN = 32
TILES = 32
GROUP = 8
WIN = 256
LOW = (0, 80, 240, 320)
ROWS = 576
MSG = ROWS + OWN
RT = 8
BIG = 32000.0
F32 = jnp.float32
BF16 = jnp.bfloat16
I16 = jnp.int16
I32 = jnp.int32
VMEM = pl.BlockSpec(memory_space=pltpu.VMEM)
SMEM = pl.BlockSpec(memory_space=pltpu.SMEM)


def swap(x, axis):
    return lax.ppermute(x, axis, [(0, 1), (1, 0)])


def pack_kernel(amps_ref, mask_ref, msg_ref, acc):
    mask = mask_ref[...].astype(F32)
    row = lax.broadcasted_iota(I32, (OWN, OWN), 0)
    col = lax.broadcasted_iota(I32, (OWN, OWN), 1)
    mask16 = mask.astype(BF16)
    in_tile = jnp.dot((col < row).astype(BF16), mask16, preferred_element_type=F32)
    count = jnp.dot(jnp.ones((OWN, OWN), BF16), mask16, preferred_element_type=F32)
    same = row // GROUP == col // GROUP
    before = jnp.dot(count.astype(BF16), ((row < col) & same).astype(BF16), preferred_element_type=F32)
    lane = col // GROUP
    total = [jnp.sum(jnp.where(lane == g, count, 0.0), axis=1, keepdims=True) for g in range(4)]
    start1 = jnp.maximum(total[0], float(LOW[1]))
    end1 = start1 + total[1]
    start3 = ROWS - total[3]
    start2 = jnp.minimum(start3, float(LOW[2] + WIN)) - total[2]
    over = (end1 > LOW[1] + WIN) | (start2 < LOW[2]) | (end1 > start2)
    offset = jnp.where(
        lane == 0,
        0.0,
        jnp.where(lane == 1, start1 - LOW[1], jnp.where(lane == 2, start2 - LOW[2], start3 - LOW[3])),
    )
    place = jnp.where(mask > 0.0, in_tile + before + offset, -1.0)
    over = jnp.broadcast_to(jnp.where(over, 1.0, 0.0), (OWN, TILE - TILES))
    msg_ref[0, ROWS:MSG, :] = jnp.concatenate([place, over], axis=1).astype(BF16)
    acc[...] = jnp.zeros_like(acc)
    spots = lax.broadcasted_iota(I32, (OWN, WIN), 1).astype(F32)
    for g in range(4):
        tiles = range(g * GROUP, (g + 1) * GROUP)
        hot = jnp.concatenate([(place[:, t : t + 1] == spots).astype(BF16) for t in tiles], axis=0)
        val = jnp.concatenate([amps_ref[:, t * TILE : (t + 1) * TILE] for t in tiles], axis=0)
        acc[LOW[g] : LOW[g] + WIN, :] += lax.dot_general(
            hot, val, (((0,), (0,)), ((), ())), preferred_element_type=F32
        )
    msg_ref[0, :ROWS, :] = acc[...].astype(BF16)


def pack(amps, mask):
    return pl.pallas_call(
        pack_kernel,
        out_shape=jax.ShapeDtypeStruct((1, MSG, TILE), BF16),
        scratch_shapes=[pltpu.VMEM((ROWS, TILE), F32)],
        compiler_params=pltpu.CompilerParams(vmem_limit_bytes=8 << 20),
    )(amps, mask)


def keep_kernel(mask_ref, ints_ref, out_ref):
    r = pl.program_id(0)
    for t in range(TILES):
        kept = jnp.where(mask_ref[r, t] > 0, 1.0, 0.0).astype(BF16)
        out_ref[:, t * TILE : (t + 1) * TILE] = ints_ref[:, t * TILE : (t + 1) * TILE] * kept


def keep(ints, mask):
    block = pl.BlockSpec((TILE, TILES * TILE), lambda r: (r, 0))
    return pl.pallas_call(
        keep_kernel,
        grid=(RT,),
        in_specs=[SMEM, block],
        out_specs=block,
        out_shape=jax.ShapeDtypeStruct(ints.shape, BF16),
        compiler_params=pltpu.CompilerParams(vmem_limit_bytes=8 << 20),
        cost_estimate=pl.CostEstimate(flops=4 << 20, bytes_accessed=16 << 20, transcendentals=0),
    )(mask, ints)


def unpack_kernel(sizes, row_ref, *refs):
    ins, (out_ref, over_ref, buf, top) = refs[: len(sizes)], refs[len(sizes) :]
    i = pl.program_id(0)
    low = 0
    for size, ref in zip(sizes, ins, strict=True):

        @pl.when((i >= low) & (i < low + size))
        def _(ref=ref, low=low):
            buf[...] = ref[i - low]

        low += size
    place = buf[ROWS:MSG, :].astype(F32)
    seen = jnp.where(i == 0, 0.0, top[...])
    top[...] = jnp.maximum(seen, place[:8, :])
    over_ref[...] = jnp.broadcast_to(top[:, TILE - 1 :], (8, TILE)).astype(I32)
    spots = lax.broadcasted_iota(I32, (OWN, WIN), 1).astype(F32)
    for g in range(4):
        tiles = range(g * GROUP, (g + 1) * GROUP)
        hot = jnp.concatenate([(place[:, t : t + 1] == spots).astype(BF16) for t in tiles], axis=0)
        got = jnp.dot(hot, buf[LOW[g] : LOW[g] + WIN, :], preferred_element_type=F32).astype(BF16)
        for n, t in enumerate(tiles):
            out_ref[:, t * TILE : (t + 1) * TILE] = got[n * OWN : (n + 1) * OWN, :]


def unpack(rows, messages):
    sizes = [m.shape[0] for m in messages]
    whole = [pl.BlockSpec(m.shape, lambda i, rows: (0, 0, 0)) for m in messages]
    return pl.pallas_call(
        lambda *refs: unpack_kernel(sizes, *refs),
        grid_spec=pltpu.PrefetchScalarGridSpec(
            num_scalar_prefetch=1,
            grid=(sum(sizes),),
            in_specs=whole,
            out_specs=[
                pl.BlockSpec((OWN, TILES * TILE), lambda i, rows: (rows[i], 0)),
                pl.BlockSpec((8, TILE), lambda i, rows: (0, 0)),
            ],
            scratch_shapes=[pltpu.VMEM((MSG, TILE), BF16), pltpu.VMEM((8, TILE), F32)],
        ),
        out_shape=[
            jax.ShapeDtypeStruct((sum(sizes) * OWN, TILES * TILE), BF16),
            jax.ShapeDtypeStruct((8, TILE), I32),
        ],
        compiler_params=pltpu.CompilerParams(vmem_limit_bytes=16 << 20),
        cost_estimate=pl.CostEstimate(flops=5_000_000_000, bytes_accessed=7 << 20, transcendentals=0),
    )(rows, *messages)


def code(value):
    most = jnp.max(jnp.abs(value), axis=1, keepdims=True)
    power = jnp.ceil(jnp.log2(jnp.maximum(most, 1e-37)))
    return jnp.round(value * jnp.exp2(-power) * BIG).astype(I32).astype(I16), power


def decode(msg_ref, t):
    scale = jnp.exp2(msg_ref[RT, :, t : t + 1].astype(I32).astype(F32))
    return msg_ref[t].astype(I32).astype(F32) * (1.0 / BIG) * scale


def product_kernel(amps_ref, over_ref, ints_ref, own_ref, *outs):
    j = pl.program_id(0)
    value = lax.dot_general(amps_ref[...], ints_ref[...], (((1,), (1,)), ((), ())), preferred_element_type=F32)
    lane = lax.broadcasted_iota(I32, (TILE, TILE), 1)
    for n in range(2):
        t = 2 * j + n
        own_ref[t] = value[:TILE, n * TILE : (n + 1) * TILE]
        for d, out in enumerate(outs):
            coded, power = code(value[(d + 1) * TILE : (d + 2) * TILE, n * TILE : (n + 1) * TILE])
            out[t] = coded
            flag = jnp.broadcast_to(over_ref[:1, :], (TILE, TILE))
            before = jnp.where(t == 0, flag, out[RT].astype(I32))
            out[RT] = jnp.where(lane == t, power.astype(I32), before).astype(I16)


def product(amps, over, ints):
    coded = jax.ShapeDtypeStruct((RT + 1, TILE, TILE), I16)
    whole = lambda shape: pl.BlockSpec(shape, lambda j: (0,) * len(shape))
    return pl.pallas_call(
        product_kernel,
        grid=(RT // 2,),
        in_specs=[
            whole(amps.shape),
            whole(over.shape),
            pl.BlockSpec((2 * TILE, TILES * TILE), lambda j: (j, 0)),
        ],
        out_specs=[whole((RT, TILE, TILE))] + [whole(coded.shape)] * 3,
        out_shape=[jax.ShapeDtypeStruct((RT, TILE, TILE), F32)] + [coded] * 3,
        compiler_params=pltpu.CompilerParams(vmem_limit_bytes=32 << 20),
        cost_estimate=pl.CostEstimate(flops=6_000_000_000, bytes_accessed=16 << 20, transcendentals=0),
    )(amps, over, ints)


def add_kernel(over_ref, own_ref, a_ref, b_ref, c_ref, sum_ref, out_ref):
    lane = lax.broadcasted_iota(I32, (TILE, TILE), 1)
    powers = jnp.broadcast_to(over_ref[:1, :], (TILE, TILE))
    for ref in (a_ref, b_ref, c_ref):
        powers = jnp.maximum(powers, ref[RT].astype(I32))
    for t in range(RT):
        value = own_ref[t] + decode(a_ref, t) + decode(b_ref, t) + decode(c_ref, t)
        sum_ref[t] = value
        out_ref[t], power = code(value)
        powers = jnp.where(lane == t, power.astype(I32), powers)
    out_ref[RT] = powers.astype(I16)


def add(over, own, parts):
    return pl.pallas_call(
        add_kernel,
        in_specs=[VMEM] * 5,
        out_specs=[VMEM] * 2,
        out_shape=[
            jax.ShapeDtypeStruct(own.shape, F32),
            jax.ShapeDtypeStruct((RT + 1, TILE, TILE), I16),
        ],
        compiler_params=pltpu.CompilerParams(vmem_limit_bytes=8 << 20),
    )(over, own, *parts)


def last_kernel(near_ref, first_ref, second_ref, flag_ref, got_ref, out_ref, over_ref):
    near = near_ref[0] > 0
    for t in range(RT):
        mine = jnp.where(near, first_ref[t], second_ref[t])
        out_ref[:, t * TILE : (t + 1) * TILE] = (mine + decode(got_ref, t)).astype(BF16)
    over_ref[...] = jnp.maximum(
        got_ref[RT, :16, TILE - 16 :].astype(I32), flag_ref[RT, :16, TILE - 16 :].astype(I32)
    )


def last(near, first, second, flag, got):
    return pl.pallas_call(
        last_kernel,
        in_specs=[SMEM] + [VMEM] * 4,
        out_specs=[VMEM] * 2,
        out_shape=[jax.ShapeDtypeStruct((TILE, RT * TILE), BF16), jax.ShapeDtypeStruct((16, 16), I32)],
        compiler_params=pltpu.CompilerParams(vmem_limit_bytes=8 << 20),
    )(near, first, second, flag, got)


def plain(amplitudes, amp_mask, kept_ints):
    kept = (
        amplitudes.reshape(OWN, TILES, TILE) * amp_mask.astype(BF16)[:, :, None]
    ).reshape(OWN, TILES * TILE)
    value = lax.dot_general(
        lax.all_gather(kept, ("xh", "z", "core"), axis=0, tiled=True),
        kept_ints,
        (((1,), (1,)), ((), ())),
        preferred_element_type=F32,
    )
    return lax.psum_scatter(value, ("xl", "y"), scatter_dimension=0, tiled=True).astype(BF16)


RING = [(2 * z, 2 * ((z + 1) % 8)) for z in range(8)] + [(2 * z + 1, 2 * ((z + 7) % 8) + 1) for z in range(8)]

SHIFT = (0, 0, -1, -1, 1, 1, -2, -2, 2, 2, -3, -3, 3, 3, 4, 4)
OTHER = (0, 1, 0, 1, 1, 0, 0, 1, 1, 0, 0, 1, 1, 0, 0, 1)


def local(amplitudes, integrals, amp_mask, int_mask):
    z, core, y = (lax.axis_index(name).astype(I32) for name in ("z", "core", "y"))
    near = lax.axis_index("xl") == lax.axis_index("xh")
    up = 1 - 2 * core

    own = pack(amplitudes, amp_mask)
    pair = jnp.concatenate([own, swap(own, "core")], axis=0)
    pairs = [pair, swap(pair, "xh")]
    kept_ints = keep(integrals, int_mask)

    far = (z + up * jnp.asarray(SHIFT, I32)) & 7
    rows = (((far >> 1) - y) & 3) * 4 + (far & 1) * 2 + (core ^ jnp.asarray(OTHER, I32))

    held = [[pair] for pair in pairs]
    for hop in range(1, 5):
        for chunk in range(2):
            block = held[chunk][-2] if hop > 1 else held[chunk][0]
            block = lax.ppermute(block if hop < 4 else block[:1], ("z", "core"), RING)
            held[chunk] += [block, swap(block, "core")]

    sums, coded = [], []
    over = None
    for chunk in range(2):
        amps, flag = unpack(rows, held[chunk])
        over = flag if over is None else jnp.maximum(over, flag)
        own_part, *parts = product(amps, over, kept_ints)
        got = [
            lax.ppermute(part, "y", [(i, (i + d + 1) % 4) for i in range(4)]) for d, part in enumerate(parts)
        ]
        total, sent = add(over, own_part, got)
        sums.append(total)
        coded.append(sent)
    sent = jnp.where(near, coded[1], coded[0])
    sent = sent.at[RT, :, TILE - 16 :].set(coded[1][RT, :, TILE - 16 :])
    got = swap(sent, "xl")
    out, over = last(near.astype(I32).reshape(1), sums[0], sums[1], sent, got)
    return lax.cond(
        jnp.max(over) > 0,
        lambda out: plain(amplitudes, amp_mask, kept_ints),
        lambda out: out,
        out,
    )


def solution(mesh):
    fine = Mesh(mesh.devices.reshape(2, 8, 2, 2, 4), ("xh", "z", "core", "xl", "y"))
    blk, col = ("xh", "z", "core"), ("xl", "y")
    return jax.shard_map(
        local, mesh=fine, in_specs=(P(blk, col),) * 4, out_specs=P(col, blk), check_vma=False
    )
```

time: 198 us -> 132 us (0.67); the launches traced: 194 us -> 132 us
  waiting for transfers between devices: 154 us -> 45.3 us
  Pallas kernels: 0 us -> 43.2 us
  starting transfers between devices: 0.04 us -> 21.3 us
  matrix products: 20.1 us -> 0 us
  local copies, waits for them, and re-layouts: 1.34 us -> 6.98 us
  other arithmetic: 4.96 us -> 0.77 us
    all_gather x1 -> x0, waiting for transfers between devices: 104 us -> none  [local(): lax.all_gather(kept_amps, 'blk', axis=0, tiled=True)]
    reduce_scatter x1 -> x0, waiting for transfers between devices: 50.1 us -> none  [local(): lax.psum_scatter(partial_value, 'col', scatter_dimension=0, tiled=True)]
    ppermute x0 -> x25, waiting for transfers between devices: none -> 45.3 us  [the longest x8 23.2 us: local(): block = lax.ppermute(block if hop < 4 else block[:1], ('z', 'core'), RING)]
    pallas_call x0 -> x9, Pallas kernels: none -> 43.2 us  [the longest x2 17 us: product(): pl.pallas_call(product_kernel, grid=(RT // 2,), in_specs=[whole(amps.shap...]
    ppermute x0 -> x25, starting transfers between devices: none -> 21.3 us  [the longest x11 9.48 us: swap(): return lax.ppermute(x, axis, [(0, 1), (1, 0)])]
    dot_general x1 -> x0, matrix products: 20.1 us -> none  [local(): lax.dot_general(lax.all_gather(kept_amps, 'blk', axis=0, tiled=True), kep...]
    unnamed x0 -> x16, local copies, waits for them, and re-layouts: none -> 6.48 us
    convert_element_type x3 -> x0, other arithmetic: 3.19 us -> none  [the longest x1 1.78 us: local(): return summed.astype(jnp.bfloat16)]
  transfers between devices with their start and end apart: 2 -> 25, of which waited for: 2 -> 9; matrix products, arithmetic and copies ran while one was open for 0% -> 0% of each run, Pallas kernels for 0% -> 30%
where the time goes in v2:
time: 132 us
  waiting for transfers between devices  45.3 us (34%)
  Pallas kernels  43.2 us (33%)
  starting transfers between devices  21.3 us (16%)
  between operations  14.2 us (11%)
  local copies, waits for them, and re-layouts  6.98 us (5%)
    ppermute x8, waiting for transfers between devices, local(): block = lax.ppermute(block if hop < 4 else block[:1], ('z', 'core'), RING)  23.2 us
    pallas_call x2, Pallas kernels, product(): pl.pallas_call(product_kernel, grid=(RT // 2,), in_specs=[whole(amps.shap...  17 us
    pallas_call x2, Pallas kernels, unpack(): pl.pallas_call(lambda *refs: unpack_kernel(sizes, *refs), grid_spec=pltpu...  15.6 us
    ppermute x6, waiting for transfers between devices, local(): lax.ppermute(part, 'y', [(i, (i + d + 1) % 4) for i in range(4)])  13.4 us
    ppermute x11, starting transfers between devices, swap(): return lax.ppermute(x, axis, [(0, 1), (1, 0)])  9.48 us
    ppermute x11, waiting for transfers between devices, swap(): return lax.ppermute(x, axis, [(0, 1), (1, 0)])  8.65 us
    ppermute x6, starting transfers between devices, local(): lax.ppermute(part, 'y', [(i, (i + d + 1) % 4) for i in range(4)])  7.57 us
    unnamed x16, local copies, waits for them, and re-layouts  6.48 us
  transfers between devices with their start and end apart: 25, of which 9 were waited for; matrix products, arithmetic and copies ran while one was open for 0% of the time, Pallas kernels for 30%

profile of v2, /device:TPU:24, one launch (start us, length us, event | category | flops | bytes accessed | tf_op | source)
XLA Modules:
  0.0 131.8 jit_solution(3435730697147554816)
XLA Ops:
  6.5 1.8 %shard_map.66 = bf16[1,608,128]{2,1,0:T(8,128)(2,1)S(1)} custom-call(bf16[32,4096]{1,0:T(8,128)(2,1)} %amps_ref.1, s32[32,32]{1,0:T(8,128)} %mask_ref.2), custom_call_target="tpu_custom_call" | custom-call | tf_op jit(solution)/shard_map/pallas_call | solution.py:67
  8.4 1.4 %collective-permute-done = bf16[1,608,128]{2,1,0:T(8,128)(2,1)S(1)} collective-permute-done((bf16[1,608,128]{2,1,0:T(8,128)(2,1)S(1)}, bf16[1,608,128]{2,1,0:T(8,128)(2,1)S(1)}, u32[]{:S(2)}, u32[]{:S(2)}) %collective-permute-start) | collective-permute-done | bytes 155680 | tf_op jit(solution)/shard_map/ppermute | solution.py:27
  9.8 2.0 %collective-permute-start.1 = (bf16[2,608,128]{2,1,0:T(8,128)(2,1)S(1)}, bf16[2,608,128]{2,1,0:T(8,128)(2,1)S(1)}, u32[]{:S(2)}, u32[]{:S(2)}) collective-permute-start(bf16[2,608,128]{2,1,0:T(8,128)(2,1)S(1)} %pad_maximum_fusion.refs_1_), channel_id=1, source_target_pairs={{0,16},{16,32},{32,48},{48,64},{64,80},{80,96},{96,112},{112,0},{8... | collective-permute-start | bytes 933896 | tf_op jit(solution)/shard_map/ppermute | solution.py:269
  11.8 3.0 %collective-permute-start.12 = (bf16[2,608,128]{2,1,0:T(8,128)(2,1)S(1)}, bf16[2,608,128]{2,1,0:T(8,128)(2,1)S(1)}, u32[]{:S(2)}, u32[]{:S(2)}) collective-permute-start(bf16[2,608,128]{2,1,0:T(8,128)(2,1)S(1)} %pad_maximum_fusion.refs_1_), channel_id=1, source_target_pairs={{0,128},{128,0},{1,129},{129,1},{2,130},{130,2},{3,131},{131,3},{4... | collective-permute-start | bytes 933896 | tf_op jit(solution)/shard_map/ppermute | solution.py:27
  14.9 5.8 %collective-permute-done.1.refs_2_ = bf16[2,608,128]{2,1,0:T(8,128)(2,1)S(1)} collective-permute-done((bf16[2,608,128]{2,1,0:T(8,128)(2,1)S(1)}, bf16[2,608,128]{2,1,0:T(8,128)(2,1)S(1)}, u32[]{:S(2)}, u32[]{:S(2)}) %collective-permute-start.1) | collective-permute-done | bytes 311328 | tf_op jit(solution)/shard_map/ppermute | solution.py:269
  20.7 2.2 %collective-permute-start.13 = (bf16[2,608,128]{2,1,0:T(8,128)(2,1)S(1)}, bf16[2,608,128]{2,1,0:T(8,128)(2,1)S(1)}, u32[]{:S(2)}, u32[]{:S(2)}) collective-permute-start(bf16[2,608,128]{2,1,0:T(8,128)(2,1)S(1)} %collective-permute-done.12.refs_1_), channel_id=1, source_target_pairs={{0,16},{16,32},{32,48},{48,64},{64,80},{80,96},{96,112},{112,0},{8... | collective-permute-start | bytes 933896 | tf_op jit(solution)/shard_map/ppermute | solution.py:269
  22.8 5.9 %collective-permute-done.3.refs_4_ = bf16[2,608,128]{2,1,0:T(8,128)(2,1)S(1)} collective-permute-done((bf16[2,608,128]{2,1,0:T(8,128)(2,1)S(1)}, bf16[2,608,128]{2,1,0:T(8,128)(2,1)S(1)}, u32[]{:S(2)}, u32[]{:S(2)}) %collective-permute-start.3) | collective-permute-done | bytes 311328 | tf_op jit(solution)/shard_map/ppermute | solution.py:269
  28.8 3.5 %collective-permute-done.13.refs_2_ = bf16[2,608,128]{2,1,0:T(8,128)(2,1)S(1)} collective-permute-done((bf16[2,608,128]{2,1,0:T(8,128)(2,1)S(1)}, bf16[2,608,128]{2,1,0:T(8,128)(2,1)S(1)}, u32[]{:S(2)}, u32[]{:S(2)}) %collective-permute-start.13) | collective-permute-done | bytes 311328 | tf_op jit(solution)/shard_map/ppermute | solution.py:269
  32.3 4.6 %collective-permute-done.5.refs_6_ = bf16[2,608,128]{2,1,0:T(8,128)(2,1)S(1)} collective-permute-done((bf16[2,608,128]{2,1,0:T(8,128)(2,1)S(1)}, bf16[2,608,128]{2,1,0:T(8,128)(2,1)S(1)}, u32[]{:S(2)}, u32[]{:S(2)}) %collective-permute-start.5) | collective-permute-done | bytes 311328 | tf_op jit(solution)/shard_map/ppermute | solution.py:269
  37.0 3.4 %collective-permute-done.15.refs_4_ = bf16[2,608,128]{2,1,0:T(8,128)(2,1)S(1)} collective-permute-done((bf16[2,608,128]{2,1,0:T(8,128)(2,1)S(1)}, bf16[2,608,128]{2,1,0:T(8,128)(2,1)S(1)}, u32[]{:S(2)}, u32[]{:S(2)}) %collective-permute-start.15) | collective-permute-done | bytes 311328 | tf_op jit(solution)/shard_map/ppermute | solution.py:269
  41.5 3.4 %copy-done = bf16[1024,4096]{1,0:T(8,128)(2,1)S(1)} copy-done((bf16[1024,4096]{1,0:T(8,128)(2,1)S(1)}, bf16[1024,4096]{1,0:T(8,128)(2,1)}, u32[]{:S(2)}) %copy-start) | copy-done | bytes 8388632
  44.9 0.7 copy-done.1
  45.6 6.3 %shard_map.68.ints_ref = bf16[1024,4096]{1,0:T(8,128)(2,1)} custom-call(s32[8,32]{1,0:T(8,128)S(1)} %copy-done.1, bf16[1024,4096]{1,0:T(8,128)(2,1)S(1)} %copy-done), custom_call_target="tpu_custom_call" | custom-call | flops 4194304 | bytes 16777216 | tf_op jit(solution)/shard_map/pallas_call | solution.py:84
  51.9 0.6 collective-permute-start.14
  52.6 0.7 copy-done.2
  53.4 2.9 %collective-permute-start.18 = (bf16[2,608,128]{2,1,0:T(8,128)(2,1)S(1)}, bf16[2,608,128]{2,1,0:T(8,128)(2,1)S(1)}, u32[]{:S(2)}, u32[]{:S(2)}) collective-permute-start(bf16[2,608,128]{2,1,0:T(8,128)(2,1)S(1)} %collective-permute-done.17.refs_6_), channel_id=1, source_target_pairs={{0,8},{8,0},{1,9},{9,1},{2,10},{10,2},{3,11},{11,3},{4,12},{12,4},... | collective-permute-start | bytes 933896 | tf_op jit(solution)/shard_map/ppermute | solution.py:27
  56.3 1.0 copy-done.3
  57.2 8.3 %shard_map.67 = (bf16[512,4096]{1,0:T(8,128)(2,1)S(1)}, s32[8,128]{1,0:T(8,128)S(1)}) custom-call(s32[16]{0:T(128)S(1)} %xor_add_fusion.refs_0_, bf16[2,608,128]{2,1,0:T(8,128)(2,1)S(1)} %pad_maximum_fusion.refs_1_, bf16[2,608,128]{2,1,0:T(8,128)(2,1)S(1)} %collective-permute-done.1.refs_2_, bf16[2,608,128]{2,1,0:T(8,128)(2,1)S(1)} %collective-permute-done.2.refs_3_, ...), custom_call_target="tpu_custom_call" | custom-call | flops 5000000000 | bytes 7340032 | tf_op jit(solution)/shard_map/pallas_call | solution.py:122
  65.6 8.5 %shard_map.69 = (f32[8,128,128]{2,1,0:T(8,128)S(1)}, s16[9,128,128]{2,1,0:T(8,128)(2,1)S(1)}, s16[9,128,128]{2,1,0:T(8,128)(2,1)}, s16[9,128,128]{2,1,0:T(8,128)(2,1)}) custom-call(bf16[512,4096]{1,0:T(8,128)(2,1)S(1)} %get-tuple-element.49.amps_ref, s32[8,128]{1,0:T(8,128)S(1)} %get-tuple-element.48.over_ref, bf16[1024,4096]{1,0:T(8,128)(2,1)} %shard_map.68.ints_ref), custom_call_target="tpu_custom_call" | custom-call | flops 6000000000 | bytes 16777216 | tf_op jit(solution)/shard_map/pallas_call | solution.py:172
  74.3 2.6 %collective-permute-start.10 = (s16[9,128,128]{2,1,0:T(8,128)(2,1)}, s16[9,128,128]{2,1,0:T(8,128)(2,1)S(1)}, u32[]{:S(2)}, u32[]{:S(2)}) collective-permute-start(s16[9,128,128]{2,1,0:T(8,128)(2,1)} %get-tuple-element.52), channel_id=1, source_target_pairs={{0,2},{1,3},{2,0},{3,1},{4,6},{5,7},{6,4},{7,5},{8,10},{9,11},{10,... | collective-permute-start | bytes 884744 | tf_op jit(solution)/shard_map/ppermute | solution.py:279
  76.9 7.3 %shard_map.71 = (bf16[512,4096]{1,0:T(8,128)(2,1)S(1)}, s32[8,128]{1,0:T(8,128)S(1)}) custom-call(s32[16]{0:T(128)S(1)} %xor_add_fusion.refs_0_, bf16[2,608,128]{2,1,0:T(8,128)(2,1)S(1)} %collective-permute-done.12.refs_1_, bf16[2,608,128]{2,1,0:T(8,128)(2,1)S(1)} %collective-permute-done.13.refs_2_, ...), custom_call_target="tpu_custom_call" | custom-call | flops 5000000000 | bytes 7340032 | tf_op jit(solution)/shard_map/pallas_call | solution.py:122
  84.3 8.5 %shard_map.72 = (f32[8,128,128]{2,1,0:T(8,128)S(1)}, s16[9,128,128]{2,1,0:T(8,128)(2,1)}, s16[9,128,128]{2,1,0:T(8,128)(2,1)}, s16[9,128,128]{2,1,0:T(8,128)(2,1)}) custom-call(bf16[512,4096]{1,0:T(8,128)(2,1)S(1)} %get-tuple-element.56.amps_ref, s32[8,128]{1,0:T(8,128)S(1)} %max.3.over_ref, bf16[1024,4096]{1,0:T(8,128)(2,1)} %shard_map.68.ints_ref), custom_call_target="tpu_custom_call" | custom-call | flops 6000000000 | bytes 16777216 | tf_op jit(solution)/shard_map/pallas_call | solution.py:172
  92.8 3.2 %collective-permute-start.21 = (s16[9,128,128]{2,1,0:T(8,128)(2,1)}, s16[9,128,128]{2,1,0:T(8,128)(2,1)S(1)}, u32[]{:S(2)}, u32[]{:S(2)}) collective-permute-start(s16[9,128,128]{2,1,0:T(8,128)(2,1)} %get-tuple-element.58), channel_id=1, source_target_pairs={{0,1},{1,2},{2,3},{3,0},{4,5},{5,6},{6,7},{7,4},{8,9},{9,10},{10,1... | collective-permute-start | bytes 884744 | tf_op jit(solution)/shard_map/ppermute | solution.py:279
  96.1 1.4 %collective-permute-start.23 = (s16[9,128,128]{2,1,0:T(8,128)(2,1)}, s16[9,128,128]{2,1,0:T(8,128)(2,1)S(1)}, u32[]{:S(2)}, u32[]{:S(2)}) collective-permute-start(s16[9,128,128]{2,1,0:T(8,128)(2,1)} %get-tuple-element.60), channel_id=1, source_target_pairs={{0,3},{1,0},{2,1},{3,2},{4,7},{5,4},{6,5},{7,6},{8,11},{9,8},{10,9... | collective-permute-start | bytes 884744 | tf_op jit(solution)/shard_map/ppermute | solution.py:279
  97.6 1.2 shard_map.70
  98.7 10.0 %collective-permute-done.21.a_ref = s16[9,128,128]{2,1,0:T(8,128)(2,1)S(1)} collective-permute-done((s16[9,128,128]{2,1,0:T(8,128)(2,1)}, s16[9,128,128]{2,1,0:T(8,128)(2,1)S(1)}, u32[]{:S(2)}, u32[]{:S(2)}) %collective-permute-start.21) | collective-permute-done | bytes 294944 | tf_op jit(solution)/shard_map/ppermute | solution.py:279
  108.7 3.4 %collective-permute-done.23.c_ref = s16[9,128,128]{2,1,0:T(8,128)(2,1)S(1)} collective-permute-done((s16[9,128,128]{2,1,0:T(8,128)(2,1)}, s16[9,128,128]{2,1,0:T(8,128)(2,1)S(1)}, u32[]{:S(2)}, u32[]{:S(2)}) %collective-permute-start.23) | collective-permute-done | bytes 294944 | tf_op jit(solution)/shard_map/ppermute | solution.py:279
  112.1 1.2 shard_map.73
  113.9 1.6 %collective-permute-start.24 = (s16[9,128,128]{2,1,0:T(8,128)(2,1)S(1)}, s16[9,128,128]{2,1,0:T(8,128)(2,1)S(1)}, u32[]{:S(2)}, u32[]{:S(2)}) collective-permute-start(s16[9,128,128]{2,1,0:T(8,128)(2,1)S(1)} %scatter.4.flag_ref), channel_id=1, source_target_pairs={{0,4},{4,0},{1,5},{5,1},{2,6},{6,2},{3,7},{7,3},{8,12},{12,8},{9,1... | collective-permute-start | bytes 884744 | tf_op jit(solution)/shard_map/ppermute | solution.py:27
  115.5 7.2 %collective-permute-done.24.got_ref = s16[9,128,128]{2,1,0:T(8,128)(2,1)S(1)} collective-permute-done((s16[9,128,128]{2,1,0:T(8,128)(2,1)S(1)}, s16[9,128,128]{2,1,0:T(8,128)(2,1)S(1)}, u32[]{:S(2)}, u32[]{:S(2)}) %collective-permute-start.24) | collective-permute-done | bytes 294944 | tf_op jit(solution)/shard_map/ppermute | solution.py:27
  123.0 0.6 reduce_max.9
  124.3 0.7 copy-done.7
  (53 shorter events, 2.8 us)
Async XLA Ops:
  8.3 1.5 %collective-permute-start = (bf16[1,608,128]{2,1,0:T(8,128)(2,1)S(1)}, bf16[1,608,128]{2,1,0:T(8,128)(2,1)S(1)}, u32[]{:S(2)}, u32[]{:S(2)}) collective-permute-start(bf16[1,608,128]{2,1,0:T(8,128)(2,1)S(1)} %shard_map.66), channel_id=1, source_target_pairs={{0,8},{8,0},{1,9},{9,1},{2,10},{10,2},{3,11},{11,3},{4,12},{12,4},... | collective-permute-start | bytes 466952 | tf_op jit(solution)/shard_map/ppermute | solution.py:27
  9.8 10.8 %collective-permute-start.1 = (bf16[2,608,128]{2,1,0:T(8,128)(2,1)S(1)}, bf16[2,608,128]{2,1,0:T(8,128)(2,1)S(1)}, u32[]{:S(2)}, u32[]{:S(2)}) collective-permute-start(bf16[2,608,128]{2,1,0:T(8,128)(2,1)S(1)} %pad_maximum_fusion.refs_1_), channel_id=1, source_target_pairs={{0,16},{16,32},{32,48},{48,64},{64,80},{80,96},{96,112},{112,0},{8... | collective-permute-start | bytes 933896 | tf_op jit(solution)/shard_map/ppermute | solution.py:269
  11.8 8.8 %collective-permute-start.12 = (bf16[2,608,128]{2,1,0:T(8,128)(2,1)S(1)}, bf16[2,608,128]{2,1,0:T(8,128)(2,1)S(1)}, u32[]{:S(2)}, u32[]{:S(2)}) collective-permute-start(bf16[2,608,128]{2,1,0:T(8,128)(2,1)S(1)} %pad_maximum_fusion.refs_1_), channel_id=1, source_target_pairs={{0,128},{128,0},{1,129},{129,1},{2,130},{130,2},{3,131},{131,3},{4... | collective-permute-start | bytes 933896 | tf_op jit(solution)/shard_map/ppermute | solution.py:27
  20.6 8.1 %collective-permute-start.3 = (bf16[2,608,128]{2,1,0:T(8,128)(2,1)S(1)}, bf16[2,608,128]{2,1,0:T(8,128)(2,1)S(1)}, u32[]{:S(2)}, u32[]{:S(2)}) collective-permute-start(bf16[2,608,128]{2,1,0:T(8,128)(2,1)S(1)} %collective-permute-done.1.refs_2_), channel_id=1, source_target_pairs={{0,16},{16,32},{32,48},{48,64},{64,80},{80,96},{96,112},{112,0},{8... | collective-permute-start | bytes 933896 | tf_op jit(solution)/shard_map/ppermute | solution.py:269
  20.7 11.6 %collective-permute-start.13 = (bf16[2,608,128]{2,1,0:T(8,128)(2,1)S(1)}, bf16[2,608,128]{2,1,0:T(8,128)(2,1)S(1)}, u32[]{:S(2)}, u32[]{:S(2)}) collective-permute-start(bf16[2,608,128]{2,1,0:T(8,128)(2,1)S(1)} %collective-permute-done.12.refs_1_), channel_id=1, source_target_pairs={{0,16},{16,32},{32,48},{48,64},{64,80},{80,96},{96,112},{112,0},{8... | collective-permute-start | bytes 933896 | tf_op jit(solution)/shard_map/ppermute | solution.py:269
  28.8 8.1 %collective-permute-start.5 = (bf16[2,608,128]{2,1,0:T(8,128)(2,1)S(1)}, bf16[2,608,128]{2,1,0:T(8,128)(2,1)S(1)}, u32[]{:S(2)}, u32[]{:S(2)}) collective-permute-start(bf16[2,608,128]{2,1,0:T(8,128)(2,1)S(1)} %collective-permute-done.3.refs_4_), channel_id=1, source_target_pairs={{0,16},{16,32},{32,48},{48,64},{64,80},{80,96},{96,112},{112,0},{8... | collective-permute-start | bytes 933896 | tf_op jit(solution)/shard_map/ppermute | solution.py:269
  32.3 8.1 %collective-permute-start.15 = (bf16[2,608,128]{2,1,0:T(8,128)(2,1)S(1)}, bf16[2,608,128]{2,1,0:T(8,128)(2,1)S(1)}, u32[]{:S(2)}, u32[]{:S(2)}) collective-permute-start(bf16[2,608,128]{2,1,0:T(8,128)(2,1)S(1)} %collective-permute-done.13.refs_2_), channel_id=1, source_target_pairs={{0,16},{16,32},{32,48},{48,64},{64,80},{80,96},{96,112},{112,0},{8... | collective-permute-start | bytes 933896 | tf_op jit(solution)/shard_map/ppermute | solution.py:269
  36.9 15.0 %collective-permute-start.7 = (bf16[1,608,128]{2,1,0:T(8,128)(2,1)S(1)}, bf16[1,608,128]{2,1,0:T(8,128)(2,1)S(1)}, u32[]{:S(2)}, u32[]{:S(2)}) collective-permute-start(bf16[1,608,128]{2,1,0:T(8,128)(2,1)S(1)} %slice.37), channel_id=1, source_target_pairs={{0,16},{16,32},{32,48},{48,64},{64,80},{80,96},{96,112},{112,0},{8... | collective-permute-start | bytes 466952 | tf_op jit(solution)/shard_map/ppermute | solution.py:269
  40.4 11.5 %collective-permute-start.17 = (bf16[2,608,128]{2,1,0:T(8,128)(2,1)S(1)}, bf16[2,608,128]{2,1,0:T(8,128)(2,1)S(1)}, u32[]{:S(2)}, u32[]{:S(2)}) collective-permute-start(bf16[2,608,128]{2,1,0:T(8,128)(2,1)S(1)} %collective-permute-done.15.refs_4_), channel_id=1, source_target_pairs={{0,16},{16,32},{32,48},{48,64},{64,80},{80,96},{96,112},{112,0},{8... | collective-permute-start | bytes 933896 | tf_op jit(solution)/shard_map/ppermute | solution.py:269
  40.4 12.1 %collective-permute-start.2 = (bf16[2,608,128]{2,1,0:T(8,128)(2,1)S(1)}, bf16[2,608,128]{2,1,0:T(8,128)(2,1)S(1)}, u32[]{:S(2)}, u32[]{:S(2)}) collective-permute-start(bf16[2,608,128]{2,1,0:T(8,128)(2,1)S(1)} %collective-permute-done.1.refs_2_), channel_id=1, source_target_pairs={{0,8},{8,0},{1,9},{9,1},{2,10},{10,2},{3,11},{11,3},{4,12},{12,4},... | collective-permute-start | bytes 933896 | tf_op jit(solution)/shard_map/ppermute | solution.py:27
  41.0 11.6 %collective-permute-start.4 = (bf16[2,608,128]{2,1,0:T(8,128)(2,1)S(1)}, bf16[2,608,128]{2,1,0:T(8,128)(2,1)S(1)}, u32[]{:S(2)}, u32[]{:S(2)}) collective-permute-start(bf16[2,608,128]{2,1,0:T(8,128)(2,1)S(1)} %collective-permute-done.3.refs_4_), channel_id=1, source_target_pairs={{0,8},{8,0},{1,9},{9,1},{2,10},{10,2},{3,11},{11,3},{4,12},{12,4},... | collective-permute-start | bytes 933896 | tf_op jit(solution)/shard_map/ppermute | solution.py:27
  41.0 15.3 %collective-permute-start.6 = (bf16[2,608,128]{2,1,0:T(8,128)(2,1)S(1)}, bf16[2,608,128]{2,1,0:T(8,128)(2,1)}, u32[]{:S(2)}, u32[]{:S(2)}) collective-permute-start(bf16[2,608,128]{2,1,0:T(8,128)(2,1)S(1)} %collective-permute-done.5.refs_6_), channel_id=1, source_target_pairs={{0,8},{8,0},{1,9},{9,1},{2,10},{10,2},{3,11},{11,3},{4,12},{12,4},... | collective-permute-start | bytes 933896 | tf_op jit(solution)/shard_map/ppermute | solution.py:27
  41.5 3.4 %copy-start = (bf16[1024,4096]{1,0:T(8,128)(2,1)S(1)}, bf16[1024,4096]{1,0:T(8,128)(2,1)}, u32[]{:S(2)}) copy-start(bf16[1024,4096]{1,0:T(8,128)(2,1)} %ints_ref.1) | copy-start | bytes 25165828
  45.5 6.3 %copy-start.5 = (s32[16]{0:T(128)S(1)}, s32[16]{0:T(128)}, u32[]{:S(2)}) copy-start(s32[16]{0:T(128)} %constant.74.clone) | copy-start | bytes 196
  45.5 6.3 %copy-start.6 = (s32[16]{0:T(128)S(1)}, s32[16]{0:T(128)}, u32[]{:S(2)}) copy-start(s32[16]{0:T(128)} %constant.73.clone) | copy-start | bytes 196
  51.9 1.5 %collective-permute-start.8 = (bf16[1,608,128]{2,1,0:T(8,128)(2,1)S(1)}, bf16[1,608,128]{2,1,0:T(8,128)(2,1)S(1)}, u32[]{:S(2)}, u32[]{:S(2)}) collective-permute-start(bf16[1,608,128]{2,1,0:T(8,128)(2,1)S(1)} %collective-permute-done.7.refs_8_), channel_id=1, source_target_pairs={{0,8},{8,0},{1,9},{9,1},{2,10},{10,2},{3,11},{11,3},{4,12},{12,4},... | collective-permute-start | bytes 466952 | tf_op jit(solution)/shard_map/ppermute | solution.py:27
  51.9 22.4 %collective-permute-start.14 = (bf16[2,608,128]{2,1,0:T(8,128)(2,1)S(1)}, bf16[2,608,128]{2,1,0:T(8,128)(2,1)S(1)}, u32[]{:S(2)}, u32[]{:S(2)}) collective-permute-start(bf16[2,608,128]{2,1,0:T(8,128)(2,1)S(1)} %collective-permute-done.13.refs_2_), channel_id=1, source_target_pairs={{0,8},{8,0},{1,9},{9,1},{2,10},{10,2},{3,11},{11,3},{4,12},{12,4},... | collective-permute-start | bytes 933896 | tf_op jit(solution)/shard_map/ppermute | solution.py:27
  52.5 24.4 %collective-permute-start.16 = (bf16[2,608,128]{2,1,0:T(8,128)(2,1)S(1)}, bf16[2,608,128]{2,1,0:T(8,128)(2,1)S(1)}, u32[]{:S(2)}, u32[]{:S(2)}) collective-permute-start(bf16[2,608,128]{2,1,0:T(8,128)(2,1)S(1)} %collective-permute-done.15.refs_4_), channel_id=1, source_target_pairs={{0,8},{8,0},{1,9},{9,1},{2,10},{10,2},{3,11},{11,3},{4,12},{12,4},... | collective-permute-start | bytes 933896 | tf_op jit(solution)/shard_map/ppermute | solution.py:27
  52.6 0.7 copy-start.2
  53.4 12.1 %collective-permute-start.19 = (bf16[1,608,128]{2,1,0:T(8,128)(2,1)S(1)}, bf16[1,608,128]{2,1,0:T(8,128)(2,1)S(1)}, u32[]{:S(2)}, u32[]{:S(2)}) collective-permute-start(bf16[1,608,128]{2,1,0:T(8,128)(2,1)S(1)} %slice.38), channel_id=1, source_target_pairs={{0,16},{16,32},{32,48},{48,64},{64,80},{80,96},{96,112},{112,0},{8... | collective-permute-start | bytes 466952 | tf_op jit(solution)/shard_map/ppermute | solution.py:269
  53.4 23.6 %collective-permute-start.18 = (bf16[2,608,128]{2,1,0:T(8,128)(2,1)S(1)}, bf16[2,608,128]{2,1,0:T(8,128)(2,1)S(1)}, u32[]{:S(2)}, u32[]{:S(2)}) collective-permute-start(bf16[2,608,128]{2,1,0:T(8,128)(2,1)S(1)} %collective-permute-done.17.refs_6_), channel_id=1, source_target_pairs={{0,8},{8,0},{1,9},{9,1},{2,10},{10,2},{3,11},{11,3},{4,12},{12,4},... | collective-permute-start | bytes 933896 | tf_op jit(solution)/shard_map/ppermute | solution.py:27
  56.3 1.0 copy-start.3
  65.5 11.4 %collective-permute-start.20 = (bf16[1,608,128]{2,1,0:T(8,128)(2,1)S(1)}, bf16[1,608,128]{2,1,0:T(8,128)(2,1)S(1)}, u32[]{:S(2)}, u32[]{:S(2)}) collective-permute-start(bf16[1,608,128]{2,1,0:T(8,128)(2,1)S(1)} %collective-permute-done.19.refs_8_), channel_id=1, source_target_pairs={{0,8},{8,0},{1,9},{9,1},{2,10},{10,2},{3,11},{11,3},{4,12},{12,4},... | collective-permute-start | bytes 466952 | tf_op jit(solution)/shard_map/ppermute | solution.py:27
  74.1 22.0 %collective-permute-start.9 = (s16[9,128,128]{2,1,0:T(8,128)(2,1)S(1)}, s16[9,128,128]{2,1,0:T(8,128)(2,1)S(1)}, u32[]{:S(2)}, u32[]{:S(2)}) collective-permute-start(s16[9,128,128]{2,1,0:T(8,128)(2,1)S(1)} %get-tuple-element.51), channel_id=1, source_target_pairs={{0,1},{1,2},{2,3},{3,0},{4,5},{5,6},{6,7},{7,4},{8,9},{9,10},{10,1... | collective-permute-start | bytes 884744 | tf_op jit(solution)/shard_map/ppermute | solution.py:279
  74.3 23.2 %collective-permute-start.10 = (s16[9,128,128]{2,1,0:T(8,128)(2,1)}, s16[9,128,128]{2,1,0:T(8,128)(2,1)S(1)}, u32[]{:S(2)}, u32[]{:S(2)}) collective-permute-start(s16[9,128,128]{2,1,0:T(8,128)(2,1)} %get-tuple-element.52), channel_id=1, source_target_pairs={{0,2},{1,3},{2,0},{3,1},{4,6},{5,7},{6,4},{7,5},{8,10},{9,11},{10,... | collective-permute-start | bytes 884744 | tf_op jit(solution)/shard_map/ppermute | solution.py:279
  76.9 20.6 %collective-permute-start.11 = (s16[9,128,128]{2,1,0:T(8,128)(2,1)}, s16[9,128,128]{2,1,0:T(8,128)(2,1)S(1)}, u32[]{:S(2)}, u32[]{:S(2)}) collective-permute-start(s16[9,128,128]{2,1,0:T(8,128)(2,1)} %get-tuple-element.53), channel_id=1, source_target_pairs={{0,3},{1,0},{2,1},{3,2},{4,7},{5,4},{6,5},{7,6},{8,11},{9,8},{10,9... | collective-permute-start | bytes 884744 | tf_op jit(solution)/shard_map/ppermute | solution.py:279
  84.3 40.0 %copy-start.4 = (s32[32,32]{1,0:T(8,128)S(1)}, s32[32,32]{1,0:T(8,128)}, u32[]{:S(2)}) copy-start(s32[32,32]{1,0:T(8,128)} %mask_ref.2) | copy-start | bytes 12292
  92.8 15.9 %collective-permute-start.21 = (s16[9,128,128]{2,1,0:T(8,128)(2,1)}, s16[9,128,128]{2,1,0:T(8,128)(2,1)S(1)}, u32[]{:S(2)}, u32[]{:S(2)}) collective-permute-start(s16[9,128,128]{2,1,0:T(8,128)(2,1)} %get-tuple-element.58), channel_id=1, source_target_pairs={{0,1},{1,2},{2,3},{3,0},{4,5},{5,6},{6,7},{7,4},{8,9},{9,10},{10,1... | collective-permute-start | bytes 884744 | tf_op jit(solution)/shard_map/ppermute | solution.py:279
  96.0 12.7 %collective-permute-start.22 = (s16[9,128,128]{2,1,0:T(8,128)(2,1)}, s16[9,128,128]{2,1,0:T(8,128)(2,1)S(1)}, u32[]{:S(2)}, u32[]{:S(2)}) collective-permute-start(s16[9,128,128]{2,1,0:T(8,128)(2,1)} %get-tuple-element.59), channel_id=1, source_target_pairs={{0,2},{1,3},{2,0},{3,1},{4,6},{5,7},{6,4},{7,5},{8,10},{9,11},{10,... | collective-permute-start | bytes 884744 | tf_op jit(solution)/shard_map/ppermute | solution.py:279
  96.1 16.0 %collective-permute-start.23 = (s16[9,128,128]{2,1,0:T(8,128)(2,1)}, s16[9,128,128]{2,1,0:T(8,128)(2,1)S(1)}, u32[]{:S(2)}, u32[]{:S(2)}) collective-permute-start(s16[9,128,128]{2,1,0:T(8,128)(2,1)} %get-tuple-element.60), channel_id=1, source_target_pairs={{0,3},{1,0},{2,1},{3,2},{4,7},{5,4},{6,5},{7,6},{8,11},{9,8},{10,9... | collective-permute-start | bytes 884744 | tf_op jit(solution)/shard_map/ppermute | solution.py:279
  113.9 8.8 %collective-permute-start.24 = (s16[9,128,128]{2,1,0:T(8,128)(2,1)S(1)}, s16[9,128,128]{2,1,0:T(8,128)(2,1)S(1)}, u32[]{:S(2)}, u32[]{:S(2)}) collective-permute-start(s16[9,128,128]{2,1,0:T(8,128)(2,1)S(1)} %scatter.4.flag_ref), channel_id=1, source_target_pairs={{0,4},{4,0},{1,5},{5,1},{2,6},{6,2},{3,7},{7,3},{8,12},{12,8},{9,1... | collective-permute-start | bytes 884744 | tf_op jit(solution)/shard_map/ppermute | solution.py:27
  124.3 0.7 copy-start.7
  (1 other events, 0.7 us)

commit v3 on v2

v3 whole, which is shorter than its diff:
```python
import jax
import jax.numpy as jnp
from jax import lax
from jax.experimental import pallas as pl
from jax.experimental.pallas import tpu as pltpu
from jax.sharding import Mesh, PartitionSpec as P

TILE = 128
OWN = 32
TILES = 32
GROUP = 8
WIN = 256
LOW = (0, 80, 240, 320)
ROWS = 576
MSG = ROWS + OWN
RT = 8
META = 16
BIG = 32000.0
F32 = jnp.float32
BF16 = jnp.bfloat16
I16 = jnp.int16
I32 = jnp.int32
VMEM = pl.BlockSpec(memory_space=pltpu.VMEM)
SMEM = pl.BlockSpec(memory_space=pltpu.SMEM)


def swap(x, axis):
    return lax.ppermute(x, axis, [(0, 1), (1, 0)])


def pack_kernel(amps_ref, mask_ref, msg_ref, acc):
    mask = mask_ref[...].astype(F32)
    row = lax.broadcasted_iota(I32, (OWN, OWN), 0)
    col = lax.broadcasted_iota(I32, (OWN, OWN), 1)
    mask16 = mask.astype(BF16)
    in_tile = jnp.dot((col < row).astype(BF16), mask16, preferred_element_type=F32)
    count = jnp.dot(jnp.ones((OWN, OWN), BF16), mask16, preferred_element_type=F32)
    same = row // GROUP == col // GROUP
    before = jnp.dot(count.astype(BF16), ((row < col) & same).astype(BF16), preferred_element_type=F32)
    lane = col // GROUP
    total = [jnp.sum(jnp.where(lane == g, count, 0.0), axis=1, keepdims=True) for g in range(4)]
    start1 = jnp.maximum(total[0], float(LOW[1]))
    end1 = start1 + total[1]
    start3 = ROWS - total[3]
    start2 = jnp.minimum(start3, float(LOW[2] + WIN)) - total[2]
    over = (end1 > LOW[1] + WIN) | (start2 < LOW[2]) | (end1 > start2)
    offset = jnp.where(
        lane == 0,
        0.0,
        jnp.where(lane == 1, start1 - LOW[1], jnp.where(lane == 2, start2 - LOW[2], start3 - LOW[3])),
    )
    place = jnp.where(mask > 0.0, in_tile + before + offset, -1.0)
    over = jnp.broadcast_to(jnp.where(over, 1.0, 0.0), (OWN, TILE - TILES))
    msg_ref[0, ROWS:MSG, :] = jnp.concatenate([place, over], axis=1).astype(BF16)
    acc[...] = jnp.zeros_like(acc)
    spots = lax.broadcasted_iota(I32, (OWN, WIN), 1).astype(F32)
    for g in range(4):
        tiles = range(g * GROUP, (g + 1) * GROUP)
        hot = jnp.concatenate([(place[:, t : t + 1] == spots).astype(BF16) for t in tiles], axis=0)
        val = jnp.concatenate([amps_ref[:, t * TILE : (t + 1) * TILE] for t in tiles], axis=0)
        acc[LOW[g] : LOW[g] + WIN, :] += lax.dot_general(
            hot, val, (((0,), (0,)), ((), ())), preferred_element_type=F32
        )
    msg_ref[0, :ROWS, :] = acc[...].astype(BF16)


def pack(amps, mask):
    return pl.pallas_call(
        pack_kernel,
        out_shape=jax.ShapeDtypeStruct((1, MSG, TILE), BF16),
        scratch_shapes=[pltpu.VMEM((ROWS, TILE), F32)],
        compiler_params=pltpu.CompilerParams(vmem_limit_bytes=8 << 20),
    )(amps, mask)


def code(value):
    most = jnp.max(jnp.abs(value), axis=1, keepdims=True)
    power = jnp.ceil(jnp.log2(jnp.maximum(most, 1e-37)))
    return jnp.round(value * jnp.exp2(-power) * BIG).astype(I32).astype(I16), power


def tile_rows(t):
    return pl.ds(t * TILE, TILE)


def scales(msg_ref):
    powers = msg_ref[RT * TILE :, :].astype(I32).astype(F32)
    return jnp.exp2(jnp.transpose(jnp.concatenate([powers] * (TILE // META), axis=0)))


def decode(msg_ref, scale, t):
    return msg_ref[tile_rows(t), :].astype(I32).astype(F32) * (1.0 / BIG) * scale[:, t : t + 1]


def flags(msg_ref):
    return msg_ref[RT * TILE :, :].astype(I32)


def powers_and_flags(powers, flag):
    row = lax.broadcasted_iota(I32, (META, TILE), 0)
    powers = jnp.transpose(powers)[:META, :].astype(I32)
    return jnp.where(row < RT, powers, flag).astype(I16)


def chunk_kernel(sizes, row_ref, mask_ref, before_ref, ints_ref, *refs):
    ins, (own_ref, a_ref, b_ref, c_ref, over_ref, got, amps, held, sem) = refs[: len(sizes)], refs[len(sizes) :]
    loads = [
        pltpu.make_async_copy(ints_ref.at[pl.ds(j * 2 * TILE, 2 * TILE), :], held.at[j], sem.at[j])
        for j in range(RT // 2)
    ]
    for load in loads:
        load.start()
    i = 0
    for size, ref in zip(sizes, ins, strict=True):
        got[i : i + size] = ref[...]
        i += size
    spots = lax.broadcasted_iota(I32, (OWN, WIN), 1).astype(F32)

    def unpack(i, over):
        place = got[i, ROWS:MSG, :].astype(F32)
        rows = pl.ds(pl.multiple_of(row_ref[i] * OWN, OWN), OWN)
        for g in range(4):
            tiles = range(g * GROUP, (g + 1) * GROUP)
            hot = jnp.concatenate([(place[:, t : t + 1] == spots).astype(BF16) for t in tiles], axis=0)
            value = jnp.dot(hot, got[i, LOW[g] : LOW[g] + WIN, :], preferred_element_type=F32).astype(BF16)
            for n, t in enumerate(tiles):
                amps[rows, t * TILE : (t + 1) * TILE] = value[n * OWN : (n + 1) * OWN, :]
        return jnp.maximum(over, place[:META, TILE - 1 :])

    over = lax.fori_loop(0, i, unpack, jnp.zeros((META, 1), F32))
    over = jnp.maximum(jnp.broadcast_to(over, (META, TILE)).astype(I32), before_ref[...])
    over_ref[...] = over
    lane = lax.broadcasted_iota(I32, (TILE, TILE), 1)
    for load in loads:
        load.wait()

    def multiply(j, powers):
        for n in range(2):
            for t in range(TILES):
                kept = jnp.where(mask_ref[2 * j + n, t] > 0, 1.0, 0.0).astype(BF16)
                part = (j, slice(n * TILE, (n + 1) * TILE), slice(t * TILE, (t + 1) * TILE))
                held[part] = held[part] * kept
        value = lax.dot_general(amps[...], held[j], (((1,), (1,)), ((), ())), preferred_element_type=F32)
        for n in range(2):
            t = 2 * j + n
            own_ref[t] = value[:TILE, n * TILE : (n + 1) * TILE]
            new = []
            for d, out in enumerate((a_ref, b_ref, c_ref)):
                coded, power = code(value[(d + 1) * TILE : (d + 2) * TILE, n * TILE : (n + 1) * TILE])
                out[pl.ds(pl.multiple_of(t * TILE, TILE), TILE), :] = coded
                new.append(jnp.where(lane == t, power, powers[d]))
            powers = tuple(new)
        return powers

    powers = lax.fori_loop(0, RT // 2, multiply, (jnp.zeros((TILE, TILE), F32),) * 3)
    for d, out in enumerate((a_ref, b_ref, c_ref)):
        out[RT * TILE :, :] = powers_and_flags(powers[d], over)


def chunk_sums(rows, mask, before, ints, messages):
    sizes = [m.shape[0] for m in messages]
    coded = jax.ShapeDtypeStruct((RT * TILE + META, TILE), I16)
    return pl.pallas_call(
        lambda *refs: chunk_kernel(sizes, *refs),
        in_specs=[SMEM, SMEM, VMEM, pl.BlockSpec(memory_space=pl.ANY)] + [VMEM] * len(sizes),
        out_specs=[VMEM] * 5,
        out_shape=[
            jax.ShapeDtypeStruct((RT, TILE, TILE), F32),
            coded,
            coded,
            coded,
            jax.ShapeDtypeStruct((META, TILE), I32),
        ],
        scratch_shapes=[
            pltpu.VMEM((sum(sizes), MSG, TILE), BF16),
            pltpu.VMEM((sum(sizes) * OWN, TILES * TILE), BF16),
            pltpu.VMEM((RT // 2, 2 * TILE, TILES * TILE), BF16),
            pltpu.SemaphoreType.DMA((RT // 2,)),
        ],
        compiler_params=pltpu.CompilerParams(vmem_limit_bytes=44 << 20),
        cost_estimate=pl.CostEstimate(flops=10_000_000_000, bytes_accessed=16 << 20, transcendentals=0),
    )(rows, mask, before, ints, *messages)


def add_kernel(over_ref, own_ref, a_ref, b_ref, c_ref, sum_ref, out_ref):
    lane = lax.broadcasted_iota(I32, (TILE, TILE), 1)
    parts = (a_ref, b_ref, c_ref)
    scale = [scales(ref) for ref in parts]
    powers = jnp.zeros((TILE, TILE), F32)
    for t in range(RT):
        value = own_ref[t]
        for ref, by in zip(parts, scale, strict=True):
            value = value + decode(ref, by, t)
        sum_ref[t] = value
        out_ref[tile_rows(t), :], power = code(value)
        powers = jnp.where(lane == t, power, powers)
    flag = over_ref[...]
    for ref in parts:
        flag = jnp.maximum(flag, jnp.broadcast_to(flags(ref)[META - 1 :, :], (META, TILE)))
    out_ref[RT * TILE :, :] = powers_and_flags(powers, flag)


def add(over, own, parts):
    return pl.pallas_call(
        add_kernel,
        in_specs=[VMEM] * 5,
        out_specs=[VMEM] * 2,
        out_shape=[
            jax.ShapeDtypeStruct(own.shape, F32),
            jax.ShapeDtypeStruct((RT * TILE + META, TILE), I16),
        ],
        compiler_params=pltpu.CompilerParams(vmem_limit_bytes=8 << 20),
    )(over, own, *parts)


def choose_kernel(near_ref, first_ref, second_ref, out_ref):
    near = near_ref[0] > 0
    both = RT * TILE
    out_ref[:both, :] = jnp.where(near, second_ref[:both, :].astype(I32), first_ref[:both, :].astype(I32)).astype(I16)
    first, second = flags(first_ref), flags(second_ref)
    row = lax.broadcasted_iota(I32, (META, TILE), 0)
    out_ref[both:, :] = jnp.where((row >= RT) | near, second, first).astype(I16)


def choose(near, first, second):
    return pl.pallas_call(
        choose_kernel,
        in_specs=[SMEM] + [VMEM] * 2,
        out_specs=VMEM,
        out_shape=jax.ShapeDtypeStruct(first.shape, I16),
        compiler_params=pltpu.CompilerParams(vmem_limit_bytes=8 << 20),
    )(near, first, second)


def last_kernel(near_ref, first_ref, second_ref, sent_ref, got_ref, out_ref, over_ref):
    near = near_ref[0] > 0
    scale = scales(got_ref)
    for t in range(RT):
        mine = jnp.where(near, first_ref[t], second_ref[t])
        out_ref[:, t * TILE : (t + 1) * TILE] = (mine + decode(got_ref, scale, t)).astype(BF16)
    over_ref[...] = jnp.maximum(flags(sent_ref), flags(got_ref))


def last(near, first, second, sent, got):
    return pl.pallas_call(
        last_kernel,
        in_specs=[SMEM] + [VMEM] * 4,
        out_specs=[VMEM] * 2,
        out_shape=[jax.ShapeDtypeStruct((TILE, RT * TILE), BF16), jax.ShapeDtypeStruct((META, TILE), I32)],
        compiler_params=pltpu.CompilerParams(vmem_limit_bytes=8 << 20),
    )(near, first, second, sent, got)


def plain(amplitudes, integrals, amp_mask, int_mask):
    kept = (
        amplitudes.reshape(OWN, TILES, TILE) * amp_mask.astype(BF16)[:, :, None]
    ).reshape(OWN, TILES * TILE)
    copies = jnp.broadcast_to(kept, (32,) + kept.shape)
    every = lax.all_to_all(copies, ("xh", "z", "core"), 0, 0).reshape(32 * OWN, TILES * TILE)
    ints = (
        integrals.reshape(RT, TILE, TILES, TILE) * int_mask.astype(BF16)[:, None, :, None]
    ).reshape(integrals.shape)
    value = lax.dot_general(every, ints, (((1,), (1,)), ((), ())), preferred_element_type=F32)
    parts = lax.all_to_all(value.reshape(8, TILE, RT * TILE), ("xl", "y"), 0, 0)
    return jnp.sum(parts, axis=0).astype(BF16)


RING = [(2 * z, 2 * ((z + 1) % 8)) for z in range(8)] + [(2 * z + 1, 2 * ((z + 7) % 8) + 1) for z in range(8)]

SHIFT = (0, 0, -1, -1, 1, 1, -2, -2, 2, 2, -3, -3, 3, 3, 4, 4)
OTHER = (0, 1, 0, 1, 1, 0, 0, 1, 1, 0, 0, 1, 1, 0, 0, 1)


def local(amplitudes, integrals, amp_mask, int_mask):
    z, core, y = (lax.axis_index(name).astype(I32) for name in ("z", "core", "y"))
    near = lax.axis_index("xl") == lax.axis_index("xh")
    up = 1 - 2 * core

    far = (z + up * jnp.asarray(SHIFT, I32)) & 7
    rows = (((far >> 1) - y) & 3) * 4 + (far & 1) * 2 + (core ^ jnp.asarray(OTHER, I32))

    own = pack(amplitudes, amp_mask)
    block = jnp.concatenate([own, swap(own, "core")], axis=0)
    held = [[block], [swap(block, "xh")]]
    for hop in range(1, 5):
        block = lax.ppermute(block if hop < 4 else block[:1], ("z", "core"), RING)
        other = swap(block, "xh")
        held[0] += [block, swap(block, "core")]
        held[1] += [other, swap(other, "core")]

    sums, coded = [], []
    over = jnp.zeros((META, TILE), I32)
    for chunk in range(2):
        own_part, *parts, over = chunk_sums(rows, int_mask, over, integrals, held[chunk])
        got = [
            lax.ppermute(part, "y", [(i, (i + d + 1) % 4) for i in range(4)]) for d, part in enumerate(parts)
        ]
        total, sent = add(over, own_part, got)
        sums.append(total)
        coded.append(sent)
    near = near.astype(I32).reshape(1)
    sent = choose(near, *coded)
    out, over = last(near, *sums, sent, swap(sent, "xl"))
    return lax.cond(
        jnp.max(over[META - 1]) > 0,
        lambda out: plain(amplitudes, integrals, amp_mask, int_mask),
        lambda out: out,
        out,
    )


def solution(mesh):
    fine = Mesh(mesh.devices.reshape(2, 8, 2, 2, 4), ("xh", "z", "core", "xl", "y"))
    blk, col = ("xh", "z", "core"), ("xl", "y")
    return jax.shard_map(
        local, mesh=fine, in_specs=(P(blk, col),) * 4, out_specs=P(col, blk), check_vma=False
    )
```

time: 132 us -> 115 us (0.87)
  between operations: 14.2 us -> 0.82 us
  Pallas kernels: 43.2 us -> 34.1 us
  waiting for transfers between devices: 45.3 us -> 50.2 us
  local copies, waits for them, and re-layouts: 6.98 us -> 2.4 us
  starting transfers between devices: 21.3 us -> 25.6 us
    pallas_call x5 -> x3, Pallas kernels: 38.9 us -> 29.2 us  [the longest x2 29.1 us: chunk_sums(): pl.pallas_call(lambda *refs: chunk_kernel(sizes, *refs), in_specs=[SMEM,...]
    ppermute x11 -> x15, waiting for transfers between devices: 8.65 us -> 17.6 us  [swap(): return lax.ppermute(x, axis, [(0, 1), (1, 0)])]
    ppermute x11 -> x15, starting transfers between devices: 9.48 us -> 15.8 us  [swap(): return lax.ppermute(x, axis, [(0, 1), (1, 0)])]
    unnamed x16 -> x12, local copies, waits for them, and re-layouts: 6.48 us -> 2.39 us
    ppermute x8 -> x4, waiting for transfers between devices: 23.2 us -> 21 us  [local(): block = lax.ppermute(block if hop < 4 else block[:1], ('z', 'core'), RING)]
    ppermute x8 -> x4, starting transfers between devices: 4.26 us -> 2.08 us  [local(): block = lax.ppermute(block if hop < 4 else block[:1], ('z', 'core'), RING)]
    ppermute x6, waiting for transfers between devices: 13.4 us -> 11.6 us  [local(): lax.ppermute(part, 'y', [(i, (i + d + 1) % 4) for i in range(4)])]
  transfers between devices with their start and end apart: 25 -> 25, of which waited for: 9 -> 10; matrix products, arithmetic and copies ran while one was open for 0% -> 1% of each run, Pallas kernels for 30% -> 27%
where the time goes in v3:
time: 115 us
  waiting for transfers between devices  50.2 us (44%)
  Pallas kernels  34.1 us (30%)
  starting transfers between devices  25.6 us (22%)
  local copies, waits for them, and re-layouts  2.4 us (2%)
  other arithmetic  1.35 us (1%)
    pallas_call x2, Pallas kernels, chunk_sums(): pl.pallas_call(lambda *refs: chunk_kernel(sizes, *refs), in_specs=[SMEM,...  29.1 us
    ppermute x4, waiting for transfers between devices, local(): block = lax.ppermute(block if hop < 4 else block[:1], ('z', 'core'), RING)  21 us
    ppermute x15, waiting for transfers between devices, swap(): return lax.ppermute(x, axis, [(0, 1), (1, 0)])  17.6 us
    ppermute x15, starting transfers between devices, swap(): return lax.ppermute(x, axis, [(0, 1), (1, 0)])  15.8 us
    ppermute x6, waiting for transfers between devices, local(): lax.ppermute(part, 'y', [(i, (i + d + 1) % 4) for i in range(4)])  11.6 us
    ppermute x6, starting transfers between devices, local(): lax.ppermute(part, 'y', [(i, (i + d + 1) % 4) for i in range(4)])  7.72 us
    pallas_call x2, Pallas kernels, add(): pl.pallas_call(add_kernel, in_specs=[VMEM] * 5, out_specs=[VMEM] * 2, out...  2.86 us
    unnamed x12, local copies, waits for them, and re-layouts  2.39 us
  transfers between devices with their start and end apart: 25, of which 10 were waited for; matrix products, arithmetic and copies ran while one was open for 1% of the time, Pallas kernels for 27%

profile of v3, /device:TPU:24, one launch (start us, length us, event | category | flops | bytes accessed | tf_op | source)
XLA Modules:
  0.0 114.5 jit_solution(12968440057194616425)
XLA Ops:
  0.0 1.8 %shard_map.66 = bf16[1,608,128]{2,1,0:T(8,128)(2,1)S(1)} custom-call(bf16[32,4096]{1,0:T(8,128)(2,1)} %amps_ref.1, s32[32,32]{1,0:T(8,128)} %mask_ref.1), custom_call_target="tpu_custom_call" | custom-call | tf_op jit(solution)/shard_map/pallas_call | solution.py:68
  1.9 1.4 %collective-permute-done = bf16[1,608,128]{2,1,0:T(8,128)(2,1)S(1)} collective-permute-done((bf16[1,608,128]{2,1,0:T(8,128)(2,1)S(1)}, bf16[1,608,128]{2,1,0:T(8,128)(2,1)S(1)}, u32[]{:S(2)}, u32[]{:S(2)}) %collective-permute-start) | collective-permute-done | bytes 155680 | tf_op jit(solution)/shard_map/ppermute | solution.py:28
  3.3 2.0 %collective-permute-start.1 = (bf16[2,608,128]{2,1,0:T(8,128)(2,1)S(1)}, bf16[2,608,128]{2,1,0:T(8,128)(2,1)S(1)}, u32[]{:S(2)}, u32[]{:S(2)}) collective-permute-start(bf16[2,608,128]{2,1,0:T(8,128)(2,1)S(1)} %pad_maximum_fusion.refs_4_), channel_id=1, source_target_pairs={{0,16},{16,32},{32,48},{48,64},{64,80},{80,96},{96,112},{112,0},{8... | collective-permute-start | bytes 933896 | tf_op jit(solution)/shard_map/ppermute | solution.py:286
  5.3 8.8 %collective-permute-done.1.refs_5_ = bf16[2,608,128]{2,1,0:T(8,128)(2,1)S(1)} collective-permute-done((bf16[2,608,128]{2,1,0:T(8,128)(2,1)S(1)}, bf16[2,608,128]{2,1,0:T(8,128)(2,1)S(1)}, u32[]{:S(2)}, u32[]{:S(2)}) %collective-permute-start.1) | collective-permute-done | bytes 311328 | tf_op jit(solution)/shard_map/ppermute | solution.py:286
  14.1 8.1 %collective-permute-done.3.refs_7_ = bf16[2,608,128]{2,1,0:T(8,128)(2,1)S(1)} collective-permute-done((bf16[2,608,128]{2,1,0:T(8,128)(2,1)S(1)}, bf16[2,608,128]{2,1,0:T(8,128)(2,1)S(1)}, u32[]{:S(2)}, u32[]{:S(2)}) %collective-permute-start.3) | collective-permute-done | bytes 311328 | tf_op jit(solution)/shard_map/ppermute | solution.py:286
  22.2 3.0 %collective-permute-start.13 = (bf16[2,608,128]{2,1,0:T(8,128)(2,1)S(1)}, bf16[2,608,128]{2,1,0:T(8,128)(2,1)S(1)}, u32[]{:S(2)}, u32[]{:S(2)}) collective-permute-start(bf16[2,608,128]{2,1,0:T(8,128)(2,1)S(1)} %collective-permute-done.1.refs_5_), channel_id=1, source_target_pairs={{0,128},{128,0},{1,129},{129,1},{2,130},{130,2},{3,131},{131,3},{4... | collective-permute-start | bytes 933896 | tf_op jit(solution)/shard_map/ppermute | solution.py:28
  25.2 0.5 collective-permute-start.2
  25.8 0.5 collective-permute-start.15
  26.3 4.1 %collective-permute-done.5.refs_9_ = bf16[2,608,128]{2,1,0:T(8,128)(2,1)S(1)} collective-permute-done((bf16[2,608,128]{2,1,0:T(8,128)(2,1)S(1)}, bf16[2,608,128]{2,1,0:T(8,128)(2,1)S(1)}, u32[]{:S(2)}, u32[]{:S(2)}) %collective-permute-start.5) | collective-permute-done | bytes 311328 | tf_op jit(solution)/shard_map/ppermute | solution.py:286
  30.5 3.4 %collective-permute-done.13.refs_5_ = bf16[2,608,128]{2,1,0:T(8,128)(2,1)S(1)} collective-permute-done((bf16[2,608,128]{2,1,0:T(8,128)(2,1)S(1)}, bf16[2,608,128]{2,1,0:T(8,128)(2,1)S(1)}, u32[]{:S(2)}, u32[]{:S(2)}) %collective-permute-start.13) | collective-permute-done | bytes 311328 | tf_op jit(solution)/shard_map/ppermute | solution.py:28
  34.0 3.0 %collective-permute-start.17 = (bf16[2,608,128]{2,1,0:T(8,128)(2,1)S(1)}, bf16[2,608,128]{2,1,0:T(8,128)(2,1)S(1)}, u32[]{:S(2)}, u32[]{:S(2)}) collective-permute-start(bf16[2,608,128]{2,1,0:T(8,128)(2,1)S(1)} %collective-permute-done.5.refs_9_), channel_id=1, source_target_pairs={{0,128},{128,0},{1,129},{129,1},{2,130},{130,2},{3,131},{131,3},{4... | collective-permute-start | bytes 933896 | tf_op jit(solution)/shard_map/ppermute | solution.py:28
  37.0 2.9 %collective-permute-start.19 = (bf16[1,608,128]{2,1,0:T(8,128)(2,1)S(1)}, bf16[1,608,128]{2,1,0:T(8,128)(2,1)S(1)}, u32[]{:S(2)}, u32[]{:S(2)}) collective-permute-start(bf16[1,608,128]{2,1,0:T(8,128)(2,1)S(1)} %collective-permute-done.7.refs_11_), channel_id=1, source_target_pairs={{0,128},{128,0},{1,129},{129,1},{2,130},{130,2},{3,131},{131,3},{4... | collective-permute-start | bytes 466952 | tf_op jit(solution)/shard_map/ppermute | solution.py:28
  39.9 0.7 collective-permute-done.15.refs_7_
  40.6 0.7 xor_add_fusion.refs_0_
  41.3 0.7 copy-done
  42.0 3.0 %collective-permute-start.12 = (bf16[2,608,128]{2,1,0:T(8,128)(2,1)S(1)}, bf16[2,608,128]{2,1,0:T(8,128)(2,1)S(1)}, u32[]{:S(2)}, u32[]{:S(2)}) collective-permute-start(bf16[2,608,128]{2,1,0:T(8,128)(2,1)S(1)} %pad_maximum_fusion.refs_4_), channel_id=1, source_target_pairs={{0,128},{128,0},{1,129},{129,1},{2,130},{130,2},{3,131},{131,3},{4... | collective-permute-start | bytes 933896 | tf_op jit(solution)/shard_map/ppermute | solution.py:28
  45.1 5.6 %collective-permute-done.19.refs_11_ = bf16[1,608,128]{2,1,0:T(8,128)(2,1)S(1)} collective-permute-done((bf16[1,608,128]{2,1,0:T(8,128)(2,1)S(1)}, bf16[1,608,128]{2,1,0:T(8,128)(2,1)S(1)}, u32[]{:S(2)}, u32[]{:S(2)}) %collective-permute-start.19) | collective-permute-done | bytes 155680 | tf_op jit(solution)/shard_map/ppermute | solution.py:28
  50.6 0.5 collective-permute-start.16
  51.7 1.0 copy-done.1
  52.6 14.5 %shard_map.67 = (f32[8,128,128]{2,1,0:T(8,128)S(1)}, s16[1040,128]{1,0:T(8,128)(2,1)S(1)}, s16[1040,128]{1,0:T(8,128)(2,1)}, s16[1040,128]{1,0:T(8,128)(2,1)S(1)}, s32[16,128]{1,0:T(8,128)S(1)}) custom-call(s32[16]{0:T(128)S(1)} %xor_add_fusion.refs_0_, s32[8,32]{1,0:T(8,128)} %refs_1_.3, s32[16,128]{1,0:T(8,128)S(1)} %broadcast_in_dim.8.refs_2_, ...), custom_call_target="tpu_custom_call" | custom-call | flops 10000000000 | bytes 16777216 | tf_op jit(solution)/shard_map/pallas_call | solution.py:163
  67.4 2.6 %collective-permute-start.10 = (s16[1040,128]{1,0:T(8,128)(2,1)}, s16[1040,128]{1,0:T(8,128)(2,1)S(1)}, u32[]{:S(2)}, u32[]{:S(2)}) collective-permute-start(s16[1040,128]{1,0:T(8,128)(2,1)} %get-tuple-element.40), channel_id=1, source_target_pairs={{0,2},{1,3},{2,0},{3,1},{4,6},{5,7},{6,4},{7,5},{8,10},{9,11},{10,... | collective-permute-start | bytes 798728 | tf_op jit(solution)/shard_map/ppermute | solution.py:296
  70.1 14.6 %shard_map.69 = (f32[8,128,128]{2,1,0:T(8,128)S(1)}, s16[1040,128]{1,0:T(8,128)(2,1)}, s16[1040,128]{1,0:T(8,128)(2,1)}, s16[1040,128]{1,0:T(8,128)(2,1)S(1)}, s32[16,128]{1,0:T(8,128)S(1)}) custom-call(s32[16]{0:T(128)S(1)} %xor_add_fusion.refs_0_, s32[8,32]{1,0:T(8,128)S(1)} %copy-done.3, s32[16,128]{1,0:T(8,128)S(1)} %get-tuple-element.37.over_ref.refs_2_, ...), custom_call_target="tpu_custom_call" | custom-call | flops 10000000000 | bytes 16777216 | tf_op jit(solution)/shard_map/pallas_call | solution.py:163
  84.7 3.3 %collective-permute-start.21 = (s16[1040,128]{1,0:T(8,128)(2,1)}, s16[1040,128]{1,0:T(8,128)(2,1)S(1)}, u32[]{:S(2)}, u32[]{:S(2)}) collective-permute-start(s16[1040,128]{1,0:T(8,128)(2,1)} %get-tuple-element.45), channel_id=1, source_target_pairs={{0,1},{1,2},{2,3},{3,0},{4,5},{5,6},{6,7},{7,4},{8,9},{9,10},{10,1... | collective-permute-start | bytes 798728 | tf_op jit(solution)/shard_map/ppermute | solution.py:296
  88.2 1.3 %collective-permute-start.23 = (s16[1040,128]{1,0:T(8,128)(2,1)S(1)}, s16[1040,128]{1,0:T(8,128)(2,1)S(1)}, u32[]{:S(2)}, u32[]{:S(2)}) collective-permute-start(s16[1040,128]{1,0:T(8,128)(2,1)S(1)} %get-tuple-element.47), channel_id=1, source_target_pairs={{0,3},{1,0},{2,1},{3,2},{4,7},{5,4},{6,5},{7,6},{8,11},{9,8},{10,9... | collective-permute-start | bytes 798728 | tf_op jit(solution)/shard_map/ppermute | solution.py:296
  89.5 1.4 %shard_map.68 = (f32[8,128,128]{2,1,0:T(8,128)S(1)}, s16[1040,128]{1,0:T(8,128)(2,1)S(1)}) custom-call(s32[16,128]{1,0:T(8,128)S(1)} %get-tuple-element.37.over_ref.refs_2_, f32[8,128,128]{2,1,0:T(8,128)S(1)} %get-tuple-element.38.own_ref, s16[1040,128]{1,0:T(8,128)(2,1)S(1)} %collective-permute-done.9.a_ref, ...), custom_call_target="tpu_custom_call" | custom-call | tf_op jit(solution)/shard_map/pallas_call | solution.py:204
  91.0 8.3 %collective-permute-done.21.a_ref = s16[1040,128]{1,0:T(8,128)(2,1)S(1)} collective-permute-done((s16[1040,128]{1,0:T(8,128)(2,1)}, s16[1040,128]{1,0:T(8,128)(2,1)S(1)}, u32[]{:S(2)}, u32[]{:S(2)}) %collective-permute-start.21) | collective-permute-done | bytes 266272 | tf_op jit(solution)/shard_map/ppermute | solution.py:296
  99.3 3.3 %collective-permute-done.23.c_ref = s16[1040,128]{1,0:T(8,128)(2,1)S(1)} collective-permute-done((s16[1040,128]{1,0:T(8,128)(2,1)S(1)}, s16[1040,128]{1,0:T(8,128)(2,1)S(1)}, u32[]{:S(2)}, u32[]{:S(2)}) %collective-permute-start.23) | collective-permute-done | bytes 266272 | tf_op jit(solution)/shard_map/ppermute | solution.py:296
  102.6 1.4 %shard_map.70 = (f32[8,128,128]{2,1,0:T(8,128)S(1)}, s16[1040,128]{1,0:T(8,128)(2,1)S(1)}) custom-call(s32[16,128]{1,0:T(8,128)S(1)} %get-tuple-element.43.over_ref, f32[8,128,128]{2,1,0:T(8,128)S(1)} %get-tuple-element.44.own_ref, s16[1040,128]{1,0:T(8,128)(2,1)S(1)} %collective-permute-done.21.a_ref, s16[1040,128]{1,0:T(8,128)(2,1)S(1)} %collective-permute-done.22.b_ref, ...), custom_call_target="tpu_custom_call" | custom-call | tf_op jit(solution)/shard_map/pallas_call | solution.py:204
  104.1 1.6 %collective-permute-start.24 = (s16[1040,128]{1,0:T(8,128)(2,1)S(1)}, s16[1040,128]{1,0:T(8,128)(2,1)S(1)}, u32[]{:S(2)}, u32[]{:S(2)}) collective-permute-start(s16[1040,128]{1,0:T(8,128)(2,1)S(1)} %shard_map.71.sent_ref), channel_id=1, source_target_pairs={{0,4},{4,0},{1,5},{5,1},{2,6},{6,2},{3,7},{7,3},{8,12},{12,8},{9,1... | collective-permute-start | bytes 798728 | tf_op jit(solution)/shard_map/ppermute | solution.py:28
  105.7 6.5 %collective-permute-done.24.got_ref = s16[1040,128]{1,0:T(8,128)(2,1)S(1)} collective-permute-done((s16[1040,128]{1,0:T(8,128)(2,1)S(1)}, s16[1040,128]{1,0:T(8,128)(2,1)S(1)}, u32[]{:S(2)}, u32[]{:S(2)}) %collective-permute-start.24) | collective-permute-done | bytes 266272 | tf_op jit(solution)/shard_map/ppermute | solution.py:28
  112.5 0.6 slice_reduce_fusion
  113.8 0.7 copy-done.5
  (43 shorter events, 1.8 us)
Async XLA Ops:
  1.8 1.5 %collective-permute-start = (bf16[1,608,128]{2,1,0:T(8,128)(2,1)S(1)}, bf16[1,608,128]{2,1,0:T(8,128)(2,1)S(1)}, u32[]{:S(2)}, u32[]{:S(2)}) collective-permute-start(bf16[1,608,128]{2,1,0:T(8,128)(2,1)S(1)} %shard_map.66), channel_id=1, source_target_pairs={{0,8},{8,0},{1,9},{9,1},{2,10},{10,2},{3,11},{11,3},{4,12},{12,4},... | collective-permute-start | bytes 466952 | tf_op jit(solution)/shard_map/ppermute | solution.py:28
  3.3 10.8 %collective-permute-start.1 = (bf16[2,608,128]{2,1,0:T(8,128)(2,1)S(1)}, bf16[2,608,128]{2,1,0:T(8,128)(2,1)S(1)}, u32[]{:S(2)}, u32[]{:S(2)}) collective-permute-start(bf16[2,608,128]{2,1,0:T(8,128)(2,1)S(1)} %pad_maximum_fusion.refs_4_), channel_id=1, source_target_pairs={{0,16},{16,32},{32,48},{48,64},{64,80},{80,96},{96,112},{112,0},{8... | collective-permute-start | bytes 933896 | tf_op jit(solution)/shard_map/ppermute | solution.py:286
  14.1 8.1 %collective-permute-start.3 = (bf16[2,608,128]{2,1,0:T(8,128)(2,1)S(1)}, bf16[2,608,128]{2,1,0:T(8,128)(2,1)S(1)}, u32[]{:S(2)}, u32[]{:S(2)}) collective-permute-start(bf16[2,608,128]{2,1,0:T(8,128)(2,1)S(1)} %collective-permute-done.1.refs_5_), channel_id=1, source_target_pairs={{0,16},{16,32},{32,48},{48,64},{64,80},{80,96},{96,112},{112,0},{8... | collective-permute-start | bytes 933896 | tf_op jit(solution)/shard_map/ppermute | solution.py:286
  22.2 8.1 %collective-permute-start.5 = (bf16[2,608,128]{2,1,0:T(8,128)(2,1)S(1)}, bf16[2,608,128]{2,1,0:T(8,128)(2,1)S(1)}, u32[]{:S(2)}, u32[]{:S(2)}) collective-permute-start(bf16[2,608,128]{2,1,0:T(8,128)(2,1)S(1)} %collective-permute-done.3.refs_7_), channel_id=1, source_target_pairs={{0,16},{16,32},{32,48},{48,64},{64,80},{80,96},{96,112},{112,0},{8... | collective-permute-start | bytes 933896 | tf_op jit(solution)/shard_map/ppermute | solution.py:286
  22.2 11.7 %collective-permute-start.13 = (bf16[2,608,128]{2,1,0:T(8,128)(2,1)S(1)}, bf16[2,608,128]{2,1,0:T(8,128)(2,1)S(1)}, u32[]{:S(2)}, u32[]{:S(2)}) collective-permute-start(bf16[2,608,128]{2,1,0:T(8,128)(2,1)S(1)} %collective-permute-done.1.refs_5_), channel_id=1, source_target_pairs={{0,128},{128,0},{1,129},{129,1},{2,130},{130,2},{3,131},{131,3},{4... | collective-permute-start | bytes 933896 | tf_op jit(solution)/shard_map/ppermute | solution.py:28
  25.2 11.7 %collective-permute-start.2 = (bf16[2,608,128]{2,1,0:T(8,128)(2,1)S(1)}, bf16[2,608,128]{2,1,0:T(8,128)(2,1)S(1)}, u32[]{:S(2)}, u32[]{:S(2)}) collective-permute-start(bf16[2,608,128]{2,1,0:T(8,128)(2,1)S(1)} %collective-permute-done.1.refs_5_), channel_id=1, source_target_pairs={{0,8},{8,0},{1,9},{9,1},{2,10},{10,2},{3,11},{11,3},{4,12},{12,4},... | collective-permute-start | bytes 933896 | tf_op jit(solution)/shard_map/ppermute | solution.py:28
  25.8 14.9 %collective-permute-start.15 = (bf16[2,608,128]{2,1,0:T(8,128)(2,1)S(1)}, bf16[2,608,128]{2,1,0:T(8,128)(2,1)S(1)}, u32[]{:S(2)}, u32[]{:S(2)}) collective-permute-start(bf16[2,608,128]{2,1,0:T(8,128)(2,1)S(1)} %collective-permute-done.3.refs_7_), channel_id=1, source_target_pairs={{0,128},{128,0},{1,129},{129,1},{2,130},{130,2},{3,131},{131,3},{4... | collective-permute-start | bytes 933896 | tf_op jit(solution)/shard_map/ppermute | solution.py:28
  30.3 6.7 %collective-permute-start.7 = (bf16[1,608,128]{2,1,0:T(8,128)(2,1)S(1)}, bf16[1,608,128]{2,1,0:T(8,128)(2,1)S(1)}, u32[]{:S(2)}, u32[]{:S(2)}) collective-permute-start(bf16[1,608,128]{2,1,0:T(8,128)(2,1)S(1)} %slice.8), channel_id=1, source_target_pairs={{0,16},{16,32},{32,48},{48,64},{64,80},{80,96},{96,112},{112,0},{8... | collective-permute-start | bytes 466952 | tf_op jit(solution)/shard_map/ppermute | solution.py:286
  30.4 10.9 %collective-permute-start.4 = (bf16[2,608,128]{2,1,0:T(8,128)(2,1)S(1)}, bf16[2,608,128]{2,1,0:T(8,128)(2,1)S(1)}, u32[]{:S(2)}, u32[]{:S(2)}) collective-permute-start(bf16[2,608,128]{2,1,0:T(8,128)(2,1)S(1)} %collective-permute-done.3.refs_7_), channel_id=1, source_target_pairs={{0,8},{8,0},{1,9},{9,1},{2,10},{10,2},{3,11},{11,3},{4,12},{12,4},... | collective-permute-start | bytes 933896 | tf_op jit(solution)/shard_map/ppermute | solution.py:28
  34.0 17.2 %collective-permute-start.17 = (bf16[2,608,128]{2,1,0:T(8,128)(2,1)S(1)}, bf16[2,608,128]{2,1,0:T(8,128)(2,1)S(1)}, u32[]{:S(2)}, u32[]{:S(2)}) collective-permute-start(bf16[2,608,128]{2,1,0:T(8,128)(2,1)S(1)} %collective-permute-done.5.refs_9_), channel_id=1, source_target_pairs={{0,128},{128,0},{1,129},{129,1},{2,130},{130,2},{3,131},{131,3},{4... | collective-permute-start | bytes 933896 | tf_op jit(solution)/shard_map/ppermute | solution.py:28
  37.0 14.3 %collective-permute-start.6 = (bf16[2,608,128]{2,1,0:T(8,128)(2,1)S(1)}, bf16[2,608,128]{2,1,0:T(8,128)(2,1)}, u32[]{:S(2)}, u32[]{:S(2)}) collective-permute-start(bf16[2,608,128]{2,1,0:T(8,128)(2,1)S(1)} %collective-permute-done.5.refs_9_), channel_id=1, source_target_pairs={{0,8},{8,0},{1,9},{9,1},{2,10},{10,2},{3,11},{11,3},{4,12},{12,4},... | collective-permute-start | bytes 933896 | tf_op jit(solution)/shard_map/ppermute | solution.py:28
  37.0 13.6 %collective-permute-start.19 = (bf16[1,608,128]{2,1,0:T(8,128)(2,1)S(1)}, bf16[1,608,128]{2,1,0:T(8,128)(2,1)S(1)}, u32[]{:S(2)}, u32[]{:S(2)}) collective-permute-start(bf16[1,608,128]{2,1,0:T(8,128)(2,1)S(1)} %collective-permute-done.7.refs_11_), channel_id=1, source_target_pairs={{0,128},{128,0},{1,129},{129,1},{2,130},{130,2},{3,131},{131,3},{4... | collective-permute-start | bytes 466952 | tf_op jit(solution)/shard_map/ppermute | solution.py:28
  40.6 10.0 %collective-permute-start.8 = (bf16[1,608,128]{2,1,0:T(8,128)(2,1)S(1)}, bf16[1,608,128]{2,1,0:T(8,128)(2,1)S(1)}, u32[]{:S(2)}, u32[]{:S(2)}) collective-permute-start(bf16[1,608,128]{2,1,0:T(8,128)(2,1)S(1)} %collective-permute-done.7.refs_11_), channel_id=1, source_target_pairs={{0,8},{8,0},{1,9},{9,1},{2,10},{10,2},{3,11},{11,3},{4,12},{12,4},... | collective-permute-start | bytes 466952 | tf_op jit(solution)/shard_map/ppermute | solution.py:28
  41.3 0.7 copy-start
  42.0 25.1 %collective-permute-start.12 = (bf16[2,608,128]{2,1,0:T(8,128)(2,1)S(1)}, bf16[2,608,128]{2,1,0:T(8,128)(2,1)S(1)}, u32[]{:S(2)}, u32[]{:S(2)}) collective-permute-start(bf16[2,608,128]{2,1,0:T(8,128)(2,1)S(1)} %pad_maximum_fusion.refs_4_), channel_id=1, source_target_pairs={{0,128},{128,0},{1,129},{129,1},{2,130},{130,2},{3,131},{131,3},{4... | collective-permute-start | bytes 933896 | tf_op jit(solution)/shard_map/ppermute | solution.py:28
  50.6 16.8 %collective-permute-start.14 = (bf16[2,608,128]{2,1,0:T(8,128)(2,1)S(1)}, bf16[2,608,128]{2,1,0:T(8,128)(2,1)S(1)}, u32[]{:S(2)}, u32[]{:S(2)}) collective-permute-start(bf16[2,608,128]{2,1,0:T(8,128)(2,1)S(1)} %collective-permute-done.13.refs_5_), channel_id=1, source_target_pairs={{0,8},{8,0},{1,9},{9,1},{2,10},{10,2},{3,11},{11,3},{4,12},{12,4},... | collective-permute-start | bytes 933896 | tf_op jit(solution)/shard_map/ppermute | solution.py:28
  50.6 19.4 %collective-permute-start.16 = (bf16[2,608,128]{2,1,0:T(8,128)(2,1)S(1)}, bf16[2,608,128]{2,1,0:T(8,128)(2,1)S(1)}, u32[]{:S(2)}, u32[]{:S(2)}) collective-permute-start(bf16[2,608,128]{2,1,0:T(8,128)(2,1)S(1)} %collective-permute-done.15.refs_7_), channel_id=1, source_target_pairs={{0,8},{8,0},{1,9},{9,1},{2,10},{10,2},{3,11},{11,3},{4,12},{12,4},... | collective-permute-start | bytes 933896 | tf_op jit(solution)/shard_map/ppermute | solution.py:28
  51.2 18.9 %collective-permute-start.20 = (bf16[1,608,128]{2,1,0:T(8,128)(2,1)S(1)}, bf16[1,608,128]{2,1,0:T(8,128)(2,1)S(1)}, u32[]{:S(2)}, u32[]{:S(2)}) collective-permute-start(bf16[1,608,128]{2,1,0:T(8,128)(2,1)S(1)} %collective-permute-done.19.refs_11_), channel_id=1, source_target_pairs={{0,8},{8,0},{1,9},{9,1},{2,10},{10,2},{3,11},{11,3},{4,12},{12,4},... | collective-permute-start | bytes 466952 | tf_op jit(solution)/shard_map/ppermute | solution.py:28
  51.2 18.8 %collective-permute-start.18 = (bf16[2,608,128]{2,1,0:T(8,128)(2,1)S(1)}, bf16[2,608,128]{2,1,0:T(8,128)(2,1)S(1)}, u32[]{:S(2)}, u32[]{:S(2)}) collective-permute-start(bf16[2,608,128]{2,1,0:T(8,128)(2,1)S(1)} %collective-permute-done.17.refs_9_), channel_id=1, source_target_pairs={{0,8},{8,0},{1,9},{9,1},{2,10},{10,2},{3,11},{11,3},{4,12},{12,4},... | collective-permute-start | bytes 933896 | tf_op jit(solution)/shard_map/ppermute | solution.py:28
  51.7 1.0 copy-start.1
  52.6 17.4 %copy-start.3 = (s32[8,32]{1,0:T(8,128)S(1)}, s32[8,32]{1,0:T(8,128)}, u32[]{:S(2)}) copy-start(s32[8,32]{1,0:T(8,128)} %refs_1_.3) | copy-start | bytes 3076
  52.6 17.4 %copy-start.4 = (bf16[1024,4096]{1,0:T(8,128)(2,1)S(1)}, bf16[1024,4096]{1,0:T(8,128)(2,1)}, u32[]{:S(2)}) copy-start(bf16[1024,4096]{1,0:T(8,128)(2,1)} %refs_3_.3) | copy-start | bytes 25165828
  67.1 21.1 %collective-permute-start.9 = (s16[1040,128]{1,0:T(8,128)(2,1)S(1)}, s16[1040,128]{1,0:T(8,128)(2,1)S(1)}, u32[]{:S(2)}, u32[]{:S(2)}) collective-permute-start(s16[1040,128]{1,0:T(8,128)(2,1)S(1)} %get-tuple-element.39), channel_id=1, source_target_pairs={{0,1},{1,2},{2,3},{3,0},{4,5},{5,6},{6,7},{7,4},{8,9},{9,10},{10,1... | collective-permute-start | bytes 798728 | tf_op jit(solution)/shard_map/ppermute | solution.py:296
  67.4 22.1 %collective-permute-start.10 = (s16[1040,128]{1,0:T(8,128)(2,1)}, s16[1040,128]{1,0:T(8,128)(2,1)S(1)}, u32[]{:S(2)}, u32[]{:S(2)}) collective-permute-start(s16[1040,128]{1,0:T(8,128)(2,1)} %get-tuple-element.40), channel_id=1, source_target_pairs={{0,2},{1,3},{2,0},{3,1},{4,6},{5,7},{6,4},{7,5},{8,10},{9,11},{10,... | collective-permute-start | bytes 798728 | tf_op jit(solution)/shard_map/ppermute | solution.py:296
  70.0 19.5 %collective-permute-start.11 = (s16[1040,128]{1,0:T(8,128)(2,1)S(1)}, s16[1040,128]{1,0:T(8,128)(2,1)S(1)}, u32[]{:S(2)}, u32[]{:S(2)}) collective-permute-start(s16[1040,128]{1,0:T(8,128)(2,1)S(1)} %get-tuple-element.41), channel_id=1, source_target_pairs={{0,3},{1,0},{2,1},{3,2},{4,7},{5,4},{6,5},{7,6},{8,11},{9,8},{10,9... | collective-permute-start | bytes 798728 | tf_op jit(solution)/shard_map/ppermute | solution.py:296
  70.1 43.7 %copy-start.2 = (s32[32,32]{1,0:T(8,128)S(1)}, s32[32,32]{1,0:T(8,128)}, u32[]{:S(2)}) copy-start(s32[32,32]{1,0:T(8,128)} %mask_ref.1) | copy-start | bytes 12292
  84.7 14.6 %collective-permute-start.21 = (s16[1040,128]{1,0:T(8,128)(2,1)}, s16[1040,128]{1,0:T(8,128)(2,1)S(1)}, u32[]{:S(2)}, u32[]{:S(2)}) collective-permute-start(s16[1040,128]{1,0:T(8,128)(2,1)} %get-tuple-element.45), channel_id=1, source_target_pairs={{0,1},{1,2},{2,3},{3,0},{4,5},{5,6},{6,7},{7,4},{8,9},{9,10},{10,1... | collective-permute-start | bytes 798728 | tf_op jit(solution)/shard_map/ppermute | solution.py:296
  88.0 11.3 %collective-permute-start.22 = (s16[1040,128]{1,0:T(8,128)(2,1)}, s16[1040,128]{1,0:T(8,128)(2,1)S(1)}, u32[]{:S(2)}, u32[]{:S(2)}) collective-permute-start(s16[1040,128]{1,0:T(8,128)(2,1)} %get-tuple-element.46), channel_id=1, source_target_pairs={{0,2},{1,3},{2,0},{3,1},{4,6},{5,7},{6,4},{7,5},{8,10},{9,11},{10,... | collective-permute-start | bytes 798728 | tf_op jit(solution)/shard_map/ppermute | solution.py:296
  88.2 14.4 %collective-permute-start.23 = (s16[1040,128]{1,0:T(8,128)(2,1)S(1)}, s16[1040,128]{1,0:T(8,128)(2,1)S(1)}, u32[]{:S(2)}, u32[]{:S(2)}) collective-permute-start(s16[1040,128]{1,0:T(8,128)(2,1)S(1)} %get-tuple-element.47), channel_id=1, source_target_pairs={{0,3},{1,0},{2,1},{3,2},{4,7},{5,4},{6,5},{7,6},{8,11},{9,8},{10,9... | collective-permute-start | bytes 798728 | tf_op jit(solution)/shard_map/ppermute | solution.py:296
  104.1 8.0 %collective-permute-start.24 = (s16[1040,128]{1,0:T(8,128)(2,1)S(1)}, s16[1040,128]{1,0:T(8,128)(2,1)S(1)}, u32[]{:S(2)}, u32[]{:S(2)}) collective-permute-start(s16[1040,128]{1,0:T(8,128)(2,1)S(1)} %shard_map.71.sent_ref), channel_id=1, source_target_pairs={{0,4},{4,0},{1,5},{5,1},{2,6},{6,2},{3,7},{7,3},{8,12},{12,8},{9,1... | collective-permute-start | bytes 798728 | tf_op jit(solution)/shard_map/ppermute | solution.py:28
  113.8 0.7 copy-start.5

commit v4 on v3

--- a/solution.py
+++ b/solution.py
@@ -102,12 +102,17 @@
     return jnp.where(row < RT, powers, flag).astype(I16)
 
 
-def chunk_kernel(sizes, row_ref, mask_ref, before_ref, ints_ref, *refs):
-    ins, (own_ref, a_ref, b_ref, c_ref, over_ref, got, amps, held, sem) = refs[: len(sizes)], refs[len(sizes) :]
-    loads = [
-        pltpu.make_async_copy(ints_ref.at[pl.ds(j * 2 * TILE, 2 * TILE), :], held.at[j], sem.at[j])
-        for j in range(RT // 2)
-    ]
+def chunk_kernel(sizes, mask, row_ref, *refs):
+    if mask:
+        mask_ref, *refs = refs
+    before_ref, ints_ref, *refs = refs
+    ins, refs = refs[: len(sizes)], refs[len(sizes) :]
+    own_ref, a_ref, b_ref, c_ref, over_ref, *refs = refs
+    if mask:
+        kept_ref, *refs = refs
+    got, amps, held, sem = refs
+    blocks = [pl.ds(j * 2 * TILE, 2 * TILE) for j in range(RT // 2)]
+    loads = [pltpu.make_async_copy(ints_ref.at[rows, :], held.at[j], sem.at[0, j]) for j, rows in enumerate(blocks)]
     for load in loads:
         load.start()
     i = 0
@@ -127,59 +132,62 @@
                 amps[rows, t * TILE : (t + 1) * TILE] = value[n * OWN : (n + 1) * OWN, :]
         return jnp.maximum(over, place[:META, TILE - 1 :])
 
-    over = lax.fori_loop(0, i, unpack, jnp.zeros((META, 1), F32))
+    over = lax.fori_loop(0, i, unpack, jnp.zeros((META, 1), F32), unroll=4)
     over = jnp.maximum(jnp.broadcast_to(over, (META, TILE)).astype(I32), before_ref[...])
     over_ref[...] = over
     lane = lax.broadcasted_iota(I32, (TILE, TILE), 1)
-    for load in loads:
+    powers = [jnp.zeros((TILE, TILE), F32)] * 3
+    stores = []
+    for j, load in enumerate(loads):
         load.wait()
-
-    def multiply(j, powers):
-        for n in range(2):
-            for t in range(TILES):
-                kept = jnp.where(mask_ref[2 * j + n, t] > 0, 1.0, 0.0).astype(BF16)
-                part = (j, slice(n * TILE, (n + 1) * TILE), slice(t * TILE, (t + 1) * TILE))
-                held[part] = held[part] * kept
+        if mask:
+            for n in range(2):
+                for t in range(TILES):
+                    kept = jnp.where(mask_ref[2 * j + n, t] > 0, 1.0, 0.0).astype(BF16)
+                    part = (j, slice(n * TILE, (n + 1) * TILE), slice(t * TILE, (t + 1) * TILE))
+                    held[part] = held[part] * kept
+            stores.append(pltpu.make_async_copy(held.at[j], kept_ref.at[blocks[j], :], sem.at[1, j]))
+            stores[j].start()
         value = lax.dot_general(amps[...], held[j], (((1,), (1,)), ((), ())), preferred_element_type=F32)
         for n in range(2):
             t = 2 * j + n
             own_ref[t] = value[:TILE, n * TILE : (n + 1) * TILE]
-            new = []
             for d, out in enumerate((a_ref, b_ref, c_ref)):
                 coded, power = code(value[(d + 1) * TILE : (d + 2) * TILE, n * TILE : (n + 1) * TILE])
-                out[pl.ds(pl.multiple_of(t * TILE, TILE), TILE), :] = coded
-                new.append(jnp.where(lane == t, power, powers[d]))
-            powers = tuple(new)
-        return powers
-
-    powers = lax.fori_loop(0, RT // 2, multiply, (jnp.zeros((TILE, TILE), F32),) * 3)
+                out[t * TILE : (t + 1) * TILE, :] = coded
+                powers[d] = jnp.where(lane == t, power, powers[d])
     for d, out in enumerate((a_ref, b_ref, c_ref)):
         out[RT * TILE :, :] = powers_and_flags(powers[d], over)
-
-
-def chunk_sums(rows, mask, before, ints, messages):
+    for store in stores:
+        store.wait()
+
+
+def chunk_sums(rows, before, ints, messages, mask=None):
     sizes = [m.shape[0] for m in messages]
+    masks = [] if mask is None else [mask]
     coded = jax.ShapeDtypeStruct((RT * TILE + META, TILE), I16)
-    return pl.pallas_call(
-        lambda *refs: chunk_kernel(sizes, *refs),
-        in_specs=[SMEM, SMEM, VMEM, pl.BlockSpec(memory_space=pl.ANY)] + [VMEM] * len(sizes),
-        out_specs=[VMEM] * 5,
+    anywhere = pl.BlockSpec(memory_space=pl.ANY)
+    return pl.pallas_call(
+        lambda *refs: chunk_kernel(sizes, mask is not None, *refs),
+        in_specs=[SMEM] * (1 + len(masks)) + [VMEM, anywhere] + [VMEM] * len(sizes),
+        out_specs=[VMEM] * 5 + [anywhere] * len(masks),
         out_shape=[
             jax.ShapeDtypeStruct((RT, TILE, TILE), F32),
             coded,
             coded,
             coded,
             jax.ShapeDtypeStruct((META, TILE), I32),
-        ],
+        ]
+        + [jax.ShapeDtypeStruct(ints.shape, BF16)] * len(masks),
         scratch_shapes=[
             pltpu.VMEM((sum(sizes), MSG, TILE), BF16),
             pltpu.VMEM((sum(sizes) * OWN, TILES * TILE), BF16),
             pltpu.VMEM((RT // 2, 2 * TILE, TILES * TILE), BF16),
-            pltpu.SemaphoreType.DMA((RT // 2,)),
+            pltpu.SemaphoreType.DMA((2, RT // 2)),
         ],
         compiler_params=pltpu.CompilerParams(vmem_limit_bytes=44 << 20),
         cost_estimate=pl.CostEstimate(flops=10_000_000_000, bytes_accessed=16 << 20, transcendentals=0),
-    )(rows, mask, before, ints, *messages)
+    )(rows, *masks, before, ints, *messages)
 
 
 def add_kernel(over_ref, own_ref, a_ref, b_ref, c_ref, sum_ref, out_ref):
@@ -279,25 +287,32 @@
     far = (z + up * jnp.asarray(SHIFT, I32)) & 7
     rows = (((far >> 1) - y) & 3) * 4 + (far & 1) * 2 + (core ^ jnp.asarray(OTHER, I32))
 
-    own = pack(amplitudes, amp_mask)
-    block = jnp.concatenate([own, swap(own, "core")], axis=0)
-    held = [[block], [swap(block, "xh")]]
+    first = pack(amplitudes, amp_mask)
+    second = swap(first, "core")
+    block = jnp.concatenate([first, second], axis=0)
+    held, far_blocks = [block], [swap(block, "xh")]
     for hop in range(1, 5):
-        block = lax.ppermute(block if hop < 4 else block[:1], ("z", "core"), RING)
-        other = swap(block, "xh")
-        held[0] += [block, swap(block, "core")]
-        held[1] += [other, swap(other, "core")]
-
-    sums, coded = [], []
+        first = lax.ppermute(first, ("z", "core"), RING)
+        block = first
+        if hop < 4:
+            second = lax.ppermute(second, ("z", "core"), RING)
+            block = jnp.concatenate([first, second], axis=0)
+        held += [block, swap(block, "core")]
+        far_blocks.append(swap(block, "xh"))
+
+    def spread(parts):
+        return [lax.ppermute(part, "y", [(i, (i + d + 1) % 4) for i in range(4)]) for d, part in enumerate(parts)]
+
     over = jnp.zeros((META, TILE), I32)
-    for chunk in range(2):
-        own_part, *parts, over = chunk_sums(rows, int_mask, over, integrals, held[chunk])
-        got = [
-            lax.ppermute(part, "y", [(i, (i + d + 1) % 4) for i in range(4)]) for d, part in enumerate(parts)
-        ]
-        total, sent = add(over, own_part, got)
-        sums.append(total)
-        coded.append(sent)
+    own_part, *parts, over, kept_ints = chunk_sums(rows, over, integrals, held, int_mask)
+    over, *far_blocks[2:] = lax.optimization_barrier((over, *far_blocks[2:]))
+    held = far_blocks[:1]
+    for block in far_blocks[1:]:
+        held += [block, swap(block, "core")]
+    sums, coded = zip(add(over, own_part, spread(parts)))
+    own_part, *parts, over = chunk_sums(rows, over, kept_ints, held)
+    total, sent = add(over, own_part, spread(parts))
+    sums, coded = (*sums, total), (*coded, sent)
     near = near.astype(I32).reshape(1)
     sent = choose(near, *coded)
     out, over = last(near, *sums, sent, swap(sent, "xl"))

time: 115 us -> 123 us (1.070); the launches traced: 115 us -> 121 us
  starting transfers between devices: 25.6 us -> 41.2 us
  waiting for transfers between devices: 50.2 us -> 41.3 us
  local copies, waits for them, and re-layouts: 2.4 us -> 0.81 us
  Pallas kernels: 34.1 us -> 35.4 us
    ppermute x10 -> x13, starting transfers between devices: 9.8 us -> 26.6 us  [the longest x6 21 us: spread(): lax.ppermute(part, 'y', [(i, (i + d + 1) % 4) for i in range(4)])]
    ppermute x15, waiting for transfers between devices: 17.6 us -> 11.7 us  [swap(): return lax.ppermute(x, axis, [(0, 1), (1, 0)])]
    ppermute x10 -> x13, waiting for transfers between devices: 32.6 us -> 29.6 us  [the longest x4 13.3 us: local(): first = lax.ppermute(first, ('z', 'core'), RING)]
    unnamed x12 -> x9, local copies, waits for them, and re-layouts: 2.39 us -> 0.74 us
    pallas_call x2, Pallas kernels: 29.1 us -> 30.3 us  [chunk_sums(): pl.pallas_call(lambda *refs: chunk_kernel(sizes, mask is not None, *refs)...]
  transfers between devices with their start and end apart: 25 -> 28, of which waited for: 10 -> 10; matrix products, arithmetic and copies ran while one was open for 1% -> 1% of each run, Pallas kernels for 27% -> 26%
where the time goes in v4:
time: 123 us; the launch traced here: 121 us
  waiting for transfers between devices  41.3 us (34%)
  starting transfers between devices  41.2 us (33%)
  Pallas kernels  35.4 us (29%)
  other arithmetic  1.35 us (1%)
    pallas_call x2, Pallas kernels, chunk_sums(): pl.pallas_call(lambda *refs: chunk_kernel(sizes, mask is not None, *refs)...  30.3 us
    ppermute x6, starting transfers between devices, spread(): lax.ppermute(part, 'y', [(i, (i + d + 1) % 4) for i in range(4)])  21 us
    ppermute x15, starting transfers between devices, swap(): return lax.ppermute(x, axis, [(0, 1), (1, 0)])  14.6 us
    ppermute x4, waiting for transfers between devices, local(): first = lax.ppermute(first, ('z', 'core'), RING)  13.3 us
    ppermute x6, waiting for transfers between devices, spread(): lax.ppermute(part, 'y', [(i, (i + d + 1) % 4) for i in range(4)])  11.8 us
    ppermute x15, waiting for transfers between devices, swap(): return lax.ppermute(x, axis, [(0, 1), (1, 0)])  11.7 us
    ppermute x3, waiting for transfers between devices, local(): second = lax.ppermute(second, ('z', 'core'), RING)  4.46 us
    ppermute x3, starting transfers between devices, local(): second = lax.ppermute(second, ('z', 'core'), RING)  3.41 us
  transfers between devices with their start and end apart: 28, of which 10 were waited for; matrix products, arithmetic and copies ran while one was open for 1% of the time, Pallas kernels for 26%

profile of v4, /device:TPU:24, one launch (start us, length us, event | category | flops | bytes accessed | tf_op | source)
XLA Modules:
  0.0 121.1 jit_solution(11647109987197804603)
XLA Ops:
  0.0 1.8 %shard_map.66 = bf16[1,608,128]{2,1,0:T(8,128)(2,1)S(1)} custom-call(bf16[32,4096]{1,0:T(8,128)(2,1)} %amps_ref.1, s32[32,32]{1,0:T(8,128)} %mask_ref.1), custom_call_target="tpu_custom_call" | custom-call | tf_op jit(solution)/shard_map/pallas_call | solution.py:68
  1.9 2.0 %collective-permute-start.1 = (bf16[1,608,128]{2,1,0:T(8,128)(2,1)S(1)}, bf16[1,608,128]{2,1,0:T(8,128)(2,1)S(1)}, u32[]{:S(2)}, u32[]{:S(2)}) collective-permute-start(bf16[1,608,128]{2,1,0:T(8,128)(2,1)S(1)} %shard_map.66), channel_id=1, source_target_pairs={{0,16},{16,32},{32,48},{48,64},{64,80},{80,96},{96,112},{112,0},{8... | collective-permute-start | bytes 466952 | tf_op jit(solution)/shard_map/ppermute | solution.py:295
  3.9 1.9 %collective-permute-start.2 = (bf16[1,608,128]{2,1,0:T(8,128)(2,1)S(1)}, bf16[1,608,128]{2,1,0:T(8,128)(2,1)S(1)}, u32[]{:S(2)}, u32[]{:S(2)}) collective-permute-start(bf16[1,608,128]{2,1,0:T(8,128)(2,1)S(1)} %collective-permute-done), channel_id=1, source_target_pairs={{0,16},{16,32},{32,48},{48,64},{64,80},{80,96},{96,112},{112,0},{8... | collective-permute-start | bytes 466952 | tf_op jit(solution)/shard_map/ppermute | solution.py:298
  5.8 5.2 %collective-permute-done.1 = bf16[1,608,128]{2,1,0:T(8,128)(2,1)S(1)} collective-permute-done((bf16[1,608,128]{2,1,0:T(8,128)(2,1)S(1)}, bf16[1,608,128]{2,1,0:T(8,128)(2,1)S(1)}, u32[]{:S(2)}, u32[]{:S(2)}) %collective-permute-start.1) | collective-permute-done | bytes 155680 | tf_op jit(solution)/shard_map/ppermute | solution.py:295
  11.1 1.6 %collective-permute-done.2 = bf16[1,608,128]{2,1,0:T(8,128)(2,1)S(1)} collective-permute-done((bf16[1,608,128]{2,1,0:T(8,128)(2,1)S(1)}, bf16[1,608,128]{2,1,0:T(8,128)(2,1)S(1)}, u32[]{:S(2)}, u32[]{:S(2)}) %collective-permute-start.2) | collective-permute-done | bytes 155680 | tf_op jit(solution)/shard_map/ppermute | solution.py:298
  12.7 3.1 %collective-permute-start.19 = (bf16[2,608,128]{2,1,0:T(8,128)(2,1)S(1)}, bf16[2,608,128]{2,1,0:T(8,128)(2,1)S(1)}, u32[]{:S(2)}, u32[]{:S(2)}) collective-permute-start(bf16[2,608,128]{2,1,0:T(8,128)(2,1)S(1)} %constant_dynamic-update-slice_fusion.refs_5_), channel_id=1, source_target_pairs={{0,128},{128,0},{1,129},{129,1},{2,130},{130,2},{3,131},{131,3},{4... | collective-permute-start | bytes 933896 | tf_op jit(solution)/shard_map/ppermute | solution.py:28
  15.8 1.9 %collective-permute-start.3 = (bf16[2,608,128]{2,1,0:T(8,128)(2,1)S(1)}, bf16[2,608,128]{2,1,0:T(8,128)(2,1)S(1)}, u32[]{:S(2)}, u32[]{:S(2)}) collective-permute-start(bf16[2,608,128]{2,1,0:T(8,128)(2,1)S(1)} %constant_dynamic-update-slice_fusion.refs_5_), channel_id=1, source_target_pairs={{0,8},{8,0},{1,9},{9,1},{2,10},{10,2},{3,11},{11,3},{4,12},{12,4},... | collective-permute-start | bytes 933896 | tf_op jit(solution)/shard_map/ppermute | solution.py:28
  18.0 1.2 collective-permute-done.5
  19.1 1.5 %collective-permute-start.8 = (bf16[1,608,128]{2,1,0:T(8,128)(2,1)S(1)}, bf16[1,608,128]{2,1,0:T(8,128)(2,1)S(1)}, u32[]{:S(2)}, u32[]{:S(2)}) collective-permute-start(bf16[1,608,128]{2,1,0:T(8,128)(2,1)S(1)} %collective-permute-done.5), channel_id=1, source_target_pairs={{0,16},{16,32},{32,48},{48,64},{64,80},{80,96},{96,112},{112,0},{8... | collective-permute-start | bytes 466952 | tf_op jit(solution)/shard_map/ppermute | solution.py:298
  20.8 3.5 %collective-permute-done.7 = bf16[1,608,128]{2,1,0:T(8,128)(2,1)S(1)} collective-permute-done((bf16[1,608,128]{2,1,0:T(8,128)(2,1)S(1)}, bf16[1,608,128]{2,1,0:T(8,128)(2,1)S(1)}, u32[]{:S(2)}, u32[]{:S(2)}) %collective-permute-start.7) | collective-permute-done | bytes 155680 | tf_op jit(solution)/shard_map/ppermute | solution.py:295
  24.2 1.6 %collective-permute-done.8 = bf16[1,608,128]{2,1,0:T(8,128)(2,1)S(1)} collective-permute-done((bf16[1,608,128]{2,1,0:T(8,128)(2,1)S(1)}, bf16[1,608,128]{2,1,0:T(8,128)(2,1)S(1)}, u32[]{:S(2)}, u32[]{:S(2)}) %collective-permute-start.8) | collective-permute-done | bytes 155680 | tf_op jit(solution)/shard_map/ppermute | solution.py:298
  26.0 4.6 %collective-permute-done.10.refs_11_ = bf16[1,608,128]{2,1,0:T(8,128)(2,1)S(1)} collective-permute-done((bf16[1,608,128]{2,1,0:T(8,128)(2,1)S(1)}, bf16[1,608,128]{2,1,0:T(8,128)(2,1)S(1)}, u32[]{:S(2)}, u32[]{:S(2)}) %collective-permute-start.10) | collective-permute-done | bytes 155680 | tf_op jit(solution)/shard_map/ppermute | solution.py:295
  30.7 0.7 xor_add_fusion.refs_0_
  31.4 2.8 %collective-permute-start.18 = (bf16[2,608,128]{2,1,0:T(8,128)(2,1)S(1)}, bf16[2,608,128]{2,1,0:T(8,128)(2,1)S(1)}, u32[]{:S(2)}, u32[]{:S(2)}) collective-permute-start(bf16[2,608,128]{2,1,0:T(8,128)(2,1)S(1)} %pad_maximum_fusion.refs_4_), channel_id=1, source_target_pairs={{0,128},{128,0},{1,129},{129,1},{2,130},{130,2},{3,131},{131,3},{4... | collective-permute-start | bytes 933896 | tf_op jit(solution)/shard_map/ppermute | solution.py:28
  34.2 0.8 collective-permute-start.12
  35.0 2.7 %collective-permute-start.13 = (bf16[2,608,128]{2,1,0:T(8,128)(2,1)S(1)}, bf16[2,608,128]{2,1,0:T(8,128)(2,1)S(1)}, u32[]{:S(2)}, u32[]{:S(2)}) collective-permute-start(bf16[2,608,128]{2,1,0:T(8,128)(2,1)S(1)} %constant_dynamic-update-slice_fusion.4.refs_9_), channel_id=1, source_target_pairs={{0,128},{128,0},{1,129},{129,1},{2,130},{130,2},{3,131},{131,3},{4... | collective-permute-start | bytes 933896 | tf_op jit(solution)/shard_map/ppermute | solution.py:28
  37.7 0.8 collective-permute-start.14
  38.8 15.7 %shard_map.67 = (f32[8,128,128]{2,1,0:T(8,128)S(1)}, s16[1040,128]{1,0:T(8,128)(2,1)S(1)}, s16[1040,128]{1,0:T(8,128)(2,1)S(1)}, s16[1040,128]{1,0:T(8,128)(2,1)...) custom-call(s32[16]{0:T(128)S(1)} %xor_add_fusion.refs_0_, s32[8,32]{1,0:T(8,128)} %refs_1_.1, ...), custom_call_target="tpu_custom_call" | custom-call | flops 10000000000 | bytes 16777216 | tf_op jit(solution)/shard_map/pallas_call | solution.py:170
  54.5 4.9 %collective-permute-done.14.refs_10_ = bf16[1,608,128]{2,1,0:T(8,128)(2,1)S(1)} collective-permute-done((bf16[1,608,128]{2,1,0:T(8,128)(2,1)S(1)}, bf16[1,608,128]{2,1,0:T(8,128)(2,1)S(1)}, u32[]{:S(2)}, u32[]{:S(2)}) %collective-permute-start.14) | collective-permute-done | bytes 155680 | tf_op jit(solution)/shard_map/ppermute | solution.py:28
  60.3 2.6 %collective-permute-start.16 = (s16[1040,128]{1,0:T(8,128)(2,1)S(1)}, s16[1040,128]{1,0:T(8,128)(2,1)S(1)}, u32[]{:S(2)}, u32[]{:S(2)}) collective-permute-start(s16[1040,128]{1,0:T(8,128)(2,1)S(1)} %get-tuple-element.46), channel_id=1, source_target_pairs={{0,2},{1,3},{2,0},{3,1},{4,6},{5,7},{6,4},{7,5},{8,10},{9,11},{10,... | collective-permute-start | bytes 798728 | tf_op jit(solution)/shard_map/ppermute | solution.py:304
  62.9 13.3 %collective-permute-start.17 = (s16[1040,128]{1,0:T(8,128)(2,1)S(1)}, s16[1040,128]{1,0:T(8,128)(2,1)S(1)}, u32[]{:S(2)}, u32[]{:S(2)}) collective-permute-start(s16[1040,128]{1,0:T(8,128)(2,1)S(1)} %get-tuple-element.47), channel_id=1, source_target_pairs={{0,3},{1,0},{2,1},{3,2},{4,7},{5,4},{6,5},{7,6},{8,11},{9,8},{10,9... | collective-permute-start | bytes 798728 | tf_op jit(solution)/shard_map/ppermute | solution.py:304
  76.3 14.7 %shard_map.69 = (f32[8,128,128]{2,1,0:T(8,128)S(1)}, s16[1040,128]{1,0:T(8,128)(2,1)}, s16[1040,128]{1,0:T(8,128)(2,1)}, s16[1040,128]{1,0:T(8,128)(2,1)S(1)}, s32[16,128]{1,0:T(8,128)S(1)}) custom-call(s32[16]{0:T(128)S(1)} %xor_add_fusion.refs_0_, s32[16,128]{1,0:T(8,128)S(1)} %get-tuple-element.43.over_ref.refs_1_, ...), custom_call_target="tpu_custom_call" | custom-call | flops 10000000000 | bytes 16777216 | tf_op jit(solution)/shard_map/pallas_call | solution.py:170
  90.9 3.3 %collective-permute-start.24 = (s16[1040,128]{1,0:T(8,128)(2,1)}, s16[1040,128]{1,0:T(8,128)(2,1)S(1)}, u32[]{:S(2)}, u32[]{:S(2)}) collective-permute-start(s16[1040,128]{1,0:T(8,128)(2,1)} %get-tuple-element.55), channel_id=1, source_target_pairs={{0,1},{1,2},{2,3},{3,0},{4,5},{5,6},{6,7},{7,4},{8,9},{9,10},{10,1... | collective-permute-start | bytes 798728 | tf_op jit(solution)/shard_map/ppermute | solution.py:304
  94.4 1.3 %collective-permute-start.26 = (s16[1040,128]{1,0:T(8,128)(2,1)S(1)}, s16[1040,128]{1,0:T(8,128)(2,1)S(1)}, u32[]{:S(2)}, u32[]{:S(2)}) collective-permute-start(s16[1040,128]{1,0:T(8,128)(2,1)S(1)} %get-tuple-element.57), channel_id=1, source_target_pairs={{0,3},{1,0},{2,1},{3,2},{4,7},{5,4},{6,5},{7,6},{8,11},{9,8},{10,9... | collective-permute-start | bytes 798728 | tf_op jit(solution)/shard_map/ppermute | solution.py:304
  95.8 1.4 %shard_map.68 = (f32[8,128,128]{2,1,0:T(8,128)S(1)}, s16[1040,128]{1,0:T(8,128)(2,1)S(1)}) custom-call(s32[16,128]{1,0:T(8,128)S(1)} %get-tuple-element.43.over_ref.refs_1_, f32[8,128,128]{2,1,0:T(8,128)S(1)} %get-tuple-element.44.own_ref, s16[1040,128]{1,0:T(8,128)(2,1)S(1)} %collective-permute-done.15.a_ref, ...), custom_call_target="tpu_custom_call" | custom-call | tf_op jit(solution)/shard_map/pallas_call | solution.py:212
  97.2 8.4 %collective-permute-done.24.a_ref = s16[1040,128]{1,0:T(8,128)(2,1)S(1)} collective-permute-done((s16[1040,128]{1,0:T(8,128)(2,1)}, s16[1040,128]{1,0:T(8,128)(2,1)S(1)}, u32[]{:S(2)}, u32[]{:S(2)}) %collective-permute-start.24) | collective-permute-done | bytes 266272 | tf_op jit(solution)/shard_map/ppermute | solution.py:304
  105.6 3.3 %collective-permute-done.26.c_ref = s16[1040,128]{1,0:T(8,128)(2,1)S(1)} collective-permute-done((s16[1040,128]{1,0:T(8,128)(2,1)S(1)}, s16[1040,128]{1,0:T(8,128)(2,1)S(1)}, u32[]{:S(2)}, u32[]{:S(2)}) %collective-permute-start.26) | collective-permute-done | bytes 266272 | tf_op jit(solution)/shard_map/ppermute | solution.py:304
  109.0 1.4 %shard_map.70 = (f32[8,128,128]{2,1,0:T(8,128)S(1)}, s16[1040,128]{1,0:T(8,128)(2,1)S(1)}) custom-call(s32[16,128]{1,0:T(8,128)S(1)} %get-tuple-element.53.over_ref, f32[8,128,128]{2,1,0:T(8,128)S(1)} %get-tuple-element.54.own_ref, s16[1040,128]{1,0:T(8,128)(2,1)S(1)} %collective-permute-done.24.a_ref, s16[1040,128]{1,0:T(8,128)(2,1)S(1)} %collective-permute-done.25.b_ref, ...), custom_call_target="tpu_custom_call" | custom-call | tf_op jit(solution)/shard_map/pallas_call | solution.py:212
  110.5 1.3 %collective-permute-start.27 = (s16[1040,128]{1,0:T(8,128)(2,1)S(1)}, s16[1040,128]{1,0:T(8,128)(2,1)S(1)}, u32[]{:S(2)}, u32[]{:S(2)}) collective-permute-start(s16[1040,128]{1,0:T(8,128)(2,1)S(1)} %shard_map.71.sent_ref), channel_id=1, source_target_pairs={{0,4},{4,0},{1,5},{5,1},{2,6},{6,2},{3,7},{7,3},{8,12},{12,8},{9,1... | collective-permute-start | bytes 798728 | tf_op jit(solution)/shard_map/ppermute | solution.py:28
  111.7 6.8 %collective-permute-done.27.got_ref = s16[1040,128]{1,0:T(8,128)(2,1)S(1)} collective-permute-done((s16[1040,128]{1,0:T(8,128)(2,1)S(1)}, s16[1040,128]{1,0:T(8,128)(2,1)S(1)}, u32[]{:S(2)}, u32[]{:S(2)}) %collective-permute-start.27) | collective-permute-done | bytes 266272 | tf_op jit(solution)/shard_map/ppermute | solution.py:28
  118.9 0.6 slice_reduce_fusion
  120.2 0.7 copy-done.2
  (48 shorter events, 2.4 us)
Async XLA Ops:
  1.8 2.1 %collective-permute-start = (bf16[1,608,128]{2,1,0:T(8,128)(2,1)S(1)}, bf16[1,608,128]{2,1,0:T(8,128)(2,1)S(1)}, u32[]{:S(2)}, u32[]{:S(2)}) collective-permute-start(bf16[1,608,128]{2,1,0:T(8,128)(2,1)S(1)} %shard_map.66), channel_id=1, source_target_pairs={{0,8},{8,0},{1,9},{9,1},{2,10},{10,2},{3,11},{11,3},{4,12},{12,4},... | collective-permute-start | bytes 466952 | tf_op jit(solution)/shard_map/ppermute | solution.py:28
  1.9 9.1 %collective-permute-start.1 = (bf16[1,608,128]{2,1,0:T(8,128)(2,1)S(1)}, bf16[1,608,128]{2,1,0:T(8,128)(2,1)S(1)}, u32[]{:S(2)}, u32[]{:S(2)}) collective-permute-start(bf16[1,608,128]{2,1,0:T(8,128)(2,1)S(1)} %shard_map.66), channel_id=1, source_target_pairs={{0,16},{16,32},{32,48},{48,64},{64,80},{80,96},{96,112},{112,0},{8... | collective-permute-start | bytes 466952 | tf_op jit(solution)/shard_map/ppermute | solution.py:295
  3.9 8.8 %collective-permute-start.2 = (bf16[1,608,128]{2,1,0:T(8,128)(2,1)S(1)}, bf16[1,608,128]{2,1,0:T(8,128)(2,1)S(1)}, u32[]{:S(2)}, u32[]{:S(2)}) collective-permute-start(bf16[1,608,128]{2,1,0:T(8,128)(2,1)S(1)} %collective-permute-done), channel_id=1, source_target_pairs={{0,16},{16,32},{32,48},{48,64},{64,80},{80,96},{96,112},{112,0},{8... | collective-permute-start | bytes 466952 | tf_op jit(solution)/shard_map/ppermute | solution.py:298
  11.0 6.7 %collective-permute-start.4 = (bf16[1,608,128]{2,1,0:T(8,128)(2,1)S(1)}, bf16[1,608,128]{2,1,0:T(8,128)(2,1)S(1)}, u32[]{:S(2)}, u32[]{:S(2)}) collective-permute-start(bf16[1,608,128]{2,1,0:T(8,128)(2,1)S(1)} %collective-permute-done.1), channel_id=1, source_target_pairs={{0,16},{16,32},{32,48},{48,64},{64,80},{80,96},{96,112},{112,0},{8... | collective-permute-start | bytes 466952 | tf_op jit(solution)/shard_map/ppermute | solution.py:295
  12.7 6.4 %collective-permute-start.5 = (bf16[1,608,128]{2,1,0:T(8,128)(2,1)S(1)}, bf16[1,608,128]{2,1,0:T(8,128)(2,1)S(1)}, u32[]{:S(2)}, u32[]{:S(2)}) collective-permute-start(bf16[1,608,128]{2,1,0:T(8,128)(2,1)S(1)} %collective-permute-done.2), channel_id=1, source_target_pairs={{0,16},{16,32},{32,48},{48,64},{64,80},{80,96},{96,112},{112,0},{8... | collective-permute-start | bytes 466952 | tf_op jit(solution)/shard_map/ppermute | solution.py:298
  12.7 18.7 %collective-permute-start.19 = (bf16[2,608,128]{2,1,0:T(8,128)(2,1)S(1)}, bf16[2,608,128]{2,1,0:T(8,128)(2,1)S(1)}, u32[]{:S(2)}, u32[]{:S(2)}) collective-permute-start(bf16[2,608,128]{2,1,0:T(8,128)(2,1)S(1)} %constant_dynamic-update-slice_fusion.refs_5_), channel_id=1, source_target_pairs={{0,128},{128,0},{1,129},{129,1},{2,130},{130,2},{3,131},{131,3},{4... | collective-permute-start | bytes 933896 | tf_op jit(solution)/shard_map/ppermute | solution.py:28
  15.8 18.4 %collective-permute-start.3 = (bf16[2,608,128]{2,1,0:T(8,128)(2,1)S(1)}, bf16[2,608,128]{2,1,0:T(8,128)(2,1)S(1)}, u32[]{:S(2)}, u32[]{:S(2)}) collective-permute-start(bf16[2,608,128]{2,1,0:T(8,128)(2,1)S(1)} %constant_dynamic-update-slice_fusion.refs_5_), channel_id=1, source_target_pairs={{0,8},{8,0},{1,9},{9,1},{2,10},{10,2},{3,11},{11,3},{4,12},{12,4},... | collective-permute-start | bytes 933896 | tf_op jit(solution)/shard_map/ppermute | solution.py:28
  17.8 6.4 %collective-permute-start.7 = (bf16[1,608,128]{2,1,0:T(8,128)(2,1)S(1)}, bf16[1,608,128]{2,1,0:T(8,128)(2,1)S(1)}, u32[]{:S(2)}, u32[]{:S(2)}) collective-permute-start(bf16[1,608,128]{2,1,0:T(8,128)(2,1)S(1)} %collective-permute-done.4), channel_id=1, source_target_pairs={{0,16},{16,32},{32,48},{48,64},{64,80},{80,96},{96,112},{112,0},{8... | collective-permute-start | bytes 466952 | tf_op jit(solution)/shard_map/ppermute | solution.py:295
  19.1 6.7 %collective-permute-start.8 = (bf16[1,608,128]{2,1,0:T(8,128)(2,1)S(1)}, bf16[1,608,128]{2,1,0:T(8,128)(2,1)S(1)}, u32[]{:S(2)}, u32[]{:S(2)}) collective-permute-start(bf16[1,608,128]{2,1,0:T(8,128)(2,1)S(1)} %collective-permute-done.5), channel_id=1, source_target_pairs={{0,16},{16,32},{32,48},{48,64},{64,80},{80,96},{96,112},{112,0},{8... | collective-permute-start | bytes 466952 | tf_op jit(solution)/shard_map/ppermute | solution.py:298
  20.7 17.1 %collective-permute-start.6 = (bf16[2,608,128]{2,1,0:T(8,128)(2,1)S(1)}, bf16[2,608,128]{2,1,0:T(8,128)(2,1)S(1)}, u32[]{:S(2)}, u32[]{:S(2)}) collective-permute-start(bf16[2,608,128]{2,1,0:T(8,128)(2,1)S(1)} %constant_dynamic-update-slice_fusion.2.refs_7_), channel_id=1, source_target_pairs={{0,8},{8,0},{1,9},{9,1},{2,10},{10,2},{3,11},{11,3},{4,12},{12,4},... | collective-permute-start | bytes 933896 | tf_op jit(solution)/shard_map/ppermute | solution.py:28
  24.2 6.4 %collective-permute-start.10 = (bf16[1,608,128]{2,1,0:T(8,128)(2,1)S(1)}, bf16[1,608,128]{2,1,0:T(8,128)(2,1)S(1)}, u32[]{:S(2)}, u32[]{:S(2)}) collective-permute-start(bf16[1,608,128]{2,1,0:T(8,128)(2,1)S(1)} %collective-permute-done.7), channel_id=1, source_target_pairs={{0,16},{16,32},{32,48},{48,64},{64,80},{80,96},{96,112},{112,0},{8... | collective-permute-start | bytes 466952 | tf_op jit(solution)/shard_map/ppermute | solution.py:295
  25.9 12.6 %collective-permute-start.9 = (bf16[2,608,128]{2,1,0:T(8,128)(2,1)S(1)}, bf16[2,608,128]{2,1,0:T(8,128)(2,1)S(1)}, u32[]{:S(2)}, u32[]{:S(2)}) collective-permute-start(bf16[2,608,128]{2,1,0:T(8,128)(2,1)S(1)} %constant_dynamic-update-slice_fusion.4.refs_9_), channel_id=1, source_target_pairs={{0,8},{8,0},{1,9},{9,1},{2,10},{10,2},{3,11},{11,3},{4,12},{12,4},... | collective-permute-start | bytes 933896 | tf_op jit(solution)/shard_map/ppermute | solution.py:28
  30.7 4.4 %collective-permute-start.11 = (bf16[1,608,128]{2,1,0:T(8,128)(2,1)S(1)}, bf16[1,608,128]{2,1,0:T(8,128)(2,1)S(1)}, u32[]{:S(2)}, u32[]{:S(2)}) collective-permute-start(bf16[1,608,128]{2,1,0:T(8,128)(2,1)S(1)} %collective-permute-done.10.refs_11_), channel_id=1, source_target_pairs={{0,8},{8,0},{1,9},{9,1},{2,10},{10,2},{3,11},{11,3},{4,12},{12,4},... | collective-permute-start | bytes 466952 | tf_op jit(solution)/shard_map/ppermute | solution.py:28
  31.4 28.7 %collective-permute-start.18 = (bf16[2,608,128]{2,1,0:T(8,128)(2,1)S(1)}, bf16[2,608,128]{2,1,0:T(8,128)(2,1)S(1)}, u32[]{:S(2)}, u32[]{:S(2)}) collective-permute-start(bf16[2,608,128]{2,1,0:T(8,128)(2,1)S(1)} %pad_maximum_fusion.refs_4_), channel_id=1, source_target_pairs={{0,128},{128,0},{1,129},{129,1},{2,130},{130,2},{3,131},{131,3},{4... | collective-permute-start | bytes 933896 | tf_op jit(solution)/shard_map/ppermute | solution.py:28
  34.2 25.2 %collective-permute-start.12 = (bf16[2,608,128]{2,1,0:T(8,128)(2,1)S(1)}, bf16[2,608,128]{2,1,0:T(8,128)(2,1)S(1)}, u32[]{:S(2)}, u32[]{:S(2)}) collective-permute-start(bf16[2,608,128]{2,1,0:T(8,128)(2,1)S(1)} %constant_dynamic-update-slice_fusion.2.refs_7_), channel_id=1, source_target_pairs={{0,128},{128,0},{1,129},{129,1},{2,130},{130,2},{3,131},{131,3},{4... | collective-permute-start | bytes 933896 | tf_op jit(solution)/shard_map/ppermute | solution.py:28
  35.0 24.4 %collective-permute-start.13 = (bf16[2,608,128]{2,1,0:T(8,128)(2,1)S(1)}, bf16[2,608,128]{2,1,0:T(8,128)(2,1)S(1)}, u32[]{:S(2)}, u32[]{:S(2)}) collective-permute-start(bf16[2,608,128]{2,1,0:T(8,128)(2,1)S(1)} %constant_dynamic-update-slice_fusion.4.refs_9_), channel_id=1, source_target_pairs={{0,128},{128,0},{1,129},{129,1},{2,130},{130,2},{3,131},{131,3},{4... | collective-permute-start | bytes 933896 | tf_op jit(solution)/shard_map/ppermute | solution.py:28
  37.7 21.7 %collective-permute-start.14 = (bf16[1,608,128]{2,1,0:T(8,128)(2,1)S(1)}, bf16[1,608,128]{2,1,0:T(8,128)(2,1)S(1)}, u32[]{:S(2)}, u32[]{:S(2)}) collective-permute-start(bf16[1,608,128]{2,1,0:T(8,128)(2,1)S(1)} %collective-permute-done.10.refs_11_), channel_id=1, source_target_pairs={{0,128},{128,0},{1,129},{129,1},{2,130},{130,2},{3,131},{131,3},{4... | collective-permute-start | bytes 466952 | tf_op jit(solution)/shard_map/ppermute | solution.py:28
  38.6 21.7 %collective-permute-start.20 = (bf16[2,608,128]{2,1,0:T(8,128)(2,1)S(1)}, bf16[2,608,128]{2,1,0:T(8,128)(2,1)S(1)}, u32[]{:S(2)}, u32[]{:S(2)}) collective-permute-start(bf16[2,608,128]{2,1,0:T(8,128)(2,1)S(1)} %collective-permute-done.19.refs_4_), channel_id=1, source_target_pairs={{0,8},{8,0},{1,9},{9,1},{2,10},{10,2},{3,11},{11,3},{4,12},{12,4},... | collective-permute-start | bytes 933896 | tf_op jit(solution)/shard_map/ppermute | solution.py:28
  59.4 16.8 %collective-permute-start.21 = (bf16[2,608,128]{2,1,0:T(8,128)(2,1)S(1)}, bf16[2,608,128]{2,1,0:T(8,128)(2,1)S(1)}, u32[]{:S(2)}, u32[]{:S(2)}) collective-permute-start(bf16[2,608,128]{2,1,0:T(8,128)(2,1)S(1)} %collective-permute-done.12.refs_6_), channel_id=1, source_target_pairs={{0,8},{8,0},{1,9},{9,1},{2,10},{10,2},{3,11},{11,3},{4,12},{12,4},... | collective-permute-start | bytes 933896 | tf_op jit(solution)/shard_map/ppermute | solution.py:28
  59.5 16.8 %collective-permute-start.22 = (bf16[2,608,128]{2,1,0:T(8,128)(2,1)S(1)}, bf16[2,608,128]{2,1,0:T(8,128)(2,1)S(1)}, u32[]{:S(2)}, u32[]{:S(2)}) collective-permute-start(bf16[2,608,128]{2,1,0:T(8,128)(2,1)S(1)} %collective-permute-done.13.refs_8_), channel_id=1, source_target_pairs={{0,8},{8,0},{1,9},{9,1},{2,10},{10,2},{3,11},{11,3},{4,12},{12,4},... | collective-permute-start | bytes 933896 | tf_op jit(solution)/shard_map/ppermute | solution.py:28
  60.0 2.9 %collective-permute-start.23 = (bf16[1,608,128]{2,1,0:T(8,128)(2,1)S(1)}, bf16[1,608,128]{2,1,0:T(8,128)(2,1)S(1)}, u32[]{:S(2)}, u32[]{:S(2)}) collective-permute-start(bf16[1,608,128]{2,1,0:T(8,128)(2,1)S(1)} %collective-permute-done.14.refs_10_), channel_id=1, source_target_pairs={{0,8},{8,0},{1,9},{9,1},{2,10},{10,2},{3,11},{11,3},{4,12},{12,4},... | collective-permute-start | bytes 466952 | tf_op jit(solution)/shard_map/ppermute | solution.py:28
  60.1 34.4 %collective-permute-start.15 = (s16[1040,128]{1,0:T(8,128)(2,1)S(1)}, s16[1040,128]{1,0:T(8,128)(2,1)S(1)}, u32[]{:S(2)}, u32[]{:S(2)}) collective-permute-start(s16[1040,128]{1,0:T(8,128)(2,1)S(1)} %get-tuple-element.45), channel_id=1, source_target_pairs={{0,1},{1,2},{2,3},{3,0},{4,5},{5,6},{6,7},{7,4},{8,9},{9,10},{10,1... | collective-permute-start | bytes 798728 | tf_op jit(solution)/shard_map/ppermute | solution.py:304
  60.3 35.5 %collective-permute-start.16 = (s16[1040,128]{1,0:T(8,128)(2,1)S(1)}, s16[1040,128]{1,0:T(8,128)(2,1)S(1)}, u32[]{:S(2)}, u32[]{:S(2)}) collective-permute-start(s16[1040,128]{1,0:T(8,128)(2,1)S(1)} %get-tuple-element.46), channel_id=1, source_target_pairs={{0,2},{1,3},{2,0},{3,1},{4,6},{5,7},{6,4},{7,5},{8,10},{9,11},{10,... | collective-permute-start | bytes 798728 | tf_op jit(solution)/shard_map/ppermute | solution.py:304
  62.9 32.9 %collective-permute-start.17 = (s16[1040,128]{1,0:T(8,128)(2,1)S(1)}, s16[1040,128]{1,0:T(8,128)(2,1)S(1)}, u32[]{:S(2)}, u32[]{:S(2)}) collective-permute-start(s16[1040,128]{1,0:T(8,128)(2,1)S(1)} %get-tuple-element.47), channel_id=1, source_target_pairs={{0,3},{1,0},{2,1},{3,2},{4,7},{5,4},{6,5},{7,6},{8,11},{9,8},{10,9... | collective-permute-start | bytes 798728 | tf_op jit(solution)/shard_map/ppermute | solution.py:304
  76.2 43.9 %copy-start = (s32[32,32]{1,0:T(8,128)S(1)}, s32[32,32]{1,0:T(8,128)}, u32[]{:S(2)}) copy-start(s32[32,32]{1,0:T(8,128)} %mask_ref.1) | copy-start | bytes 12292
  76.3 43.9 %copy-start.1 = (s32[8,32]{1,0:T(8,128)S(1)}, s32[8,32]{1,0:T(8,128)}, u32[]{:S(2)}) copy-start(s32[8,32]{1,0:T(8,128)} %refs_1_.1) | copy-start | bytes 3076
  90.9 14.7 %collective-permute-start.24 = (s16[1040,128]{1,0:T(8,128)(2,1)}, s16[1040,128]{1,0:T(8,128)(2,1)S(1)}, u32[]{:S(2)}, u32[]{:S(2)}) collective-permute-start(s16[1040,128]{1,0:T(8,128)(2,1)} %get-tuple-element.55), channel_id=1, source_target_pairs={{0,1},{1,2},{2,3},{3,0},{4,5},{5,6},{6,7},{7,4},{8,9},{9,10},{10,1... | collective-permute-start | bytes 798728 | tf_op jit(solution)/shard_map/ppermute | solution.py:304
  94.2 11.4 %collective-permute-start.25 = (s16[1040,128]{1,0:T(8,128)(2,1)}, s16[1040,128]{1,0:T(8,128)(2,1)S(1)}, u32[]{:S(2)}, u32[]{:S(2)}) collective-permute-start(s16[1040,128]{1,0:T(8,128)(2,1)} %get-tuple-element.56), channel_id=1, source_target_pairs={{0,2},{1,3},{2,0},{3,1},{4,6},{5,7},{6,4},{7,5},{8,10},{9,11},{10,... | collective-permute-start | bytes 798728 | tf_op jit(solution)/shard_map/ppermute | solution.py:304
  94.4 14.5 %collective-permute-start.26 = (s16[1040,128]{1,0:T(8,128)(2,1)S(1)}, s16[1040,128]{1,0:T(8,128)(2,1)S(1)}, u32[]{:S(2)}, u32[]{:S(2)}) collective-permute-start(s16[1040,128]{1,0:T(8,128)(2,1)S(1)} %get-tuple-element.57), channel_id=1, source_target_pairs={{0,3},{1,0},{2,1},{3,2},{4,7},{5,4},{6,5},{7,6},{8,11},{9,8},{10,9... | collective-permute-start | bytes 798728 | tf_op jit(solution)/shard_map/ppermute | solution.py:304
  110.5 8.1 %collective-permute-start.27 = (s16[1040,128]{1,0:T(8,128)(2,1)S(1)}, s16[1040,128]{1,0:T(8,128)(2,1)S(1)}, u32[]{:S(2)}, u32[]{:S(2)}) collective-permute-start(s16[1040,128]{1,0:T(8,128)(2,1)S(1)} %shard_map.71.sent_ref), channel_id=1, source_target_pairs={{0,4},{4,0},{1,5},{5,1},{2,6},{6,2},{3,7},{7,3},{8,12},{12,8},{9,1... | collective-permute-start | bytes 798728 | tf_op jit(solution)/shard_map/ppermute | solution.py:28
  120.2 0.7 copy-start.2

commit v5 on v4

--- a/solution.py
+++ b/solution.py
@@ -111,10 +111,15 @@
     if mask:
         kept_ref, *refs = refs
     got, amps, held, sem = refs
-    blocks = [pl.ds(j * 2 * TILE, 2 * TILE) for j in range(RT // 2)]
-    loads = [pltpu.make_async_copy(ints_ref.at[rows, :], held.at[j], sem.at[0, j]) for j, rows in enumerate(blocks)]
-    for load in loads:
-        load.start()
+
+    def load(j):
+        return pltpu.make_async_copy(ints_ref.at[pl.ds(j * 2 * TILE, 2 * TILE), :], held.at[j], sem.at[0, j])
+
+    def store(j):
+        return pltpu.make_async_copy(held.at[j], kept_ref.at[pl.ds(j * 2 * TILE, 2 * TILE), :], sem.at[1, j])
+
+    for j in range(RT // 2):
+        load(j).start()
     i = 0
     for size, ref in zip(sizes, ins, strict=True):
         got[i : i + size] = ref[...]
@@ -136,30 +141,34 @@
     over = jnp.maximum(jnp.broadcast_to(over, (META, TILE)).astype(I32), before_ref[...])
     over_ref[...] = over
     lane = lax.broadcasted_iota(I32, (TILE, TILE), 1)
-    powers = [jnp.zeros((TILE, TILE), F32)] * 3
-    stores = []
-    for j, load in enumerate(loads):
-        load.wait()
+
+    def multiply(j, powers):
+        load(j).wait()
         if mask:
             for n in range(2):
                 for t in range(TILES):
                     kept = jnp.where(mask_ref[2 * j + n, t] > 0, 1.0, 0.0).astype(BF16)
                     part = (j, slice(n * TILE, (n + 1) * TILE), slice(t * TILE, (t + 1) * TILE))
                     held[part] = held[part] * kept
-            stores.append(pltpu.make_async_copy(held.at[j], kept_ref.at[blocks[j], :], sem.at[1, j]))
-            stores[j].start()
+            store(j).start()
         value = lax.dot_general(amps[...], held[j], (((1,), (1,)), ((), ())), preferred_element_type=F32)
         for n in range(2):
             t = 2 * j + n
             own_ref[t] = value[:TILE, n * TILE : (n + 1) * TILE]
+            new = []
             for d, out in enumerate((a_ref, b_ref, c_ref)):
                 coded, power = code(value[(d + 1) * TILE : (d + 2) * TILE, n * TILE : (n + 1) * TILE])
-                out[t * TILE : (t + 1) * TILE, :] = coded
-                powers[d] = jnp.where(lane == t, power, powers[d])
+                out[pl.ds(pl.multiple_of(t * TILE, TILE), TILE), :] = coded
+                new.append(jnp.where(lane == t, power, powers[d]))
+            powers = tuple(new)
+        return powers
+
+    powers = lax.fori_loop(0, RT // 2, multiply, (jnp.zeros((TILE, TILE), F32),) * 3)
     for d, out in enumerate((a_ref, b_ref, c_ref)):
         out[RT * TILE :, :] = powers_and_flags(powers[d], over)
-    for store in stores:
-        store.wait()
+    if mask:
+        for j in range(RT // 2):
+            store(j).wait()
 
 
 def chunk_sums(rows, before, ints, messages, mask=None):
@@ -246,15 +255,15 @@
     for t in range(RT):
         mine = jnp.where(near, first_ref[t], second_ref[t])
         out_ref[:, t * TILE : (t + 1) * TILE] = (mine + decode(got_ref, scale, t)).astype(BF16)
-    over_ref[...] = jnp.maximum(flags(sent_ref), flags(got_ref))
+    over_ref[0] = jnp.max(jnp.maximum(flags(sent_ref), flags(got_ref))[RT:, :])
 
 
 def last(near, first, second, sent, got):
     return pl.pallas_call(
         last_kernel,
         in_specs=[SMEM] + [VMEM] * 4,
-        out_specs=[VMEM] * 2,
-        out_shape=[jax.ShapeDtypeStruct((TILE, RT * TILE), BF16), jax.ShapeDtypeStruct((META, TILE), I32)],
+        out_specs=[VMEM, SMEM],
+        out_shape=[jax.ShapeDtypeStruct((TILE, RT * TILE), BF16), jax.ShapeDtypeStruct((1,), I32)],
         compiler_params=pltpu.CompilerParams(vmem_limit_bytes=8 << 20),
     )(near, first, second, sent, got)
 
@@ -275,8 +284,8 @@
 
 RING = [(2 * z, 2 * ((z + 1) % 8)) for z in range(8)] + [(2 * z + 1, 2 * ((z + 7) % 8) + 1) for z in range(8)]
 
-SHIFT = (0, 0, -1, -1, 1, 1, -2, -2, 2, 2, -3, -3, 3, 3, 4, 4)
-OTHER = (0, 1, 0, 1, 1, 0, 0, 1, 1, 0, 0, 1, 1, 0, 0, 1)
+SHIFT = (0, 0, -1, -1, -2, -2, 1, 1, 2, 2, -3, -3, 4, 3, 3, 4)
+OTHER = (0, 1, 0, 1, 0, 1, 1, 0, 1, 0, 0, 1, 0, 1, 0, 1)
 
 
 def local(amplitudes, integrals, amp_mask, int_mask):
@@ -287,28 +296,24 @@
     far = (z + up * jnp.asarray(SHIFT, I32)) & 7
     rows = (((far >> 1) - y) & 3) * 4 + (far & 1) * 2 + (core ^ jnp.asarray(OTHER, I32))
 
-    first = pack(amplitudes, amp_mask)
-    second = swap(first, "core")
-    block = jnp.concatenate([first, second], axis=0)
-    held, far_blocks = [block], [swap(block, "xh")]
+    own = pack(amplitudes, amp_mask)
+    across = swap(own, "xh")
+    blocks = [[jnp.concatenate([message, swap(message, "core")], axis=0)] for message in (own, across)]
     for hop in range(1, 5):
-        first = lax.ppermute(first, ("z", "core"), RING)
-        block = first
-        if hop < 4:
-            second = lax.ppermute(second, ("z", "core"), RING)
-            block = jnp.concatenate([first, second], axis=0)
-        held += [block, swap(block, "core")]
-        far_blocks.append(swap(block, "xh"))
+        for chain in blocks:
+            chain.append(lax.ppermute(chain[-1] if hop < 4 else chain[-1][:1], ("z", "core"), RING))
+    two = [jnp.concatenate(chain[1:3], axis=0) for chain in blocks]
+    rest = jnp.concatenate(blocks[0][3:], axis=0)
 
     def spread(parts):
         return [lax.ppermute(part, "y", [(i, (i + d + 1) % 4) for i in range(4)]) for d, part in enumerate(parts)]
 
     over = jnp.zeros((META, TILE), I32)
+    held = [blocks[0][0], two[0], swap(two[0], "core"), rest, swap(rest, "core")]
     own_part, *parts, over, kept_ints = chunk_sums(rows, over, integrals, held, int_mask)
-    over, *far_blocks[2:] = lax.optimization_barrier((over, *far_blocks[2:]))
-    held = far_blocks[:1]
-    for block in far_blocks[1:]:
-        held += [block, swap(block, "core")]
+    over, late = lax.optimization_barrier((over, blocks[1][4]))
+    rest = jnp.concatenate([blocks[1][3], late], axis=0)
+    held = [blocks[1][0], two[1], swap(two[1], "core"), rest, swap(rest, "core")]
     sums, coded = zip(add(over, own_part, spread(parts)))
     own_part, *parts, over = chunk_sums(rows, over, kept_ints, held)
     total, sent = add(over, own_part, spread(parts))
@@ -317,7 +322,7 @@
     sent = choose(near, *coded)
     out, over = last(near, *sums, sent, swap(sent, "xl"))
     return lax.cond(
-        jnp.max(over[META - 1]) > 0,
+        over[0] > 0,
         lambda out: plain(amplitudes, integrals, amp_mask, int_mask),
         lambda out: out,
         out,

time: 123 us -> 98.3 us (0.80); the launches traced: 121 us -> 98.1 us
  starting transfers between devices: 41.2 us -> 19.5 us
  Pallas kernels: 35.4 us -> 27.9 us
  waiting for transfers between devices: 41.3 us -> 48.2 us
    ppermute x6, starting transfers between devices: 21 us -> 7.72 us  [spread(): lax.ppermute(part, 'y', [(i, (i + d + 1) % 4) for i in range(4)])]
    pallas_call x2, Pallas kernels: 30.3 us -> 22.2 us  [chunk_sums(): pl.pallas_call(lambda *refs: chunk_kernel(sizes, mask is not None, *refs)...]
    ppermute x7 -> x8, waiting for transfers between devices: 17.8 us -> 23.8 us  [local(): lax.ppermute(chain[-1] if hop < 4 else chain[-1][:1], ('z', 'core'), RING)]
    ppermute x15 -> x8, starting transfers between devices: 14.6 us -> 9.18 us  [swap(): return lax.ppermute(x, axis, [(0, 1), (1, 0)])]
    ppermute x7 -> x8, starting transfers between devices: 5.6 us -> 2.63 us  [local(): lax.ppermute(chain[-1] if hop < 4 else chain[-1][:1], ('z', 'core'), RING)]
    ppermute x15 -> x8, waiting for transfers between devices: 11.7 us -> 12.6 us  [swap(): return lax.ppermute(x, axis, [(0, 1), (1, 0)])]
  transfers between devices with their start and end apart: 28 -> 22, of which waited for: 10 -> 12; matrix products, arithmetic and copies ran while one was open for 1% -> 1% of each run, Pallas kernels for 26% -> 24%
where the time goes in v5:
time: 98.3 us; the launch traced here: 98.1 us
  waiting for transfers between devices  48.2 us (49%)
  Pallas kernels  27.9 us (28%)
  starting transfers between devices  19.5 us (20%)
    ppermute x8, waiting for transfers between devices, local(): lax.ppermute(chain[-1] if hop < 4 else chain[-1][:1], ('z', 'core'), RING)  23.8 us
    pallas_call x2, Pallas kernels, chunk_sums(): pl.pallas_call(lambda *refs: chunk_kernel(sizes, mask is not None, *refs)...  22.2 us
    ppermute x8, waiting for transfers between devices, swap(): return lax.ppermute(x, axis, [(0, 1), (1, 0)])  12.6 us
    ppermute x6, waiting for transfers between devices, spread(): lax.ppermute(part, 'y', [(i, (i + d + 1) % 4) for i in range(4)])  11.8 us
    ppermute x8, starting transfers between devices, swap(): return lax.ppermute(x, axis, [(0, 1), (1, 0)])  9.18 us
    ppermute x6, starting transfers between devices, spread(): lax.ppermute(part, 'y', [(i, (i + d + 1) % 4) for i in range(4)])  7.72 us
    pallas_call x2, Pallas kernels, add(): pl.pallas_call(add_kernel, in_specs=[VMEM] * 5, out_specs=[VMEM] * 2, out...  2.85 us
    ppermute x8, starting transfers between devices, local(): lax.ppermute(chain[-1] if hop < 4 else chain[-1][:1], ('z', 'core'), RING)  2.63 us
  transfers between devices with their start and end apart: 22, of which 12 were waited for; matrix products, arithmetic and copies ran while one was open for 1% of the time, Pallas kernels for 24%

profile of v5, /device:TPU:24, one launch (start us, length us, event | category | flops | bytes accessed | tf_op | source)
XLA Modules:
  0.0 98.1 jit_solution(4457053523433626614)
XLA Ops:
  0.0 1.8 %shard_map.66 = bf16[1,608,128]{2,1,0:T(8,128)(2,1)S(1)} custom-call(bf16[32,4096]{1,0:T(8,128)(2,1)} %amps_ref.1, s32[32,32]{1,0:T(8,128)} %mask_ref.1), custom_call_target="tpu_custom_call" | custom-call | tf_op jit(solution)/shard_map/pallas_call | solution.py:68
  1.9 1.4 %collective-permute-done = bf16[1,608,128]{2,1,0:T(8,128)(2,1)S(1)} collective-permute-done((bf16[1,608,128]{2,1,0:T(8,128)(2,1)S(1)}, bf16[1,608,128]{2,1,0:T(8,128)(2,1)S(1)}, u32[]{:S(2)}, u32[]{:S(2)}) %collective-permute-start) | collective-permute-done | bytes 155680 | tf_op jit(solution)/shard_map/ppermute | solution.py:28
  3.3 2.0 %collective-permute-start.1 = (bf16[2,608,128]{2,1,0:T(8,128)(2,1)S(1)}, bf16[2,608,128]{2,1,0:T(8,128)(2,1)S(1)}, u32[]{:S(2)}, u32[]{:S(2)}) collective-permute-start(bf16[2,608,128]{2,1,0:T(8,128)(2,1)S(1)} %pad_maximum_fusion.refs_4_), channel_id=1, source_target_pairs={{0,16},{16,32},{32,48},{48,64},{64,80},{80,96},{96,112},{112,0},{8... | collective-permute-start | bytes 933896 | tf_op jit(solution)/shard_map/ppermute | solution.py:304
  5.3 3.0 %collective-permute-start.7 = (bf16[1,608,128]{2,1,0:T(8,128)(2,1)S(1)}, bf16[1,608,128]{2,1,0:T(8,128)(2,1)S(1)}, u32[]{:S(2)}, u32[]{:S(2)}) collective-permute-start(bf16[1,608,128]{2,1,0:T(8,128)(2,1)S(1)} %shard_map.66), channel_id=1, source_target_pairs={{0,128},{128,0},{1,129},{129,1},{2,130},{130,2},{3,131},{131,3},{4... | collective-permute-start | bytes 466952 | tf_op jit(solution)/shard_map/ppermute | solution.py:28
  8.3 3.7 %collective-permute-done.7 = bf16[1,608,128]{2,1,0:T(8,128)(2,1)S(1)} collective-permute-done((bf16[1,608,128]{2,1,0:T(8,128)(2,1)S(1)}, bf16[1,608,128]{2,1,0:T(8,128)(2,1)S(1)}, u32[]{:S(2)}, u32[]{:S(2)}) %collective-permute-start.7) | collective-permute-done | bytes 155680 | tf_op jit(solution)/shard_map/ppermute | solution.py:28
  12.0 2.7 %collective-permute-start.8 = (bf16[1,608,128]{2,1,0:T(8,128)(2,1)S(1)}, bf16[1,608,128]{2,1,0:T(8,128)(2,1)S(1)}, u32[]{:S(2)}, u32[]{:S(2)}) collective-permute-start(bf16[1,608,128]{2,1,0:T(8,128)(2,1)S(1)} %collective-permute-done.7), channel_id=1, source_target_pairs={{0,8},{8,0},{1,9},{9,1},{2,10},{10,2},{3,11},{11,3},{4,12},{12,4},... | collective-permute-start | bytes 466952 | tf_op jit(solution)/shard_map/ppermute | solution.py:28
  14.7 1.0 %collective-permute-done.8 = bf16[1,608,128]{2,1,0:T(8,128)(2,1)S(1)} collective-permute-done((bf16[1,608,128]{2,1,0:T(8,128)(2,1)S(1)}, bf16[1,608,128]{2,1,0:T(8,128)(2,1)S(1)}, u32[]{:S(2)}, u32[]{:S(2)}) %collective-permute-start.8) | collective-permute-done | bytes 155680 | tf_op jit(solution)/shard_map/ppermute | solution.py:28
  15.7 0.3 collective-permute-start.9
  16.0 6.8 %collective-permute-done.2 = bf16[2,608,128]{2,1,0:T(8,128)(2,1)S(1)} collective-permute-done((bf16[2,608,128]{2,1,0:T(8,128)(2,1)S(1)}, bf16[2,608,128]{2,1,0:T(8,128)(2,1)S(1)}, u32[]{:S(2)}, u32[]{:S(2)}) %collective-permute-start.2) | collective-permute-done | bytes 311328 | tf_op jit(solution)/shard_map/ppermute | solution.py:304
  22.8 3.3 %collective-permute-done.9 = bf16[2,608,128]{2,1,0:T(8,128)(2,1)S(1)} collective-permute-done((bf16[2,608,128]{2,1,0:T(8,128)(2,1)S(1)}, bf16[2,608,128]{2,1,0:T(8,128)(2,1)S(1)}, u32[]{:S(2)}, u32[]{:S(2)}) %collective-permute-start.9) | collective-permute-done | bytes 311328 | tf_op jit(solution)/shard_map/ppermute | solution.py:304
  26.2 4.7 %collective-permute-done.4 = bf16[2,608,128]{2,1,0:T(8,128)(2,1)S(1)} collective-permute-done((bf16[2,608,128]{2,1,0:T(8,128)(2,1)S(1)}, bf16[2,608,128]{2,1,0:T(8,128)(2,1)S(1)}, u32[]{:S(2)}, u32[]{:S(2)}) %collective-permute-start.4) | collective-permute-done | bytes 311328 | tf_op jit(solution)/shard_map/ppermute | solution.py:304
  31.1 0.9 collective-permute-start.3
  31.9 2.3 %collective-permute-done.10 = bf16[2,608,128]{2,1,0:T(8,128)(2,1)S(1)} collective-permute-done((bf16[2,608,128]{2,1,0:T(8,128)(2,1)S(1)}, bf16[2,608,128]{2,1,0:T(8,128)(2,1)S(1)}, u32[]{:S(2)}, u32[]{:S(2)}) %collective-permute-start.10) | collective-permute-done | bytes 311328 | tf_op jit(solution)/shard_map/ppermute | solution.py:304
  34.3 3.2 %collective-permute-done.5 = bf16[1,608,128]{2,1,0:T(8,128)(2,1)S(1)} collective-permute-done((bf16[1,608,128]{2,1,0:T(8,128)(2,1)S(1)}, bf16[1,608,128]{2,1,0:T(8,128)(2,1)S(1)}, u32[]{:S(2)}, u32[]{:S(2)}) %collective-permute-start.5) | collective-permute-done | bytes 155680 | tf_op jit(solution)/shard_map/ppermute | solution.py:304
  37.6 0.7 xor_add_fusion.refs_0_
  38.3 0.6 collective-permute-start.16
  38.9 3.4 %collective-permute-done.11 = bf16[2,608,128]{2,1,0:T(8,128)(2,1)S(1)} collective-permute-done((bf16[2,608,128]{2,1,0:T(8,128)(2,1)S(1)}, bf16[2,608,128]{2,1,0:T(8,128)(2,1)S(1)}, u32[]{:S(2)}, u32[]{:S(2)}) %collective-permute-start.11) | collective-permute-done | bytes 311328 | tf_op jit(solution)/shard_map/ppermute | solution.py:304
  42.4 0.3 collective-permute-start.12
  42.7 11.6 %shard_map.67 = (f32[8,128,128]{2,1,0:T(8,128)S(1)}, s16[1040,128]{1,0:T(8,128)(2,1)S(1)}, s16[1040,128]{1,0:T(8,128)(2,1)S(1)}, s16[1040,128]{1,0:T(8,128)(2,1)...) custom-call(s32[16]{0:T(128)S(1)} %xor_add_fusion.refs_0_, s32[8,32]{1,0:T(8,128)} %refs_1_.1, ...), custom_call_target="tpu_custom_call" | custom-call | flops 10000000000 | bytes 16777216 | tf_op jit(solution)/shard_map/pallas_call | solution.py:179
  54.5 0.3 collective-permute-start.13
  54.8 2.6 %collective-permute-start.14 = (s16[1040,128]{1,0:T(8,128)(2,1)S(1)}, s16[1040,128]{1,0:T(8,128)(2,1)S(1)}, u32[]{:S(2)}, u32[]{:S(2)}) collective-permute-start(s16[1040,128]{1,0:T(8,128)(2,1)S(1)} %get-tuple-element.44), channel_id=1, source_target_pairs={{0,2},{1,3},{2,0},{3,1},{4,6},{5,7},{6,4},{7,5},{8,10},{9,11},{10,... | collective-permute-start | bytes 798728 | tf_op jit(solution)/shard_map/ppermute | solution.py:309
  57.4 10.6 %shard_map.69 = (f32[8,128,128]{2,1,0:T(8,128)S(1)}, s16[1040,128]{1,0:T(8,128)(2,1)}, s16[1040,128]{1,0:T(8,128)(2,1)}, s16[1040,128]{1,0:T(8,128)(2,1)S(1)}, s32[16,128]{1,0:T(8,128)S(1)}) custom-call(s32[16]{0:T(128)S(1)} %xor_add_fusion.refs_0_, s32[16,128]{1,0:T(8,128)S(1)} %get-tuple-element.41.over_ref.refs_1_, ...), custom_call_target="tpu_custom_call" | custom-call | flops 10000000000 | bytes 16777216 | tf_op jit(solution)/shard_map/pallas_call | solution.py:179
  68.0 3.3 %collective-permute-start.18 = (s16[1040,128]{1,0:T(8,128)(2,1)}, s16[1040,128]{1,0:T(8,128)(2,1)S(1)}, u32[]{:S(2)}, u32[]{:S(2)}) collective-permute-start(s16[1040,128]{1,0:T(8,128)(2,1)} %get-tuple-element.51), channel_id=1, source_target_pairs={{0,1},{1,2},{2,3},{3,0},{4,5},{5,6},{6,7},{7,4},{8,9},{9,10},{10,1... | collective-permute-start | bytes 798728 | tf_op jit(solution)/shard_map/ppermute | solution.py:309
  71.5 1.3 %collective-permute-start.20 = (s16[1040,128]{1,0:T(8,128)(2,1)S(1)}, s16[1040,128]{1,0:T(8,128)(2,1)S(1)}, u32[]{:S(2)}, u32[]{:S(2)}) collective-permute-start(s16[1040,128]{1,0:T(8,128)(2,1)S(1)} %get-tuple-element.53), channel_id=1, source_target_pairs={{0,3},{1,0},{2,1},{3,2},{4,7},{5,4},{6,5},{7,6},{8,11},{9,8},{10,9... | collective-permute-start | bytes 798728 | tf_op jit(solution)/shard_map/ppermute | solution.py:309
  72.8 1.4 %shard_map.68 = (f32[8,128,128]{2,1,0:T(8,128)S(1)}, s16[1040,128]{1,0:T(8,128)(2,1)S(1)}) custom-call(s32[16,128]{1,0:T(8,128)S(1)} %get-tuple-element.41.over_ref.refs_1_, f32[8,128,128]{2,1,0:T(8,128)S(1)} %get-tuple-element.42.own_ref, s16[1040,128]{1,0:T(8,128)(2,1)S(1)} %collective-permute-done.13.a_ref, ...), custom_call_target="tpu_custom_call" | custom-call | tf_op jit(solution)/shard_map/pallas_call | solution.py:221
  74.3 8.5 %collective-permute-done.18.a_ref = s16[1040,128]{1,0:T(8,128)(2,1)S(1)} collective-permute-done((s16[1040,128]{1,0:T(8,128)(2,1)}, s16[1040,128]{1,0:T(8,128)(2,1)S(1)}, u32[]{:S(2)}, u32[]{:S(2)}) %collective-permute-start.18) | collective-permute-done | bytes 266272 | tf_op jit(solution)/shard_map/ppermute | solution.py:309
  82.7 3.3 %collective-permute-done.20.c_ref = s16[1040,128]{1,0:T(8,128)(2,1)S(1)} collective-permute-done((s16[1040,128]{1,0:T(8,128)(2,1)S(1)}, s16[1040,128]{1,0:T(8,128)(2,1)S(1)}, u32[]{:S(2)}, u32[]{:S(2)}) %collective-permute-start.20) | collective-permute-done | bytes 266272 | tf_op jit(solution)/shard_map/ppermute | solution.py:309
  86.1 1.4 %shard_map.70 = (f32[8,128,128]{2,1,0:T(8,128)S(1)}, s16[1040,128]{1,0:T(8,128)(2,1)S(1)}) custom-call(s32[16,128]{1,0:T(8,128)S(1)} %get-tuple-element.49.over_ref, f32[8,128,128]{2,1,0:T(8,128)S(1)} %get-tuple-element.50.own_ref, s16[1040,128]{1,0:T(8,128)(2,1)S(1)} %collective-permute-done.18.a_ref, s16[1040,128]{1,0:T(8,128)(2,1)S(1)} %collective-permute-done.19.b_ref, ...), custom_call_target="tpu_custom_call" | custom-call | tf_op jit(solution)/shard_map/pallas_call | solution.py:221
  87.6 1.8 %collective-permute-start.21 = (s16[1040,128]{1,0:T(8,128)(2,1)S(1)}, s16[1040,128]{1,0:T(8,128)(2,1)S(1)}, u32[]{:S(2)}, u32[]{:S(2)}) collective-permute-start(s16[1040,128]{1,0:T(8,128)(2,1)S(1)} %shard_map.71.sent_ref), channel_id=1, source_target_pairs={{0,4},{4,0},{1,5},{5,1},{2,6},{6,2},{3,7},{7,3},{8,12},{12,8},{9,1... | collective-permute-start | bytes 798728 | tf_op jit(solution)/shard_map/ppermute | solution.py:28
  89.4 6.5 %collective-permute-done.21.got_ref = s16[1040,128]{1,0:T(8,128)(2,1)S(1)} collective-permute-done((s16[1040,128]{1,0:T(8,128)(2,1)S(1)}, s16[1040,128]{1,0:T(8,128)(2,1)S(1)}, u32[]{:S(2)}, u32[]{:S(2)}) %collective-permute-start.21) | collective-permute-done | bytes 266272 | tf_op jit(solution)/shard_map/ppermute | solution.py:28
  95.8 0.9 shard_map.72
  97.4 0.7 copy-done.1
  (39 shorter events, 1.0 us)
Async XLA Ops:
  1.8 1.5 %collective-permute-start = (bf16[1,608,128]{2,1,0:T(8,128)(2,1)S(1)}, bf16[1,608,128]{2,1,0:T(8,128)(2,1)S(1)}, u32[]{:S(2)}, u32[]{:S(2)}) collective-permute-start(bf16[1,608,128]{2,1,0:T(8,128)(2,1)S(1)} %shard_map.66), channel_id=1, source_target_pairs={{0,8},{8,0},{1,9},{9,1},{2,10},{10,2},{3,11},{11,3},{4,12},{12,4},... | collective-permute-start | bytes 466952 | tf_op jit(solution)/shard_map/ppermute | solution.py:28
  3.3 11.4 %collective-permute-start.1 = (bf16[2,608,128]{2,1,0:T(8,128)(2,1)S(1)}, bf16[2,608,128]{2,1,0:T(8,128)(2,1)S(1)}, u32[]{:S(2)}, u32[]{:S(2)}) collective-permute-start(bf16[2,608,128]{2,1,0:T(8,128)(2,1)S(1)} %pad_maximum_fusion.refs_4_), channel_id=1, source_target_pairs={{0,16},{16,32},{32,48},{48,64},{64,80},{80,96},{96,112},{112,0},{8... | collective-permute-start | bytes 933896 | tf_op jit(solution)/shard_map/ppermute | solution.py:304
  5.3 6.7 %collective-permute-start.7 = (bf16[1,608,128]{2,1,0:T(8,128)(2,1)S(1)}, bf16[1,608,128]{2,1,0:T(8,128)(2,1)S(1)}, u32[]{:S(2)}, u32[]{:S(2)}) collective-permute-start(bf16[1,608,128]{2,1,0:T(8,128)(2,1)S(1)} %shard_map.66), channel_id=1, source_target_pairs={{0,128},{128,0},{1,129},{129,1},{2,130},{130,2},{3,131},{131,3},{4... | collective-permute-start | bytes 466952 | tf_op jit(solution)/shard_map/ppermute | solution.py:28
  12.0 3.7 %collective-permute-start.8 = (bf16[1,608,128]{2,1,0:T(8,128)(2,1)S(1)}, bf16[1,608,128]{2,1,0:T(8,128)(2,1)S(1)}, u32[]{:S(2)}, u32[]{:S(2)}) collective-permute-start(bf16[1,608,128]{2,1,0:T(8,128)(2,1)S(1)} %collective-permute-done.7), channel_id=1, source_target_pairs={{0,8},{8,0},{1,9},{9,1},{2,10},{10,2},{3,11},{11,3},{4,12},{12,4},... | collective-permute-start | bytes 466952 | tf_op jit(solution)/shard_map/ppermute | solution.py:28
  14.7 8.1 %collective-permute-start.2 = (bf16[2,608,128]{2,1,0:T(8,128)(2,1)S(1)}, bf16[2,608,128]{2,1,0:T(8,128)(2,1)S(1)}, u32[]{:S(2)}, u32[]{:S(2)}) collective-permute-start(bf16[2,608,128]{2,1,0:T(8,128)(2,1)S(1)} %collective-permute-done.1), channel_id=1, source_target_pairs={{0,16},{16,32},{32,48},{48,64},{64,80},{80,96},{96,112},{112,0},{8... | collective-permute-start | bytes 933896 | tf_op jit(solution)/shard_map/ppermute | solution.py:304
  15.7 10.4 %collective-permute-start.9 = (bf16[2,608,128]{2,1,0:T(8,128)(2,1)S(1)}, bf16[2,608,128]{2,1,0:T(8,128)(2,1)S(1)}, u32[]{:S(2)}, u32[]{:S(2)}) collective-permute-start(bf16[2,608,128]{2,1,0:T(8,128)(2,1)S(1)} %constant_dynamic-update-slice_fusion.4.refs_3_), channel_id=1, source_target_pairs={{0,16},{16,32},{32,48},{48,64},{64,80},{80,96},{96,112},{112,0},{8... | collective-permute-start | bytes 933896 | tf_op jit(solution)/shard_map/ppermute | solution.py:304
  22.8 8.1 %collective-permute-start.4 = (bf16[2,608,128]{2,1,0:T(8,128)(2,1)S(1)}, bf16[2,608,128]{2,1,0:T(8,128)(2,1)S(1)}, u32[]{:S(2)}, u32[]{:S(2)}) collective-permute-start(bf16[2,608,128]{2,1,0:T(8,128)(2,1)S(1)} %collective-permute-done.2), channel_id=1, source_target_pairs={{0,16},{16,32},{32,48},{48,64},{64,80},{80,96},{96,112},{112,0},{8... | collective-permute-start | bytes 933896 | tf_op jit(solution)/shard_map/ppermute | solution.py:304
  26.1 8.1 %collective-permute-start.10 = (bf16[2,608,128]{2,1,0:T(8,128)(2,1)S(1)}, bf16[2,608,128]{2,1,0:T(8,128)(2,1)S(1)}, u32[]{:S(2)}, u32[]{:S(2)}) collective-permute-start(bf16[2,608,128]{2,1,0:T(8,128)(2,1)S(1)} %collective-permute-done.9), channel_id=1, source_target_pairs={{0,16},{16,32},{32,48},{48,64},{64,80},{80,96},{96,112},{112,0},{8... | collective-permute-start | bytes 933896 | tf_op jit(solution)/shard_map/ppermute | solution.py:304
  30.9 6.5 %collective-permute-start.5 = (bf16[1,608,128]{2,1,0:T(8,128)(2,1)S(1)}, bf16[1,608,128]{2,1,0:T(8,128)(2,1)S(1)}, u32[]{:S(2)}, u32[]{:S(2)}) collective-permute-start(bf16[1,608,128]{2,1,0:T(8,128)(2,1)S(1)} %slice.8), channel_id=1, source_target_pairs={{0,16},{16,32},{32,48},{48,64},{64,80},{80,96},{96,112},{112,0},{8... | collective-permute-start | bytes 466952 | tf_op jit(solution)/shard_map/ppermute | solution.py:304
  31.1 11.6 %collective-permute-start.3 = (bf16[4,608,128]{2,1,0:T(8,128)(2,1)S(1)}, bf16[4,608,128]{2,1,0:T(8,128)(2,1)S(1)}, u32[]{:S(2)}, u32[]{:S(2)}) collective-permute-start(bf16[4,608,128]{2,1,0:T(8,128)(2,1)S(1)} %constant_dynamic-update-slice_fusion.refs_5_), channel_id=1, source_target_pairs={{0,8},{8,0},{1,9},{9,1},{2,10},{10,2},{3,11},{11,3},{4,12},{12,4},... | collective-permute-start | bytes 1867784 | tf_op jit(solution)/shard_map/ppermute | solution.py:28
  34.2 8.1 %collective-permute-start.11 = (bf16[2,608,128]{2,1,0:T(8,128)(2,1)S(1)}, bf16[2,608,128]{2,1,0:T(8,128)(2,1)S(1)}, u32[]{:S(2)}, u32[]{:S(2)}) collective-permute-start(bf16[2,608,128]{2,1,0:T(8,128)(2,1)S(1)} %collective-permute-done.10), channel_id=1, source_target_pairs={{0,16},{16,32},{32,48},{48,64},{64,80},{80,96},{96,112},{112,0},{8... | collective-permute-start | bytes 933896 | tf_op jit(solution)/shard_map/ppermute | solution.py:304
  37.5 5.2 %collective-permute-start.6 = (bf16[3,608,128]{2,1,0:T(8,128)(2,1)S(1)}, bf16[3,608,128]{2,1,0:T(8,128)(2,1)S(1)}, u32[]{:S(2)}, u32[]{:S(2)}) collective-permute-start(bf16[3,608,128]{2,1,0:T(8,128)(2,1)S(1)} %constant_dynamic-update-slice_fusion.2.refs_7_), channel_id=1, source_target_pairs={{0,8},{8,0},{1,9},{9,1},{2,10},{10,2},{3,11},{11,3},{4,12},{12,4},... | collective-permute-start | bytes 1400840 | tf_op jit(solution)/shard_map/ppermute | solution.py:28
  38.3 19.0 %collective-permute-start.16 = (bf16[4,608,128]{2,1,0:T(8,128)(2,1)S(1)}, bf16[4,608,128]{2,1,0:T(8,128)(2,1)S(1)}, u32[]{:S(2)}, u32[]{:S(2)}) collective-permute-start(bf16[4,608,128]{2,1,0:T(8,128)(2,1)S(1)} %constant_dynamic-update-slice_fusion.6.refs_4_), channel_id=1, source_target_pairs={{0,8},{8,0},{1,9},{9,1},{2,10},{10,2},{3,11},{11,3},{4,12},{12,4},... | collective-permute-start | bytes 1867784 | tf_op jit(solution)/shard_map/ppermute | solution.py:28
  42.4 12.0 %collective-permute-start.12 = (bf16[1,608,128]{2,1,0:T(8,128)(2,1)S(1)}, bf16[1,608,128]{2,1,0:T(8,128)(2,1)S(1)}, u32[]{:S(2)}, u32[]{:S(2)}) collective-permute-start(bf16[1,608,128]{2,1,0:T(8,128)(2,1)S(1)} %slice.9), channel_id=1, source_target_pairs={{0,16},{16,32},{32,48},{48,64},{64,80},{80,96},{96,112},{112,0},{8... | collective-permute-start | bytes 466952 | tf_op jit(solution)/shard_map/ppermute | solution.py:304
  54.4 3.0 %collective-permute-start.17 = (bf16[3,608,128]{2,1,0:T(8,128)(2,1)S(1)}, bf16[3,608,128]{2,1,0:T(8,128)(2,1)S(1)}, u32[]{:S(2)}, u32[]{:S(2)}) collective-permute-start(bf16[3,608,128]{2,1,0:T(8,128)(2,1)S(1)} %constant_dynamic-update-slice_fusion.8.refs_6_), channel_id=1, source_target_pairs={{0,8},{8,0},{1,9},{9,1},{2,10},{10,2},{3,11},{11,3},{4,12},{12,4},... | collective-permute-start | bytes 1400840 | tf_op jit(solution)/shard_map/ppermute | solution.py:28
  54.5 17.1 %collective-permute-start.13 = (s16[1040,128]{1,0:T(8,128)(2,1)S(1)}, s16[1040,128]{1,0:T(8,128)(2,1)S(1)}, u32[]{:S(2)}, u32[]{:S(2)}) collective-permute-start(s16[1040,128]{1,0:T(8,128)(2,1)S(1)} %get-tuple-element.43), channel_id=1, source_target_pairs={{0,1},{1,2},{2,3},{3,0},{4,5},{5,6},{6,7},{7,4},{8,9},{9,10},{10,1... | collective-permute-start | bytes 798728 | tf_op jit(solution)/shard_map/ppermute | solution.py:309
  54.8 18.1 %collective-permute-start.14 = (s16[1040,128]{1,0:T(8,128)(2,1)S(1)}, s16[1040,128]{1,0:T(8,128)(2,1)S(1)}, u32[]{:S(2)}, u32[]{:S(2)}) collective-permute-start(s16[1040,128]{1,0:T(8,128)(2,1)S(1)} %get-tuple-element.44), channel_id=1, source_target_pairs={{0,2},{1,3},{2,0},{3,1},{4,6},{5,7},{6,4},{7,5},{8,10},{9,11},{10,... | collective-permute-start | bytes 798728 | tf_op jit(solution)/shard_map/ppermute | solution.py:309
  57.3 15.5 %collective-permute-start.15 = (s16[1040,128]{1,0:T(8,128)(2,1)S(1)}, s16[1040,128]{1,0:T(8,128)(2,1)S(1)}, u32[]{:S(2)}, u32[]{:S(2)}) collective-permute-start(s16[1040,128]{1,0:T(8,128)(2,1)S(1)} %get-tuple-element.45), channel_id=1, source_target_pairs={{0,3},{1,0},{2,1},{3,2},{4,7},{5,4},{6,5},{7,6},{8,11},{9,8},{10,9... | collective-permute-start | bytes 798728 | tf_op jit(solution)/shard_map/ppermute | solution.py:309
  57.4 40.0 %copy-start = (s32[8,32]{1,0:T(8,128)S(1)}, s32[8,32]{1,0:T(8,128)}, u32[]{:S(2)}) copy-start(s32[8,32]{1,0:T(8,128)} %refs_1_.1) | copy-start | bytes 3076
  68.0 14.7 %collective-permute-start.18 = (s16[1040,128]{1,0:T(8,128)(2,1)}, s16[1040,128]{1,0:T(8,128)(2,1)S(1)}, u32[]{:S(2)}, u32[]{:S(2)}) collective-permute-start(s16[1040,128]{1,0:T(8,128)(2,1)} %get-tuple-element.51), channel_id=1, source_target_pairs={{0,1},{1,2},{2,3},{3,0},{4,5},{5,6},{6,7},{7,4},{8,9},{9,10},{10,1... | collective-permute-start | bytes 798728 | tf_op jit(solution)/shard_map/ppermute | solution.py:309
  71.3 11.4 %collective-permute-start.19 = (s16[1040,128]{1,0:T(8,128)(2,1)}, s16[1040,128]{1,0:T(8,128)(2,1)S(1)}, u32[]{:S(2)}, u32[]{:S(2)}) collective-permute-start(s16[1040,128]{1,0:T(8,128)(2,1)} %get-tuple-element.52), channel_id=1, source_target_pairs={{0,2},{1,3},{2,0},{3,1},{4,6},{5,7},{6,4},{7,5},{8,10},{9,11},{10,... | collective-permute-start | bytes 798728 | tf_op jit(solution)/shard_map/ppermute | solution.py:309
  71.5 14.5 %collective-permute-start.20 = (s16[1040,128]{1,0:T(8,128)(2,1)S(1)}, s16[1040,128]{1,0:T(8,128)(2,1)S(1)}, u32[]{:S(2)}, u32[]{:S(2)}) collective-permute-start(s16[1040,128]{1,0:T(8,128)(2,1)S(1)} %get-tuple-element.53), channel_id=1, source_target_pairs={{0,3},{1,0},{2,1},{3,2},{4,7},{5,4},{6,5},{7,6},{8,11},{9,8},{10,9... | collective-permute-start | bytes 798728 | tf_op jit(solution)/shard_map/ppermute | solution.py:309
  87.6 8.3 %collective-permute-start.21 = (s16[1040,128]{1,0:T(8,128)(2,1)S(1)}, s16[1040,128]{1,0:T(8,128)(2,1)S(1)}, u32[]{:S(2)}, u32[]{:S(2)}) collective-permute-start(s16[1040,128]{1,0:T(8,128)(2,1)S(1)} %shard_map.71.sent_ref), channel_id=1, source_target_pairs={{0,4},{4,0},{1,5},{5,1},{2,6},{6,2},{3,7},{7,3},{8,12},{12,8},{9,1... | collective-permute-start | bytes 798728 | tf_op jit(solution)/shard_map/ppermute | solution.py:28
  97.4 0.7 copy-start.1

commit v6 on v5

--- a/solution.py
+++ b/solution.py
@@ -84,7 +84,7 @@
 
 
 def scales(msg_ref):
-    powers = msg_ref[RT * TILE :, :].astype(I32).astype(F32)
+    powers = msg_ref[msg_ref.shape[0] - META :, :].astype(I32).astype(F32)
     return jnp.exp2(jnp.transpose(jnp.concatenate([powers] * (TILE // META), axis=0)))
 
 
@@ -93,7 +93,7 @@
 
 
 def flags(msg_ref):
-    return msg_ref[RT * TILE :, :].astype(I32)
+    return msg_ref[msg_ref.shape[0] - META :, :].astype(I32)
 
 
 def powers_and_flags(powers, flag):
@@ -102,24 +102,7 @@
     return jnp.where(row < RT, powers, flag).astype(I16)
 
 
-def chunk_kernel(sizes, mask, row_ref, *refs):
-    if mask:
-        mask_ref, *refs = refs
-    before_ref, ints_ref, *refs = refs
-    ins, refs = refs[: len(sizes)], refs[len(sizes) :]
-    own_ref, a_ref, b_ref, c_ref, over_ref, *refs = refs
-    if mask:
-        kept_ref, *refs = refs
-    got, amps, held, sem = refs
-
-    def load(j):
-        return pltpu.make_async_copy(ints_ref.at[pl.ds(j * 2 * TILE, 2 * TILE), :], held.at[j], sem.at[0, j])
-
-    def store(j):
-        return pltpu.make_async_copy(held.at[j], kept_ref.at[pl.ds(j * 2 * TILE, 2 * TILE), :], sem.at[1, j])
-
-    for j in range(RT // 2):
-        load(j).start()
+def unpack_all(sizes, row_ref, ins, got, amps):
     i = 0
     for size, ref in zip(sizes, ins, strict=True):
         got[i : i + size] = ref[...]
@@ -138,101 +121,186 @@
         return jnp.maximum(over, place[:META, TILE - 1 :])
 
     over = lax.fori_loop(0, i, unpack, jnp.zeros((META, 1), F32), unroll=4)
-    over = jnp.maximum(jnp.broadcast_to(over, (META, TILE)).astype(I32), before_ref[...])
-    over_ref[...] = over
+    return jnp.broadcast_to(over, (META, TILE)).astype(I32)
+
+
+def block_copy(ints_ref, held, sem, low):
+    return lambda j: pltpu.make_async_copy(
+        ints_ref.at[pl.ds((low + j) * 2 * TILE, 2 * TILE), :], held.at[j], sem.at[j]
+    )
+
+
+def multiply_all(amps, held, load, over, own_ref, coded_refs, prepare=None):
     lane = lax.broadcasted_iota(I32, (TILE, TILE), 1)
 
     def multiply(j, powers):
         load(j).wait()
-        if mask:
-            for n in range(2):
-                for t in range(TILES):
-                    kept = jnp.where(mask_ref[2 * j + n, t] > 0, 1.0, 0.0).astype(BF16)
-                    part = (j, slice(n * TILE, (n + 1) * TILE), slice(t * TILE, (t + 1) * TILE))
-                    held[part] = held[part] * kept
-            store(j).start()
+        if prepare is not None:
+            prepare(j)
         value = lax.dot_general(amps[...], held[j], (((1,), (1,)), ((), ())), preferred_element_type=F32)
         for n in range(2):
             t = 2 * j + n
             own_ref[t] = value[:TILE, n * TILE : (n + 1) * TILE]
             new = []
-            for d, out in enumerate((a_ref, b_ref, c_ref)):
+            for d, out in enumerate(coded_refs):
                 coded, power = code(value[(d + 1) * TILE : (d + 2) * TILE, n * TILE : (n + 1) * TILE])
                 out[pl.ds(pl.multiple_of(t * TILE, TILE), TILE), :] = coded
                 new.append(jnp.where(lane == t, power, powers[d]))
             powers = tuple(new)
         return powers
 
-    powers = lax.fori_loop(0, RT // 2, multiply, (jnp.zeros((TILE, TILE), F32),) * 3)
-    for d, out in enumerate((a_ref, b_ref, c_ref)):
-        out[RT * TILE :, :] = powers_and_flags(powers[d], over)
-    if mask:
-        for j in range(RT // 2):
-            store(j).wait()
-
-
-def chunk_sums(rows, before, ints, messages, mask=None):
+    powers = lax.fori_loop(0, held.shape[0], multiply, (jnp.zeros((TILE, TILE), F32),) * 3)
+    for d, out in enumerate(coded_refs):
+        out[out.shape[0] - META :, :] = powers_and_flags(powers[d], over)
+
+
+def first_kernel(sizes, row_ref, mask_ref, ints_ref, *refs):
+    ins, refs = refs[: len(sizes)], refs[len(sizes) :]
+    own_ref, a_ref, b_ref, c_ref, over_ref, kept_ref, got, amps, held, sem, kept_sem = refs
+    load = block_copy(ints_ref, held, sem, 0)
+    blocks = held.shape[0]
+    for j in range(blocks):
+        load(j).start()
+
+    def store(j):
+        return pltpu.make_async_copy(held.at[j], kept_ref.at[pl.ds(j * 2 * TILE, 2 * TILE), :], kept_sem.at[j])
+
+    def prepare(j):
+        for n in range(2):
+            for t in range(TILES):
+                kept = jnp.where(mask_ref[2 * j + n, t] > 0, 1.0, 0.0).astype(BF16)
+                part = (j, slice(n * TILE, (n + 1) * TILE), slice(t * TILE, (t + 1) * TILE))
+                held[part] = held[part] * kept
+        store(j).start()
+
+    over = unpack_all(sizes, row_ref, ins, got, amps)
+    over_ref[...] = over
+    multiply_all(amps, held, load, over, own_ref, (a_ref, b_ref, c_ref), prepare)
+    for j in range(blocks):
+        store(j).wait()
+
+
+def second_kernel(sizes, row_ref, before_ref, ints_ref, *refs):
+    ins, refs = refs[: len(sizes)], refs[len(sizes) :]
+    own_ref, a_ref, b_ref, c_ref, over_ref, amps, got, held, sem = refs
+    load = block_copy(ints_ref, held, sem, 0)
+    for j in range(held.shape[0]):
+        load(j).start()
+    over = jnp.maximum(unpack_all(sizes, row_ref, ins, got, amps), before_ref[...])
+    over_ref[...] = over
+    multiply_all(amps, held, load, over, own_ref, (a_ref, b_ref, c_ref))
+
+
+def third_kernel(over_ref, ints_ref, amps, own_ref, a_ref, b_ref, c_ref, held, sem):
+    load = block_copy(ints_ref, held, sem, held.shape[0])
+    for j in range(held.shape[0]):
+        load(j).start()
+    multiply_all(amps, held, load, over_ref[...], own_ref, (a_ref, b_ref, c_ref))
+
+
+ANYWHERE = pl.BlockSpec(memory_space=pl.ANY)
+FLAGS = jax.ShapeDtypeStruct((META, TILE), I32)
+AMPS = (16 * OWN, TILES * TILE)
+
+
+def sums_of(tiles):
+    coded = jax.ShapeDtypeStruct((tiles * TILE + META, TILE), I16)
+    return [jax.ShapeDtypeStruct((tiles, TILE, TILE), F32), coded, coded, coded]
+
+
+def work(tiles):
+    return {
+        "compiler_params": pltpu.CompilerParams(vmem_limit_bytes=44 << 20),
+        "cost_estimate": pl.CostEstimate(
+            flops=tiles * 1_250_000_000, bytes_accessed=tiles * (2 << 20), transcendentals=0
+        ),
+    }
+
+
+def held_blocks(tiles):
+    return pltpu.VMEM((tiles // 2, 2 * TILE, TILES * TILE), BF16)
+
+
+def first_chunk(rows, mask, ints, messages):
     sizes = [m.shape[0] for m in messages]
-    masks = [] if mask is None else [mask]
-    coded = jax.ShapeDtypeStruct((RT * TILE + META, TILE), I16)
-    anywhere = pl.BlockSpec(memory_space=pl.ANY)
-    return pl.pallas_call(
-        lambda *refs: chunk_kernel(sizes, mask is not None, *refs),
-        in_specs=[SMEM] * (1 + len(masks)) + [VMEM, anywhere] + [VMEM] * len(sizes),
-        out_specs=[VMEM] * 5 + [anywhere] * len(masks),
-        out_shape=[
-            jax.ShapeDtypeStruct((RT, TILE, TILE), F32),
-            coded,
-            coded,
-            coded,
-            jax.ShapeDtypeStruct((META, TILE), I32),
-        ]
-        + [jax.ShapeDtypeStruct(ints.shape, BF16)] * len(masks),
+    return pl.pallas_call(
+        lambda *refs: first_kernel(sizes, *refs),
+        in_specs=[SMEM, SMEM, ANYWHERE] + [VMEM] * len(sizes),
+        out_specs=[VMEM] * 5 + [ANYWHERE],
+        out_shape=[*sums_of(RT), FLAGS, jax.ShapeDtypeStruct(ints.shape, BF16)],
         scratch_shapes=[
             pltpu.VMEM((sum(sizes), MSG, TILE), BF16),
-            pltpu.VMEM((sum(sizes) * OWN, TILES * TILE), BF16),
-            pltpu.VMEM((RT // 2, 2 * TILE, TILES * TILE), BF16),
-            pltpu.SemaphoreType.DMA((2, RT // 2)),
+            pltpu.VMEM(AMPS, BF16),
+            held_blocks(RT),
+            pltpu.SemaphoreType.DMA((RT // 2,)),
+            pltpu.SemaphoreType.DMA((RT // 2,)),
         ],
-        compiler_params=pltpu.CompilerParams(vmem_limit_bytes=44 << 20),
-        cost_estimate=pl.CostEstimate(flops=10_000_000_000, bytes_accessed=16 << 20, transcendentals=0),
-    )(rows, *masks, before, ints, *messages)
-
-
-def add_kernel(over_ref, own_ref, a_ref, b_ref, c_ref, sum_ref, out_ref):
+        **work(RT),
+    )(rows, mask, ints, *messages)
+
+
+def second_chunk(rows, before, ints, messages):
+    sizes = [m.shape[0] for m in messages]
+    return pl.pallas_call(
+        lambda *refs: second_kernel(sizes, *refs),
+        in_specs=[SMEM, VMEM, ANYWHERE] + [VMEM] * len(sizes),
+        out_specs=[VMEM] * 6,
+        out_shape=[*sums_of(RT // 2), FLAGS, jax.ShapeDtypeStruct(AMPS, BF16)],
+        scratch_shapes=[
+            pltpu.VMEM((sum(sizes), MSG, TILE), BF16),
+            held_blocks(RT // 2),
+            pltpu.SemaphoreType.DMA((RT // 4,)),
+        ],
+        **work(RT // 2),
+    )(rows, before, ints, *messages)
+
+
+def second_half(over, ints, amps):
+    return pl.pallas_call(
+        third_kernel,
+        in_specs=[VMEM, ANYWHERE, VMEM],
+        out_specs=[VMEM] * 4,
+        out_shape=sums_of(RT // 2),
+        scratch_shapes=[held_blocks(RT // 2), pltpu.SemaphoreType.DMA((RT // 4,))],
+        **work(RT // 2),
+    )(over, ints, amps)
+
+
+def add_kernel(over_ref, own_ref, a_ref, b_ref, c_ref, sum_ref, *outs):
     lane = lax.broadcasted_iota(I32, (TILE, TILE), 1)
     parts = (a_ref, b_ref, c_ref)
     scale = [scales(ref) for ref in parts]
-    powers = jnp.zeros((TILE, TILE), F32)
-    for t in range(RT):
-        value = own_ref[t]
-        for ref, by in zip(parts, scale, strict=True):
-            value = value + decode(ref, by, t)
-        sum_ref[t] = value
-        out_ref[tile_rows(t), :], power = code(value)
-        powers = jnp.where(lane == t, power, powers)
     flag = over_ref[...]
     for ref in parts:
         flag = jnp.maximum(flag, jnp.broadcast_to(flags(ref)[META - 1 :, :], (META, TILE)))
-    out_ref[RT * TILE :, :] = powers_and_flags(powers, flag)
-
-
-def add(over, own, parts):
+    each = own_ref.shape[0] // len(outs)
+    for n, out in enumerate(outs):
+        powers = jnp.zeros((TILE, TILE), F32)
+        for i in range(each):
+            t = n * each + i
+            value = own_ref[t]
+            for ref, by in zip(parts, scale, strict=True):
+                value = value + decode(ref, by, t)
+            sum_ref[t] = value
+            out[tile_rows(i), :], power = code(value)
+            powers = jnp.where(lane == i, power, powers)
+        out[each * TILE :, :] = powers_and_flags(powers, flag)
+
+
+def add(over, own, parts, pieces):
+    coded = jax.ShapeDtypeStruct((RT // 2 * TILE + META, TILE), I16)
     return pl.pallas_call(
         add_kernel,
         in_specs=[VMEM] * 5,
-        out_specs=[VMEM] * 2,
-        out_shape=[
-            jax.ShapeDtypeStruct(own.shape, F32),
-            jax.ShapeDtypeStruct((RT * TILE + META, TILE), I16),
-        ],
+        out_specs=[VMEM] * (1 + pieces),
+        out_shape=[jax.ShapeDtypeStruct(own.shape, F32)] + [coded] * pieces,
         compiler_params=pltpu.CompilerParams(vmem_limit_bytes=8 << 20),
     )(over, own, *parts)
 
 
 def choose_kernel(near_ref, first_ref, second_ref, out_ref):
     near = near_ref[0] > 0
-    both = RT * TILE
+    both = first_ref.shape[0] - META
     out_ref[:both, :] = jnp.where(near, second_ref[:both, :].astype(I32), first_ref[:both, :].astype(I32)).astype(I16)
     first, second = flags(first_ref), flags(second_ref)
     row = lax.broadcasted_iota(I32, (META, TILE), 0)
@@ -249,23 +317,26 @@
     )(near, first, second)
 
 
-def last_kernel(near_ref, first_ref, second_ref, sent_ref, got_ref, out_ref, over_ref):
+def last_kernel(near_ref, first_ref, second_a, second_b, sent_ref, got_a, got_b, out_ref, over_ref):
     near = near_ref[0] > 0
-    scale = scales(got_ref)
-    for t in range(RT):
-        mine = jnp.where(near, first_ref[t], second_ref[t])
-        out_ref[:, t * TILE : (t + 1) * TILE] = (mine + decode(got_ref, scale, t)).astype(BF16)
-    over_ref[0] = jnp.max(jnp.maximum(flags(sent_ref), flags(got_ref))[RT:, :])
-
-
-def last(near, first, second, sent, got):
+    half = RT // 2
+    for n, (second_ref, got_ref) in enumerate(((second_a, got_a), (second_b, got_b))):
+        scale = scales(got_ref)
+        for i in range(half):
+            t = n * half + i
+            mine = jnp.where(near, first_ref[t], second_ref[i])
+            out_ref[:, t * TILE : (t + 1) * TILE] = (mine + decode(got_ref, scale, i)).astype(BF16)
+    over_ref[0] = jnp.max(jnp.maximum(flags(sent_ref), flags(got_b))[RT:, :])
+
+
+def last(near, first, seconds, sent, got):
     return pl.pallas_call(
         last_kernel,
-        in_specs=[SMEM] + [VMEM] * 4,
+        in_specs=[SMEM] + [VMEM] * 6,
         out_specs=[VMEM, SMEM],
         out_shape=[jax.ShapeDtypeStruct((TILE, RT * TILE), BF16), jax.ShapeDtypeStruct((1,), I32)],
         compiler_params=pltpu.CompilerParams(vmem_limit_bytes=8 << 20),
-    )(near, first, second, sent, got)
+    )(near, first, *seconds, sent, *got)
 
 
 def plain(amplitudes, integrals, amp_mask, int_mask):
@@ -297,30 +368,46 @@
     rows = (((far >> 1) - y) & 3) * 4 + (far & 1) * 2 + (core ^ jnp.asarray(OTHER, I32))
 
     own = pack(amplitudes, amp_mask)
-    across = swap(own, "xh")
-    blocks = [[jnp.concatenate([message, swap(message, "core")], axis=0)] for message in (own, across)]
-    for hop in range(1, 5):
-        for chain in blocks:
-            chain.append(lax.ppermute(chain[-1] if hop < 4 else chain[-1][:1], ("z", "core"), RING))
+
+    def hop(block):
+        return lax.ppermute(block, ("z", "core"), RING)
+
+    def with_sibling(message):
+        return jnp.concatenate([message, swap(message, "core")], axis=0)
+
+    near_chain = [with_sibling(own)]
+    first, far_pair = lax.optimization_barrier((hop(near_chain[0]), with_sibling(swap(own, "xh"))))
+    second, far_first = lax.optimization_barrier((hop(first), hop(far_pair)))
+    third, far_second = lax.optimization_barrier((hop(second), hop(far_first)))
+    near_chain += [first, second, third]
+    opposite = hop(third[:1])
+    far_chain = [far_pair, far_first, far_second, hop(far_second)]
+    blocks = [near_chain, far_chain]
+    opposite_across = swap(opposite, "xh")
     two = [jnp.concatenate(chain[1:3], axis=0) for chain in blocks]
-    rest = jnp.concatenate(blocks[0][3:], axis=0)
+    rest = jnp.concatenate([blocks[0][3], opposite], axis=0)
 
     def spread(parts):
         return [lax.ppermute(part, "y", [(i, (i + d + 1) % 4) for i in range(4)]) for d, part in enumerate(parts)]
 
-    over = jnp.zeros((META, TILE), I32)
     held = [blocks[0][0], two[0], swap(two[0], "core"), rest, swap(rest, "core")]
-    own_part, *parts, over, kept_ints = chunk_sums(rows, over, integrals, held, int_mask)
-    over, late = lax.optimization_barrier((over, blocks[1][4]))
-    rest = jnp.concatenate([blocks[1][3], late], axis=0)
+    own_part, *parts, over, kept_ints = first_chunk(rows, int_mask, integrals, held)
+    over, *late = lax.optimization_barrier((over, blocks[1][3], opposite_across))
+    rest = jnp.concatenate(late, axis=0)
     held = [blocks[1][0], two[1], swap(two[1], "core"), rest, swap(rest, "core")]
-    sums, coded = zip(add(over, own_part, spread(parts)))
-    own_part, *parts, over = chunk_sums(rows, over, kept_ints, held)
-    total, sent = add(over, own_part, spread(parts))
-    sums, coded = (*sums, total), (*coded, sent)
+    first_sum, *first_coded = add(over, own_part, spread(parts), 2)
+
     near = near.astype(I32).reshape(1)
-    sent = choose(near, *coded)
-    out, over = last(near, *sums, sent, swap(sent, "xl"))
+    seconds, got = [], []
+    own_part, *parts, over, amps = second_chunk(rows, over, kept_ints, held)
+    for half in range(2):
+        if half == 1:
+            own_part, *parts = second_half(over, kept_ints, amps)
+        total, coded = add(over, own_part, spread(parts), 1)
+        sent = choose(near, first_coded[half], coded)
+        seconds.append(total)
+        got.append(swap(sent, "xl"))
+    out, over = last(near, first_sum, seconds, sent, got)
     return lax.cond(
         over[0] > 0,
         lambda out: plain(amplitudes, integrals, amp_mask, int_mask),

time: 98.3 us -> 101 us (1.027)
  waiting for transfers between devices: 48.2 us -> 44.5 us
  starting transfers between devices: 19.5 us -> 21.9 us
  local copies, waits for them, and re-layouts: 0.97 us -> 2.9 us
  Pallas kernels: 27.9 us -> 29.1 us
    ppermute x8 -> x7, waiting for transfers between devices: 23.8 us -> 33 us  [hop(): return lax.ppermute(block, ('z', 'core'), RING)]
    ppermute x6 -> x9, waiting for transfers between devices: 11.8 us -> 3.33 us  [spread(): lax.ppermute(part, 'y', [(i, (i + d + 1) % 4) for i in range(4)])]
    ppermute x8 -> x10, waiting for transfers between devices: 12.6 us -> 8.13 us  [swap(): return lax.ppermute(x, axis, [(0, 1), (1, 0)])]
    ppermute x6 -> x9, starting transfers between devices: 7.72 us -> 11.8 us  [spread(): lax.ppermute(part, 'y', [(i, (i + d + 1) % 4) for i in range(4)])]
    ppermute x8 -> x10, starting transfers between devices: 9.18 us -> 7.93 us  [swap(): return lax.ppermute(x, axis, [(0, 1), (1, 0)])]
    pallas_call x5 -> x7, Pallas kernels: 26 us -> 27.2 us  [the longest x1 11.6 us: first_chunk(): pl.pallas_call(lambda *refs: first_kernel(sizes, *refs), in_specs=[SMEM,...]
    ppermute x8 -> x7, starting transfers between devices: 2.63 us -> 2.17 us  [hop(): return lax.ppermute(block, ('z', 'core'), RING)]
  transfers between devices with their start and end apart: 22 -> 26, of which waited for: 12 -> 11; matrix products, arithmetic and copies ran while one was open for 1% -> 3% of each run, Pallas kernels for 24% -> 26%
where the time goes in v6:
time: 101 us; the launch traced here: 100 us
  waiting for transfers between devices  44.5 us (44%)
  Pallas kernels  29.1 us (29%)
  starting transfers between devices  21.9 us (22%)
  local copies, waits for them, and re-layouts  2.9 us (3%)
    ppermute x7, waiting for transfers between devices, hop(): return lax.ppermute(block, ('z', 'core'), RING)  33 us
    ppermute x9, starting transfers between devices, spread(): lax.ppermute(part, 'y', [(i, (i + d + 1) % 4) for i in range(4)])  11.8 us
    pallas_call x1, Pallas kernels, first_chunk(): pl.pallas_call(lambda *refs: first_kernel(sizes, *refs), in_specs=[SMEM,...  11.6 us
    ppermute x10, waiting for transfers between devices, swap(): return lax.ppermute(x, axis, [(0, 1), (1, 0)])  8.13 us
    ppermute x10, starting transfers between devices, swap(): return lax.ppermute(x, axis, [(0, 1), (1, 0)])  7.93 us
    pallas_call x1, Pallas kernels, second_chunk(): pl.pallas_call(lambda *refs: second_kernel(sizes, *refs), in_specs=[SMEM,...  6.85 us
    pallas_call x1, Pallas kernels, second_half(): pl.pallas_call(third_kernel, in_specs=[VMEM, ANYWHERE, VMEM], out_specs=[...  4.59 us
    ppermute x9, waiting for transfers between devices, spread(): lax.ppermute(part, 'y', [(i, (i + d + 1) % 4) for i in range(4)])  3.33 us
  transfers between devices with their start and end apart: 26, of which 11 were waited for; matrix products, arithmetic and copies ran while one was open for 3% of the time, Pallas kernels for 26%

profile of v6, /device:TPU:24, one launch (start us, length us, event | category | flops | bytes accessed | tf_op | source)
XLA Modules:
  0.0 100.4 jit_solution(1249879506860993834)
XLA Ops:
  0.0 1.8 %shard_map.66 = bf16[1,608,128]{2,1,0:T(8,128)(2,1)S(1)} custom-call(bf16[32,4096]{1,0:T(8,128)(2,1)} %amps_ref.1, s32[32,32]{1,0:T(8,128)} %mask_ref.1), custom_call_target="tpu_custom_call" | custom-call | tf_op jit(solution)/shard_map/pallas_call | solution.py:68
  1.9 3.1 %collective-permute-start.2 = (bf16[1,608,128]{2,1,0:T(8,128)(2,1)S(1)}, bf16[1,608,128]{2,1,0:T(8,128)(2,1)S(1)}, u32[]{:S(2)}, u32[]{:S(2)}) collective-permute-start(bf16[1,608,128]{2,1,0:T(8,128)(2,1)S(1)} %shard_map.66), channel_id=1, source_target_pairs={{0,128},{128,0},{1,129},{129,1},{2,130},{130,2},{3,131},{131,3},{4... | collective-permute-start | bytes 466952 | tf_op jit(solution)/shard_map/ppermute | solution.py:28
  5.0 2.0 %collective-permute-start.1 = (bf16[2,608,128]{2,1,0:T(8,128)(2,1)S(1)}, bf16[2,608,128]{2,1,0:T(8,128)(2,1)S(1)}, u32[]{:S(2)}, u32[]{:S(2)}) collective-permute-start(bf16[2,608,128]{2,1,0:T(8,128)(2,1)S(1)} %pad_maximum_fusion.refs_3_), channel_id=1, source_target_pairs={{0,16},{16,32},{32,48},{48,64},{64,80},{80,96},{96,112},{112,0},{8... | collective-permute-start | bytes 933896 | tf_op jit(solution)/shard_map/ppermute | solution.py:373
  7.0 2.8 %collective-permute-done.2 = bf16[1,608,128]{2,1,0:T(8,128)(2,1)S(1)} collective-permute-done((bf16[1,608,128]{2,1,0:T(8,128)(2,1)S(1)}, bf16[1,608,128]{2,1,0:T(8,128)(2,1)S(1)}, u32[]{:S(2)}, u32[]{:S(2)}) %collective-permute-start.2) | collective-permute-done | bytes 155680 | tf_op jit(solution)/shard_map/ppermute | solution.py:28
  9.8 1.0 %collective-permute-start.3 = (bf16[1,608,128]{2,1,0:T(8,128)(2,1)S(1)}, bf16[1,608,128]{2,1,0:T(8,128)(2,1)S(1)}, u32[]{:S(2)}, u32[]{:S(2)}) collective-permute-start(bf16[1,608,128]{2,1,0:T(8,128)(2,1)S(1)} %collective-permute-done.2), channel_id=1, source_target_pairs={{0,8},{8,0},{1,9},{9,1},{2,10},{10,2},{3,11},{11,3},{4,12},{12,4},... | collective-permute-start | bytes 466952 | tf_op jit(solution)/shard_map/ppermute | solution.py:28
  10.9 1.0 %collective-permute-done.3 = bf16[1,608,128]{2,1,0:T(8,128)(2,1)S(1)} collective-permute-done((bf16[1,608,128]{2,1,0:T(8,128)(2,1)S(1)}, bf16[1,608,128]{2,1,0:T(8,128)(2,1)S(1)}, u32[]{:S(2)}, u32[]{:S(2)}) %collective-permute-start.3) | collective-permute-done | bytes 155680 | tf_op jit(solution)/shard_map/ppermute | solution.py:28
  11.9 4.0 %collective-permute-done.1 = bf16[2,608,128]{2,1,0:T(8,128)(2,1)S(1)} collective-permute-done((bf16[2,608,128]{2,1,0:T(8,128)(2,1)S(1)}, bf16[2,608,128]{2,1,0:T(8,128)(2,1)S(1)}, u32[]{:S(2)}, u32[]{:S(2)}) %collective-permute-start.1) | collective-permute-done | bytes 311328 | tf_op jit(solution)/shard_map/ppermute | solution.py:373
  15.9 8.1 %collective-permute-done.4 = bf16[2,608,128]{2,1,0:T(8,128)(2,1)S(1)} collective-permute-done((bf16[2,608,128]{2,1,0:T(8,128)(2,1)S(1)}, bf16[2,608,128]{2,1,0:T(8,128)(2,1)S(1)}, u32[]{:S(2)}, u32[]{:S(2)}) %collective-permute-start.4) | collective-permute-done | bytes 311328 | tf_op jit(solution)/shard_map/ppermute | solution.py:373
  24.0 3.3 %collective-permute-done.5 = bf16[2,608,128]{2,1,0:T(8,128)(2,1)S(1)} collective-permute-done((bf16[2,608,128]{2,1,0:T(8,128)(2,1)S(1)}, bf16[2,608,128]{2,1,0:T(8,128)(2,1)S(1)}, u32[]{:S(2)}, u32[]{:S(2)}) %collective-permute-start.5) | collective-permute-done | bytes 311328 | tf_op jit(solution)/shard_map/ppermute | solution.py:373
  27.3 8.1 %collective-permute-done.7 = bf16[2,608,128]{2,1,0:T(8,128)(2,1)S(1)} collective-permute-done((bf16[2,608,128]{2,1,0:T(8,128)(2,1)S(1)}, bf16[2,608,128]{2,1,0:T(8,128)(2,1)S(1)}, u32[]{:S(2)}, u32[]{:S(2)}) %collective-permute-start.7) | collective-permute-done | bytes 311328 | tf_op jit(solution)/shard_map/ppermute | solution.py:373
  35.4 3.3 %collective-permute-done.8 = bf16[2,608,128]{2,1,0:T(8,128)(2,1)S(1)} collective-permute-done((bf16[2,608,128]{2,1,0:T(8,128)(2,1)S(1)}, bf16[2,608,128]{2,1,0:T(8,128)(2,1)S(1)}, u32[]{:S(2)}, u32[]{:S(2)}) %collective-permute-start.8) | collective-permute-done | bytes 311328 | tf_op jit(solution)/shard_map/ppermute | solution.py:373
  39.0 6.2 %collective-permute-done.9 = bf16[1,608,128]{2,1,0:T(8,128)(2,1)S(1)} collective-permute-done((bf16[1,608,128]{2,1,0:T(8,128)(2,1)S(1)}, bf16[1,608,128]{2,1,0:T(8,128)(2,1)S(1)}, u32[]{:S(2)}, u32[]{:S(2)}) %collective-permute-start.9) | collective-permute-done | bytes 155680 | tf_op jit(solution)/shard_map/ppermute | solution.py:373
  46.1 1.0 constant_dynamic-update-slice_fusion.5
  47.2 1.0 %constant_dynamic-update-slice_fusion.4.refs_4_ = bf16[4,608,128]{2,1,0:T(8,128)(2,1)S(1)} fusion(bf16[4,608,128]{2,1,0:T(8,128)(2,1)S(1)} %constant_dynamic-update-slice_fusion.5, bf16[2,608,128]{2,1,0:T(8,128)(2,1)} %copy-done), kind=kLoop, calls=%fused_computation.11 | loop fusion | bytes 622592 | tf_op jit(solution)/shard_map/concatenate | solution.py:387
  48.8 1.3 %collective-permute-start.12 = (bf16[1,608,128]{2,1,0:T(8,128)(2,1)S(1)}, bf16[1,608,128]{2,1,0:T(8,128)(2,1)S(1)}, u32[]{:S(2)}, u32[]{:S(2)}) collective-permute-start(bf16[1,608,128]{2,1,0:T(8,128)(2,1)S(1)} %collective-permute-done.9), channel_id=1, source_target_pairs={{0,128},{128,0},{1,129},{129,1},{2,130},{130,2},{3,131},{131,3},{4... | collective-permute-start | bytes 466952 | tf_op jit(solution)/shard_map/ppermute | solution.py:28
  50.1 11.6 %shard_map.67 = (f32[8,128,128]{2,1,0:T(8,128)S(1)}, s16[1040,128]{1,0:T(8,128)(2,1)S(1)}, s16[1040,128]{1,0:T(8,128)(2,1)S(1)}, s16[1040,128]{1,0:T(8,128)(2,1)...) custom-call(s32[16]{0:T(128)S(1)} %xor_add_fusion.refs_0_, s32[8,32]{1,0:T(8,128)} %refs_1_.1, ...), custom_call_target="tpu_custom_call" | custom-call | flops 10000000000 | bytes 16777216 | tf_op jit(solution)/shard_map/pallas_call | solution.py:226
  62.2 2.6 %collective-permute-start.14 = (s16[1040,128]{1,0:T(8,128)(2,1)S(1)}, s16[1040,128]{1,0:T(8,128)(2,1)S(1)}, u32[]{:S(2)}, u32[]{:S(2)}) collective-permute-start(s16[1040,128]{1,0:T(8,128)(2,1)S(1)} %get-tuple-element.65), channel_id=1, source_target_pairs={{0,2},{1,3},{2,0},{3,1},{4,6},{5,7},{6,4},{7,5},{8,10},{9,11},{10,... | collective-permute-start | bytes 798728 | tf_op jit(solution)/shard_map/ppermute | solution.py:391
  64.8 6.8 %shard_map.69 = (f32[4,128,128]{2,1,0:T(8,128)S(1)}, s16[528,128]{1,0:T(8,128)(2,1)S(1)}, s16[528,128]{1,0:T(8,128)(2,1)S(1)}, s16[528,128]{1,0:T(8,128)(2,1)S(1...) custom-call(s32[16]{0:T(128)S(1)} %xor_add_fusion.refs_0_, s32[16,128]{1,0:T(8,128)S(1)} %get-tuple-element.62.over_ref.refs_1_, ...), custom_call_target="tpu_custom_call" | custom-call | flops 5000000000 | bytes 8388608 | tf_op jit(solution)/shard_map/pallas_call | solution.py:244
  71.7 3.3 %collective-permute-start.18 = (s16[528,128]{1,0:T(8,128)(2,1)S(1)}, s16[528,128]{1,0:T(8,128)(2,1)S(1)}, u32[]{:S(2)}, u32[]{:S(2)}) collective-permute-start(s16[528,128]{1,0:T(8,128)(2,1)S(1)} %get-tuple-element.73), channel_id=1, source_target_pairs={{0,1},{1,2},{2,3},{3,0},{4,5},{5,6},{6,7},{7,4},{8,9},{9,10},{10,1... | collective-permute-start | bytes 405512 | tf_op jit(solution)/shard_map/ppermute | solution.py:391
  75.2 1.7 %collective-permute-start.20 = (s16[528,128]{1,0:T(8,128)(2,1)S(1)}, s16[528,128]{1,0:T(8,128)(2,1)S(1)}, u32[]{:S(2)}, u32[]{:S(2)}) collective-permute-start(s16[528,128]{1,0:T(8,128)(2,1)S(1)} %get-tuple-element.75), channel_id=1, source_target_pairs={{0,3},{1,0},{2,1},{3,2},{4,7},{5,4},{6,5},{7,6},{8,11},{9,8},{10,9... | collective-permute-start | bytes 405512 | tf_op jit(solution)/shard_map/ppermute | solution.py:391
  76.9 4.6 %shard_map.71 = (f32[4,128,128]{2,1,0:T(8,128)S(1)}, s16[528,128]{1,0:T(8,128)(2,1)S(1)}, s16[528,128]{1,0:T(8,128)(2,1)S(1)}, s16[528,128]{1,0:T(8,128)(2,1)S(1)}) custom-call(s32[16,128]{1,0:T(8,128)S(1)} %get-tuple-element.71.over_ref, bf16[1024,4096]{1,0:T(8,128)(2,1)} %get-tuple-element.68.refs_2_.ints_ref, bf16[512,4096]{1,0:T(8,128)(2,1)S(1)} %get-tuple-element.77.amps), custom_call_target="tpu_custom_call" | custom-call | flops 5000000000 | bytes 8388608 | tf_op jit(solution)/shard_map/pallas_call | solution.py:259
  81.5 1.6 %collective-permute-start.21 = (s16[528,128]{1,0:T(8,128)(2,1)S(1)}, s16[528,128]{1,0:T(8,128)(2,1)S(1)}, u32[]{:S(2)}, u32[]{:S(2)}) collective-permute-start(s16[528,128]{1,0:T(8,128)(2,1)S(1)} %get-tuple-element.79), channel_id=1, source_target_pairs={{0,1},{1,2},{2,3},{3,0},{4,5},{5,6},{6,7},{7,4},{8,9},{9,10},{10,1... | collective-permute-start | bytes 405512 | tf_op jit(solution)/shard_map/ppermute | solution.py:391
  83.1 2.1 %collective-permute-start.22 = (s16[528,128]{1,0:T(8,128)(2,1)S(1)}, s16[528,128]{1,0:T(8,128)(2,1)S(1)}, u32[]{:S(2)}, u32[]{:S(2)}) collective-permute-start(s16[528,128]{1,0:T(8,128)(2,1)S(1)} %get-tuple-element.80), channel_id=1, source_target_pairs={{0,2},{1,3},{2,0},{3,1},{4,6},{5,7},{6,4},{7,5},{8,10},{9,11},{10,... | collective-permute-start | bytes 405512 | tf_op jit(solution)/shard_map/ppermute | solution.py:391
  85.2 1.5 %shard_map.68 = (f32[8,128,128]{2,1,0:T(8,128)S(1)}, s16[528,128]{1,0:T(8,128)(2,1)S(1)}, s16[528,128]{1,0:T(8,128)(2,1)S(1)}) custom-call(s32[16,128]{1,0:T(8,128)S(1)} %get-tuple-element.62.over_ref.refs_1_, f32[8,128,128]{2,1,0:T(8,128)S(1)} %get-tuple-element.63.own_ref, s16[1040,128]{1,0:T(8,128)(2,1)S(1)} %collective-permute-done.13.a_ref, ...), custom_call_target="tpu_custom_call" | custom-call | tf_op jit(solution)/shard_map/pallas_call | solution.py:292
  86.7 0.9 shard_map.70
  87.6 0.8 collective-permute-start.24
  88.4 1.9 %collective-permute-done.22.b_ref = s16[528,128]{1,0:T(8,128)(2,1)S(1)} collective-permute-done((s16[528,128]{1,0:T(8,128)(2,1)S(1)}, s16[528,128]{1,0:T(8,128)(2,1)S(1)}, u32[]{:S(2)}, u32[]{:S(2)}) %collective-permute-start.22) | collective-permute-done | bytes 135200 | tf_op jit(solution)/shard_map/ppermute | solution.py:391
  90.3 1.4 %collective-permute-done.23.c_ref = s16[528,128]{1,0:T(8,128)(2,1)S(1)} collective-permute-done((s16[528,128]{1,0:T(8,128)(2,1)S(1)}, s16[528,128]{1,0:T(8,128)(2,1)S(1)}, u32[]{:S(2)}, u32[]{:S(2)}) %collective-permute-start.23) | collective-permute-done | bytes 135200 | tf_op jit(solution)/shard_map/ppermute | solution.py:391
  91.8 0.9 shard_map.72
  92.7 0.8 collective-permute-start.25
  93.5 4.3 %collective-permute-done.25.got_b = s16[528,128]{1,0:T(8,128)(2,1)S(1)} collective-permute-done((s16[528,128]{1,0:T(8,128)(2,1)S(1)}, s16[528,128]{1,0:T(8,128)(2,1)S(1)}, u32[]{:S(2)}, u32[]{:S(2)}) %collective-permute-start.25) | collective-permute-done | bytes 135200 | tf_op jit(solution)/shard_map/ppermute | solution.py:28
  97.8 0.9 shard_map.75
  (53 shorter events, 3.7 us)
Async XLA Ops:
  1.8 3.2 %collective-permute-start = (bf16[1,608,128]{2,1,0:T(8,128)(2,1)S(1)}, bf16[1,608,128]{2,1,0:T(8,128)(2,1)S(1)}, u32[]{:S(2)}, u32[]{:S(2)}) collective-permute-start(bf16[1,608,128]{2,1,0:T(8,128)(2,1)S(1)} %shard_map.66), channel_id=1, source_target_pairs={{0,8},{8,0},{1,9},{9,1},{2,10},{10,2},{3,11},{11,3},{4,12},{12,4},... | collective-permute-start | bytes 466952 | tf_op jit(solution)/shard_map/ppermute | solution.py:28
  1.9 7.9 %collective-permute-start.2 = (bf16[1,608,128]{2,1,0:T(8,128)(2,1)S(1)}, bf16[1,608,128]{2,1,0:T(8,128)(2,1)S(1)}, u32[]{:S(2)}, u32[]{:S(2)}) collective-permute-start(bf16[1,608,128]{2,1,0:T(8,128)(2,1)S(1)} %shard_map.66), channel_id=1, source_target_pairs={{0,128},{128,0},{1,129},{129,1},{2,130},{130,2},{3,131},{131,3},{4... | collective-permute-start | bytes 466952 | tf_op jit(solution)/shard_map/ppermute | solution.py:28
  5.0 10.8 %collective-permute-start.1 = (bf16[2,608,128]{2,1,0:T(8,128)(2,1)S(1)}, bf16[2,608,128]{2,1,0:T(8,128)(2,1)S(1)}, u32[]{:S(2)}, u32[]{:S(2)}) collective-permute-start(bf16[2,608,128]{2,1,0:T(8,128)(2,1)S(1)} %pad_maximum_fusion.refs_3_), channel_id=1, source_target_pairs={{0,16},{16,32},{32,48},{48,64},{64,80},{80,96},{96,112},{112,0},{8... | collective-permute-start | bytes 933896 | tf_op jit(solution)/shard_map/ppermute | solution.py:373
  9.8 2.0 %collective-permute-start.3 = (bf16[1,608,128]{2,1,0:T(8,128)(2,1)S(1)}, bf16[1,608,128]{2,1,0:T(8,128)(2,1)S(1)}, u32[]{:S(2)}, u32[]{:S(2)}) collective-permute-start(bf16[1,608,128]{2,1,0:T(8,128)(2,1)S(1)} %collective-permute-done.2), channel_id=1, source_target_pairs={{0,8},{8,0},{1,9},{9,1},{2,10},{10,2},{3,11},{11,3},{4,12},{12,4},... | collective-permute-start | bytes 466952 | tf_op jit(solution)/shard_map/ppermute | solution.py:28
  15.9 8.1 %collective-permute-start.4 = (bf16[2,608,128]{2,1,0:T(8,128)(2,1)S(1)}, bf16[2,608,128]{2,1,0:T(8,128)(2,1)S(1)}, u32[]{:S(2)}, u32[]{:S(2)}) collective-permute-start(bf16[2,608,128]{2,1,0:T(8,128)(2,1)S(1)} %collective-permute-done.1), channel_id=1, source_target_pairs={{0,16},{16,32},{32,48},{48,64},{64,80},{80,96},{96,112},{112,0},{8... | collective-permute-start | bytes 933896 | tf_op jit(solution)/shard_map/ppermute | solution.py:373
  15.9 11.4 %collective-permute-start.5 = (bf16[2,608,128]{2,1,0:T(8,128)(2,1)S(1)}, bf16[2,608,128]{2,1,0:T(8,128)(2,1)S(1)}, u32[]{:S(2)}, u32[]{:S(2)}) collective-permute-start(bf16[2,608,128]{2,1,0:T(8,128)(2,1)S(1)} %pad_maximum_fusion.1.refs_3_), channel_id=1, source_target_pairs={{0,16},{16,32},{32,48},{48,64},{64,80},{80,96},{96,112},{112,0},{8... | collective-permute-start | bytes 933896 | tf_op jit(solution)/shard_map/ppermute | solution.py:373
  27.3 18.1 %copy-start.1 = (bf16[2,608,128]{2,1,0:T(8,128)(2,1)}, bf16[2,608,128]{2,1,0:T(8,128)(2,1)S(1)}, u32[]{:S(2)}) copy-start(bf16[2,608,128]{2,1,0:T(8,128)(2,1)S(1)} %collective-permute-done.5) | copy-start | bytes 933892
  27.3 8.1 %collective-permute-start.7 = (bf16[2,608,128]{2,1,0:T(8,128)(2,1)S(1)}, bf16[2,608,128]{2,1,0:T(8,128)(2,1)S(1)}, u32[]{:S(2)}, u32[]{:S(2)}) collective-permute-start(bf16[2,608,128]{2,1,0:T(8,128)(2,1)S(1)} %collective-permute-done.4), channel_id=1, source_target_pairs={{0,16},{16,32},{32,48},{48,64},{64,80},{80,96},{96,112},{112,0},{8... | collective-permute-start | bytes 933896 | tf_op jit(solution)/shard_map/ppermute | solution.py:373
  27.3 11.4 %collective-permute-start.8 = (bf16[2,608,128]{2,1,0:T(8,128)(2,1)S(1)}, bf16[2,608,128]{2,1,0:T(8,128)(2,1)S(1)}, u32[]{:S(2)}, u32[]{:S(2)}) collective-permute-start(bf16[2,608,128]{2,1,0:T(8,128)(2,1)S(1)} %collective-permute-done.5), channel_id=1, source_target_pairs={{0,16},{16,32},{32,48},{48,64},{64,80},{80,96},{96,112},{112,0},{8... | collective-permute-start | bytes 933896 | tf_op jit(solution)/shard_map/ppermute | solution.py:373
  38.7 6.6 %copy-start = (bf16[2,608,128]{2,1,0:T(8,128)(2,1)}, bf16[2,608,128]{2,1,0:T(8,128)(2,1)S(1)}, u32[]{:S(2)}) copy-start(bf16[2,608,128]{2,1,0:T(8,128)(2,1)S(1)} %collective-permute-done.8) | copy-start | bytes 933892
  38.8 6.5 %collective-permute-start.9 = (bf16[1,608,128]{2,1,0:T(8,128)(2,1)S(1)}, bf16[1,608,128]{2,1,0:T(8,128)(2,1)S(1)}, u32[]{:S(2)}, u32[]{:S(2)}) collective-permute-start(bf16[1,608,128]{2,1,0:T(8,128)(2,1)S(1)} %slice.3), channel_id=1, source_target_pairs={{0,16},{16,32},{32,48},{48,64},{64,80},{80,96},{96,112},{112,0},{8... | collective-permute-start | bytes 466952 | tf_op jit(solution)/shard_map/ppermute | solution.py:373
  38.9 11.2 %collective-permute-start.6 = (bf16[4,608,128]{2,1,0:T(8,128)(2,1)S(1)}, bf16[4,608,128]{2,1,0:T(8,128)(2,1)S(1)}, u32[]{:S(2)}, u32[]{:S(2)}) collective-permute-start(bf16[4,608,128]{2,1,0:T(8,128)(2,1)S(1)} %constant_dynamic-update-slice_fusion.refs_4_), channel_id=1, source_target_pairs={{0,8},{8,0},{1,9},{9,1},{2,10},{10,2},{3,11},{11,3},{4,12},{12,4},... | collective-permute-start | bytes 1867784 | tf_op jit(solution)/shard_map/ppermute | solution.py:28
  45.3 4.8 %collective-permute-start.10 = (bf16[3,608,128]{2,1,0:T(8,128)(2,1)S(1)}, bf16[3,608,128]{2,1,0:T(8,128)(2,1)S(1)}, u32[]{:S(2)}, u32[]{:S(2)}) collective-permute-start(bf16[3,608,128]{2,1,0:T(8,128)(2,1)S(1)} %constant_dynamic-update-slice_fusion.2.refs_6_), channel_id=1, source_target_pairs={{0,8},{8,0},{1,9},{9,1},{2,10},{10,2},{3,11},{11,3},{4,12},{12,4},... | collective-permute-start | bytes 1400840 | tf_op jit(solution)/shard_map/ppermute | solution.py:28
  47.1 14.6 %collective-permute-start.11 = (bf16[2,608,128]{2,1,0:T(8,128)(2,1)}, bf16[2,608,128]{2,1,0:T(8,128)(2,1)S(1)}, u32[]{:S(2)}, u32[]{:S(2)}) collective-permute-start(bf16[2,608,128]{2,1,0:T(8,128)(2,1)} %copy-done), channel_id=1, source_target_pairs={{0,16},{16,32},{32,48},{48,64},{64,80},{80,96},{96,112},{112,0},{8... | collective-permute-start | bytes 933896 | tf_op jit(solution)/shard_map/ppermute | solution.py:373
  48.2 16.6 %collective-permute-start.16 = (bf16[4,608,128]{2,1,0:T(8,128)(2,1)S(1)}, bf16[4,608,128]{2,1,0:T(8,128)(2,1)S(1)}, u32[]{:S(2)}, u32[]{:S(2)}) collective-permute-start(bf16[4,608,128]{2,1,0:T(8,128)(2,1)S(1)} %constant_dynamic-update-slice_fusion.4.refs_4_), channel_id=1, source_target_pairs={{0,8},{8,0},{1,9},{9,1},{2,10},{10,2},{3,11},{11,3},{4,12},{12,4},... | collective-permute-start | bytes 1867784 | tf_op jit(solution)/shard_map/ppermute | solution.py:28
  48.8 12.9 %collective-permute-start.12 = (bf16[1,608,128]{2,1,0:T(8,128)(2,1)S(1)}, bf16[1,608,128]{2,1,0:T(8,128)(2,1)S(1)}, u32[]{:S(2)}, u32[]{:S(2)}) collective-permute-start(bf16[1,608,128]{2,1,0:T(8,128)(2,1)S(1)} %collective-permute-done.9), channel_id=1, source_target_pairs={{0,128},{128,0},{1,129},{129,1},{2,130},{130,2},{3,131},{131,3},{4... | collective-permute-start | bytes 466952 | tf_op jit(solution)/shard_map/ppermute | solution.py:28
  61.8 3.0 %collective-permute-start.17 = (bf16[3,608,128]{2,1,0:T(8,128)(2,1)S(1)}, bf16[3,608,128]{2,1,0:T(8,128)(2,1)S(1)}, u32[]{:S(2)}, u32[]{:S(2)}) collective-permute-start(bf16[3,608,128]{2,1,0:T(8,128)(2,1)S(1)} %constant_dynamic-update-slice_fusion.6.refs_6_), channel_id=1, source_target_pairs={{0,8},{8,0},{1,9},{9,1},{2,10},{10,2},{3,11},{11,3},{4,12},{12,4},... | collective-permute-start | bytes 1400840 | tf_op jit(solution)/shard_map/ppermute | solution.py:28
  61.9 13.3 %collective-permute-start.13 = (s16[1040,128]{1,0:T(8,128)(2,1)S(1)}, s16[1040,128]{1,0:T(8,128)(2,1)S(1)}, u32[]{:S(2)}, u32[]{:S(2)}) collective-permute-start(s16[1040,128]{1,0:T(8,128)(2,1)S(1)} %get-tuple-element.64), channel_id=1, source_target_pairs={{0,1},{1,2},{2,3},{3,0},{4,5},{5,6},{6,7},{7,4},{8,9},{9,10},{10,1... | collective-permute-start | bytes 798728 | tf_op jit(solution)/shard_map/ppermute | solution.py:391
  62.2 19.3 %collective-permute-start.14 = (s16[1040,128]{1,0:T(8,128)(2,1)S(1)}, s16[1040,128]{1,0:T(8,128)(2,1)S(1)}, u32[]{:S(2)}, u32[]{:S(2)}) collective-permute-start(s16[1040,128]{1,0:T(8,128)(2,1)S(1)} %get-tuple-element.65), channel_id=1, source_target_pairs={{0,2},{1,3},{2,0},{3,1},{4,6},{5,7},{6,4},{7,5},{8,10},{9,11},{10,... | collective-permute-start | bytes 798728 | tf_op jit(solution)/shard_map/ppermute | solution.py:391
  64.8 18.3 %collective-permute-start.15 = (s16[1040,128]{1,0:T(8,128)(2,1)S(1)}, s16[1040,128]{1,0:T(8,128)(2,1)S(1)}, u32[]{:S(2)}, u32[]{:S(2)}) collective-permute-start(s16[1040,128]{1,0:T(8,128)(2,1)S(1)} %get-tuple-element.66), channel_id=1, source_target_pairs={{0,3},{1,0},{2,1},{3,2},{4,7},{5,4},{6,5},{7,6},{8,11},{9,8},{10,9... | collective-permute-start | bytes 798728 | tf_op jit(solution)/shard_map/ppermute | solution.py:391
  71.7 13.6 %collective-permute-start.18 = (s16[528,128]{1,0:T(8,128)(2,1)S(1)}, s16[528,128]{1,0:T(8,128)(2,1)S(1)}, u32[]{:S(2)}, u32[]{:S(2)}) collective-permute-start(s16[528,128]{1,0:T(8,128)(2,1)S(1)} %get-tuple-element.73), channel_id=1, source_target_pairs={{0,1},{1,2},{2,3},{3,0},{4,5},{5,6},{6,7},{7,4},{8,9},{9,10},{10,1... | collective-permute-start | bytes 405512 | tf_op jit(solution)/shard_map/ppermute | solution.py:391
  75.0 11.7 %collective-permute-start.19 = (s16[528,128]{1,0:T(8,128)(2,1)S(1)}, s16[528,128]{1,0:T(8,128)(2,1)S(1)}, u32[]{:S(2)}, u32[]{:S(2)}) collective-permute-start(s16[528,128]{1,0:T(8,128)(2,1)S(1)} %get-tuple-element.74), channel_id=1, source_target_pairs={{0,2},{1,3},{2,0},{3,1},{4,6},{5,7},{6,4},{7,5},{8,10},{9,11},{10,... | collective-permute-start | bytes 405512 | tf_op jit(solution)/shard_map/ppermute | solution.py:391
  75.2 11.5 %collective-permute-start.20 = (s16[528,128]{1,0:T(8,128)(2,1)S(1)}, s16[528,128]{1,0:T(8,128)(2,1)S(1)}, u32[]{:S(2)}, u32[]{:S(2)}) collective-permute-start(s16[528,128]{1,0:T(8,128)(2,1)S(1)} %get-tuple-element.75), channel_id=1, source_target_pairs={{0,3},{1,0},{2,1},{3,2},{4,7},{5,4},{6,5},{7,6},{8,11},{9,8},{10,9... | collective-permute-start | bytes 405512 | tf_op jit(solution)/shard_map/ppermute | solution.py:391
  76.8 22.5 %copy-start.2 = (s32[32,32]{1,0:T(8,128)S(1)}, s32[32,32]{1,0:T(8,128)}, u32[]{:S(2)}) copy-start(s32[32,32]{1,0:T(8,128)} %mask_ref.1) | copy-start | bytes 12292
  76.9 22.5 %copy-start.3 = (s32[8,32]{1,0:T(8,128)S(1)}, s32[8,32]{1,0:T(8,128)}, u32[]{:S(2)}) copy-start(s32[8,32]{1,0:T(8,128)} %refs_1_.1) | copy-start | bytes 3076
  81.5 7.0 %collective-permute-start.21 = (s16[528,128]{1,0:T(8,128)(2,1)S(1)}, s16[528,128]{1,0:T(8,128)(2,1)S(1)}, u32[]{:S(2)}, u32[]{:S(2)}) collective-permute-start(s16[528,128]{1,0:T(8,128)(2,1)S(1)} %get-tuple-element.79), channel_id=1, source_target_pairs={{0,1},{1,2},{2,3},{3,0},{4,5},{5,6},{6,7},{7,4},{8,9},{9,10},{10,1... | collective-permute-start | bytes 405512 | tf_op jit(solution)/shard_map/ppermute | solution.py:391
  83.1 7.2 %collective-permute-start.22 = (s16[528,128]{1,0:T(8,128)(2,1)S(1)}, s16[528,128]{1,0:T(8,128)(2,1)S(1)}, u32[]{:S(2)}, u32[]{:S(2)}) collective-permute-start(s16[528,128]{1,0:T(8,128)(2,1)S(1)} %get-tuple-element.80), channel_id=1, source_target_pairs={{0,2},{1,3},{2,0},{3,1},{4,6},{5,7},{6,4},{7,5},{8,10},{9,11},{10,... | collective-permute-start | bytes 405512 | tf_op jit(solution)/shard_map/ppermute | solution.py:391
  85.2 6.5 %collective-permute-start.23 = (s16[528,128]{1,0:T(8,128)(2,1)S(1)}, s16[528,128]{1,0:T(8,128)(2,1)S(1)}, u32[]{:S(2)}, u32[]{:S(2)}) collective-permute-start(s16[528,128]{1,0:T(8,128)(2,1)S(1)} %get-tuple-element.81), channel_id=1, source_target_pairs={{0,3},{1,0},{2,1},{3,2},{4,7},{5,4},{6,5},{7,6},{8,11},{9,8},{10,9... | collective-permute-start | bytes 405512 | tf_op jit(solution)/shard_map/ppermute | solution.py:391
  87.6 5.9 %collective-permute-start.24 = (s16[528,128]{1,0:T(8,128)(2,1)S(1)}, s16[528,128]{1,0:T(8,128)(2,1)S(1)}, u32[]{:S(2)}, u32[]{:S(2)}) collective-permute-start(s16[528,128]{1,0:T(8,128)(2,1)S(1)} %shard_map.74), channel_id=1, source_target_pairs={{0,4},{4,0},{1,5},{5,1},{2,6},{6,2},{3,7},{7,3},{8,12},{12,8},{9,1... | collective-permute-start | bytes 405512 | tf_op jit(solution)/shard_map/ppermute | solution.py:28
  92.7 5.1 %collective-permute-start.25 = (s16[528,128]{1,0:T(8,128)(2,1)S(1)}, s16[528,128]{1,0:T(8,128)(2,1)S(1)}, u32[]{:S(2)}, u32[]{:S(2)}) collective-permute-start(s16[528,128]{1,0:T(8,128)(2,1)S(1)} %shard_map.73.sent_ref), channel_id=1, source_target_pairs={{0,4},{4,0},{1,5},{5,1},{2,6},{6,2},{3,7},{7,3},{8,12},{12,8},{9,1... | collective-permute-start | bytes 405512 | tf_op jit(solution)/shard_map/ppermute | solution.py:28
  99.6 0.7 copy-start.4

commit v7 on v6

--- a/solution.py
+++ b/solution.py
@@ -368,32 +368,21 @@
     rows = (((far >> 1) - y) & 3) * 4 + (far & 1) * 2 + (core ^ jnp.asarray(OTHER, I32))
 
     own = pack(amplitudes, amp_mask)
-
-    def hop(block):
-        return lax.ppermute(block, ("z", "core"), RING)
-
-    def with_sibling(message):
-        return jnp.concatenate([message, swap(message, "core")], axis=0)
-
-    near_chain = [with_sibling(own)]
-    first, far_pair = lax.optimization_barrier((hop(near_chain[0]), with_sibling(swap(own, "xh"))))
-    second, far_first = lax.optimization_barrier((hop(first), hop(far_pair)))
-    third, far_second = lax.optimization_barrier((hop(second), hop(far_first)))
-    near_chain += [first, second, third]
-    opposite = hop(third[:1])
-    far_chain = [far_pair, far_first, far_second, hop(far_second)]
-    blocks = [near_chain, far_chain]
-    opposite_across = swap(opposite, "xh")
+    across = swap(own, "xh")
+    blocks = [[jnp.concatenate([message, swap(message, "core")], axis=0)] for message in (own, across)]
+    for hop in range(1, 5):
+        for chain in blocks:
+            chain.append(lax.ppermute(chain[-1] if hop < 4 else chain[-1][:1], ("z", "core"), RING))
     two = [jnp.concatenate(chain[1:3], axis=0) for chain in blocks]
-    rest = jnp.concatenate([blocks[0][3], opposite], axis=0)
+    rest = jnp.concatenate(blocks[0][3:], axis=0)
 
     def spread(parts):
         return [lax.ppermute(part, "y", [(i, (i + d + 1) % 4) for i in range(4)]) for d, part in enumerate(parts)]
 
     held = [blocks[0][0], two[0], swap(two[0], "core"), rest, swap(rest, "core")]
     own_part, *parts, over, kept_ints = first_chunk(rows, int_mask, integrals, held)
-    over, *late = lax.optimization_barrier((over, blocks[1][3], opposite_across))
-    rest = jnp.concatenate(late, axis=0)
+    over, late = lax.optimization_barrier((over, blocks[1][4]))
+    rest = jnp.concatenate([blocks[1][3], late], axis=0)
     held = [blocks[1][0], two[1], swap(two[1], "core"), rest, swap(rest, "core")]
     first_sum, *first_coded = add(over, own_part, spread(parts), 2)
 

time: 101 us -> 93.6 us (0.927)
  waiting for transfers between devices: 44.5 us -> 36 us
  starting transfers between devices: 21.9 us -> 25 us
  local copies, waits for them, and re-layouts: 2.9 us -> 0.97 us
    ppermute x7 -> x8, waiting for transfers between devices: 33 us -> 23.8 us  [local(): lax.ppermute(chain[-1] if hop < 4 else chain[-1][:1], ('z', 'core'), RING)]
    ppermute x10 -> x9, starting transfers between devices: 7.93 us -> 10.5 us  [swap(): return lax.ppermute(x, axis, [(0, 1), (1, 0)])]
    ppermute x10 -> x9, waiting for transfers between devices: 8.13 us -> 9.61 us  [swap(): return lax.ppermute(x, axis, [(0, 1), (1, 0)])]
    ppermute x7 -> x8, starting transfers between devices: 2.17 us -> 2.63 us  [local(): lax.ppermute(chain[-1] if hop < 4 else chain[-1][:1], ('z', 'core'), RING)]
  transfers between devices with their start and end apart: 26 -> 26, of which waited for: 11 -> 12; matrix products, arithmetic and copies ran while one was open for 3% -> 1% of each run, Pallas kernels for 26% -> 28%
where the time goes in v7:
time: 93.6 us; the launch traced here: 93 us
  waiting for transfers between devices  36 us (38%)
  Pallas kernels  29 us (31%)
  starting transfers between devices  25 us (27%)
  local copies, waits for them, and re-layouts  0.97 us (1%)
    ppermute x8, waiting for transfers between devices, local(): lax.ppermute(chain[-1] if hop < 4 else chain[-1][:1], ('z', 'core'), RING)  23.8 us
    ppermute x9, starting transfers between devices, spread(): lax.ppermute(part, 'y', [(i, (i + d + 1) % 4) for i in range(4)])  11.8 us
    pallas_call x1, Pallas kernels, first_chunk(): pl.pallas_call(lambda *refs: first_kernel(sizes, *refs), in_specs=[SMEM,...  11.6 us
    ppermute x9, starting transfers between devices, swap(): return lax.ppermute(x, axis, [(0, 1), (1, 0)])  10.5 us
    ppermute x9, waiting for transfers between devices, swap(): return lax.ppermute(x, axis, [(0, 1), (1, 0)])  9.61 us
    pallas_call x1, Pallas kernels, second_chunk(): pl.pallas_call(lambda *refs: second_kernel(sizes, *refs), in_specs=[SMEM,...  6.84 us
    pallas_call x1, Pallas kernels, second_half(): pl.pallas_call(third_kernel, in_specs=[VMEM, ANYWHERE, VMEM], out_specs=[...  4.58 us
    pallas_call x3, Pallas kernels, add(): pl.pallas_call(add_kernel, in_specs=[VMEM] * 5, out_specs=[VMEM] * (1 + p...  3.23 us
  transfers between devices with their start and end apart: 26, of which 12 were waited for; matrix products, arithmetic and copies ran while one was open for 1% of the time, Pallas kernels for 28%

profile of v7, /device:TPU:24, one launch (start us, length us, event | category | flops | bytes accessed | tf_op | source)
XLA Modules:
  0.0 93.0 jit_solution(587425484536578898)
XLA Ops:
  0.0 1.8 %shard_map.66 = bf16[1,608,128]{2,1,0:T(8,128)(2,1)S(1)} custom-call(bf16[32,4096]{1,0:T(8,128)(2,1)} %amps_ref.1, s32[32,32]{1,0:T(8,128)} %mask_ref.1), custom_call_target="tpu_custom_call" | custom-call | tf_op jit(solution)/shard_map/pallas_call | solution.py:68
  1.9 1.4 %collective-permute-done = bf16[1,608,128]{2,1,0:T(8,128)(2,1)S(1)} collective-permute-done((bf16[1,608,128]{2,1,0:T(8,128)(2,1)S(1)}, bf16[1,608,128]{2,1,0:T(8,128)(2,1)S(1)}, u32[]{:S(2)}, u32[]{:S(2)}) %collective-permute-start) | collective-permute-done | bytes 155680 | tf_op jit(solution)/shard_map/ppermute | solution.py:28
  3.3 2.0 %collective-permute-start.1 = (bf16[2,608,128]{2,1,0:T(8,128)(2,1)S(1)}, bf16[2,608,128]{2,1,0:T(8,128)(2,1)S(1)}, u32[]{:S(2)}, u32[]{:S(2)}) collective-permute-start(bf16[2,608,128]{2,1,0:T(8,128)(2,1)S(1)} %pad_maximum_fusion.refs_3_), channel_id=1, source_target_pairs={{0,16},{16,32},{32,48},{48,64},{64,80},{80,96},{96,112},{112,0},{8... | collective-permute-start | bytes 933896 | tf_op jit(solution)/shard_map/ppermute | solution.py:375
  5.3 3.0 %collective-permute-start.7 = (bf16[1,608,128]{2,1,0:T(8,128)(2,1)S(1)}, bf16[1,608,128]{2,1,0:T(8,128)(2,1)S(1)}, u32[]{:S(2)}, u32[]{:S(2)}) collective-permute-start(bf16[1,608,128]{2,1,0:T(8,128)(2,1)S(1)} %shard_map.66), channel_id=1, source_target_pairs={{0,128},{128,0},{1,129},{129,1},{2,130},{130,2},{3,131},{131,3},{4... | collective-permute-start | bytes 466952 | tf_op jit(solution)/shard_map/ppermute | solution.py:28
  8.3 3.7 %collective-permute-done.7 = bf16[1,608,128]{2,1,0:T(8,128)(2,1)S(1)} collective-permute-done((bf16[1,608,128]{2,1,0:T(8,128)(2,1)S(1)}, bf16[1,608,128]{2,1,0:T(8,128)(2,1)S(1)}, u32[]{:S(2)}, u32[]{:S(2)}) %collective-permute-start.7) | collective-permute-done | bytes 155680 | tf_op jit(solution)/shard_map/ppermute | solution.py:28
  12.0 2.7 %collective-permute-start.8 = (bf16[1,608,128]{2,1,0:T(8,128)(2,1)S(1)}, bf16[1,608,128]{2,1,0:T(8,128)(2,1)S(1)}, u32[]{:S(2)}, u32[]{:S(2)}) collective-permute-start(bf16[1,608,128]{2,1,0:T(8,128)(2,1)S(1)} %collective-permute-done.7), channel_id=1, source_target_pairs={{0,8},{8,0},{1,9},{9,1},{2,10},{10,2},{3,11},{11,3},{4,12},{12,4},... | collective-permute-start | bytes 466952 | tf_op jit(solution)/shard_map/ppermute | solution.py:28
  14.7 1.0 %collective-permute-done.8 = bf16[1,608,128]{2,1,0:T(8,128)(2,1)S(1)} collective-permute-done((bf16[1,608,128]{2,1,0:T(8,128)(2,1)S(1)}, bf16[1,608,128]{2,1,0:T(8,128)(2,1)S(1)}, u32[]{:S(2)}, u32[]{:S(2)}) %collective-permute-start.8) | collective-permute-done | bytes 155680 | tf_op jit(solution)/shard_map/ppermute | solution.py:28
  16.0 6.8 %collective-permute-done.2 = bf16[2,608,128]{2,1,0:T(8,128)(2,1)S(1)} collective-permute-done((bf16[2,608,128]{2,1,0:T(8,128)(2,1)S(1)}, bf16[2,608,128]{2,1,0:T(8,128)(2,1)S(1)}, u32[]{:S(2)}, u32[]{:S(2)}) %collective-permute-start.2) | collective-permute-done | bytes 311328 | tf_op jit(solution)/shard_map/ppermute | solution.py:375
  22.8 3.3 %collective-permute-done.9 = bf16[2,608,128]{2,1,0:T(8,128)(2,1)S(1)} collective-permute-done((bf16[2,608,128]{2,1,0:T(8,128)(2,1)S(1)}, bf16[2,608,128]{2,1,0:T(8,128)(2,1)S(1)}, u32[]{:S(2)}, u32[]{:S(2)}) %collective-permute-start.9) | collective-permute-done | bytes 311328 | tf_op jit(solution)/shard_map/ppermute | solution.py:375
  26.2 4.7 %collective-permute-done.4 = bf16[2,608,128]{2,1,0:T(8,128)(2,1)S(1)} collective-permute-done((bf16[2,608,128]{2,1,0:T(8,128)(2,1)S(1)}, bf16[2,608,128]{2,1,0:T(8,128)(2,1)S(1)}, u32[]{:S(2)}, u32[]{:S(2)}) %collective-permute-start.4) | collective-permute-done | bytes 311328 | tf_op jit(solution)/shard_map/ppermute | solution.py:375
  31.1 0.9 collective-permute-start.3
  31.9 2.3 %collective-permute-done.10 = bf16[2,608,128]{2,1,0:T(8,128)(2,1)S(1)} collective-permute-done((bf16[2,608,128]{2,1,0:T(8,128)(2,1)S(1)}, bf16[2,608,128]{2,1,0:T(8,128)(2,1)S(1)}, u32[]{:S(2)}, u32[]{:S(2)}) %collective-permute-start.10) | collective-permute-done | bytes 311328 | tf_op jit(solution)/shard_map/ppermute | solution.py:375
  34.3 3.2 %collective-permute-done.5 = bf16[1,608,128]{2,1,0:T(8,128)(2,1)S(1)} collective-permute-done((bf16[1,608,128]{2,1,0:T(8,128)(2,1)S(1)}, bf16[1,608,128]{2,1,0:T(8,128)(2,1)S(1)}, u32[]{:S(2)}, u32[]{:S(2)}) %collective-permute-start.5) | collective-permute-done | bytes 155680 | tf_op jit(solution)/shard_map/ppermute | solution.py:375
  38.9 3.4 %collective-permute-done.11 = bf16[2,608,128]{2,1,0:T(8,128)(2,1)S(1)} collective-permute-done((bf16[2,608,128]{2,1,0:T(8,128)(2,1)S(1)}, bf16[2,608,128]{2,1,0:T(8,128)(2,1)S(1)}, u32[]{:S(2)}, u32[]{:S(2)}) %collective-permute-start.11) | collective-permute-done | bytes 311328 | tf_op jit(solution)/shard_map/ppermute | solution.py:375
  42.7 11.6 %shard_map.67 = (f32[8,128,128]{2,1,0:T(8,128)S(1)}, s16[1040,128]{1,0:T(8,128)(2,1)S(1)}, s16[1040,128]{1,0:T(8,128)(2,1)S(1)}, s16[1040,128]{1,0:T(8,128)(2,1)...) custom-call(s32[16]{0:T(128)S(1)} %xor_add_fusion.refs_0_, s32[8,32]{1,0:T(8,128)} %refs_1_.1, ...), custom_call_target="tpu_custom_call" | custom-call | flops 10000000000 | bytes 16777216 | tf_op jit(solution)/shard_map/pallas_call | solution.py:226
  54.8 2.6 %collective-permute-start.14 = (s16[1040,128]{1,0:T(8,128)(2,1)S(1)}, s16[1040,128]{1,0:T(8,128)(2,1)S(1)}, u32[]{:S(2)}, u32[]{:S(2)}) collective-permute-start(s16[1040,128]{1,0:T(8,128)(2,1)S(1)} %get-tuple-element.52), channel_id=1, source_target_pairs={{0,2},{1,3},{2,0},{3,1},{4,6},{5,7},{6,4},{7,5},{8,10},{9,11},{10,... | collective-permute-start | bytes 798728 | tf_op jit(solution)/shard_map/ppermute | solution.py:380
  57.3 6.8 %shard_map.69 = (f32[4,128,128]{2,1,0:T(8,128)S(1)}, s16[528,128]{1,0:T(8,128)(2,1)S(1)}, s16[528,128]{1,0:T(8,128)(2,1)S(1)}, s16[528,128]{1,0:T(8,128)(2,1)S(1...) custom-call(s32[16]{0:T(128)S(1)} %xor_add_fusion.refs_0_, s32[16,128]{1,0:T(8,128)S(1)} %get-tuple-element.49.over_ref.refs_1_, ...), custom_call_target="tpu_custom_call" | custom-call | flops 5000000000 | bytes 8388608 | tf_op jit(solution)/shard_map/pallas_call | solution.py:244
  64.2 3.3 %collective-permute-start.18 = (s16[528,128]{1,0:T(8,128)(2,1)S(1)}, s16[528,128]{1,0:T(8,128)(2,1)S(1)}, u32[]{:S(2)}, u32[]{:S(2)}) collective-permute-start(s16[528,128]{1,0:T(8,128)(2,1)S(1)} %get-tuple-element.59), channel_id=1, source_target_pairs={{0,1},{1,2},{2,3},{3,0},{4,5},{5,6},{6,7},{7,4},{8,9},{9,10},{10,1... | collective-permute-start | bytes 405512 | tf_op jit(solution)/shard_map/ppermute | solution.py:380
  67.7 1.6 %collective-permute-start.20 = (s16[528,128]{1,0:T(8,128)(2,1)S(1)}, s16[528,128]{1,0:T(8,128)(2,1)S(1)}, u32[]{:S(2)}, u32[]{:S(2)}) collective-permute-start(s16[528,128]{1,0:T(8,128)(2,1)S(1)} %get-tuple-element.61), channel_id=1, source_target_pairs={{0,3},{1,0},{2,1},{3,2},{4,7},{5,4},{6,5},{7,6},{8,11},{9,8},{10,9... | collective-permute-start | bytes 405512 | tf_op jit(solution)/shard_map/ppermute | solution.py:380
  69.3 4.6 %shard_map.71 = (f32[4,128,128]{2,1,0:T(8,128)S(1)}, s16[528,128]{1,0:T(8,128)(2,1)S(1)}, s16[528,128]{1,0:T(8,128)(2,1)S(1)}, s16[528,128]{1,0:T(8,128)(2,1)S(1)}) custom-call(s32[16,128]{1,0:T(8,128)S(1)} %get-tuple-element.57.over_ref, bf16[1024,4096]{1,0:T(8,128)(2,1)} %get-tuple-element.55.refs_2_.ints_ref, bf16[512,4096]{1,0:T(8,128)(2,1)S(1)} %get-tuple-element.63.amps), custom_call_target="tpu_custom_call" | custom-call | flops 5000000000 | bytes 8388608 | tf_op jit(solution)/shard_map/pallas_call | solution.py:259
  73.9 1.7 %collective-permute-start.21 = (s16[528,128]{1,0:T(8,128)(2,1)S(1)}, s16[528,128]{1,0:T(8,128)(2,1)S(1)}, u32[]{:S(2)}, u32[]{:S(2)}) collective-permute-start(s16[528,128]{1,0:T(8,128)(2,1)S(1)} %get-tuple-element.65), channel_id=1, source_target_pairs={{0,1},{1,2},{2,3},{3,0},{4,5},{5,6},{6,7},{7,4},{8,9},{9,10},{10,1... | collective-permute-start | bytes 405512 | tf_op jit(solution)/shard_map/ppermute | solution.py:380
  75.6 2.1 %collective-permute-start.22 = (s16[528,128]{1,0:T(8,128)(2,1)S(1)}, s16[528,128]{1,0:T(8,128)(2,1)S(1)}, u32[]{:S(2)}, u32[]{:S(2)}) collective-permute-start(s16[528,128]{1,0:T(8,128)(2,1)S(1)} %get-tuple-element.66), channel_id=1, source_target_pairs={{0,2},{1,3},{2,0},{3,1},{4,6},{5,7},{6,4},{7,5},{8,10},{9,11},{10,... | collective-permute-start | bytes 405512 | tf_op jit(solution)/shard_map/ppermute | solution.py:380
  77.8 1.5 %shard_map.68 = (f32[8,128,128]{2,1,0:T(8,128)S(1)}, s16[528,128]{1,0:T(8,128)(2,1)S(1)}, s16[528,128]{1,0:T(8,128)(2,1)S(1)}) custom-call(s32[16,128]{1,0:T(8,128)S(1)} %get-tuple-element.49.over_ref.refs_1_, f32[8,128,128]{2,1,0:T(8,128)S(1)} %get-tuple-element.50.own_ref, s16[1040,128]{1,0:T(8,128)(2,1)S(1)} %collective-permute-done.13.a_ref, ...), custom_call_target="tpu_custom_call" | custom-call | tf_op jit(solution)/shard_map/pallas_call | solution.py:292
  79.2 0.9 shard_map.70
  80.2 1.6 %collective-permute-start.24 = (s16[528,128]{1,0:T(8,128)(2,1)S(1)}, s16[528,128]{1,0:T(8,128)(2,1)S(1)}, u32[]{:S(2)}, u32[]{:S(2)}) collective-permute-start(s16[528,128]{1,0:T(8,128)(2,1)S(1)} %shard_map.74), channel_id=1, source_target_pairs={{0,4},{4,0},{1,5},{5,1},{2,6},{6,2},{3,7},{7,3},{8,12},{12,8},{9,1... | collective-permute-start | bytes 405512 | tf_op jit(solution)/shard_map/ppermute | solution.py:28
  81.8 1.1 %collective-permute-done.22.b_ref = s16[528,128]{1,0:T(8,128)(2,1)S(1)} collective-permute-done((s16[528,128]{1,0:T(8,128)(2,1)S(1)}, s16[528,128]{1,0:T(8,128)(2,1)S(1)}, u32[]{:S(2)}, u32[]{:S(2)}) %collective-permute-start.22) | collective-permute-done | bytes 135200 | tf_op jit(solution)/shard_map/ppermute | solution.py:380
  82.9 1.4 %collective-permute-done.23.c_ref = s16[528,128]{1,0:T(8,128)(2,1)S(1)} collective-permute-done((s16[528,128]{1,0:T(8,128)(2,1)S(1)}, s16[528,128]{1,0:T(8,128)(2,1)S(1)}, u32[]{:S(2)}, u32[]{:S(2)}) %collective-permute-start.23) | collective-permute-done | bytes 135200 | tf_op jit(solution)/shard_map/ppermute | solution.py:380
  84.3 0.9 shard_map.72
  85.2 1.6 %collective-permute-start.25 = (s16[528,128]{1,0:T(8,128)(2,1)S(1)}, s16[528,128]{1,0:T(8,128)(2,1)S(1)}, u32[]{:S(2)}, u32[]{:S(2)}) collective-permute-start(s16[528,128]{1,0:T(8,128)(2,1)S(1)} %shard_map.73.sent_ref), channel_id=1, source_target_pairs={{0,4},{4,0},{1,5},{5,1},{2,6},{6,2},{3,7},{7,3},{8,12},{12,8},{9,1... | collective-permute-start | bytes 405512 | tf_op jit(solution)/shard_map/ppermute | solution.py:28
  86.8 3.5 %collective-permute-done.25.got_b = s16[528,128]{1,0:T(8,128)(2,1)S(1)} collective-permute-done((s16[528,128]{1,0:T(8,128)(2,1)S(1)}, s16[528,128]{1,0:T(8,128)(2,1)S(1)}, u32[]{:S(2)}, u32[]{:S(2)}) %collective-permute-start.25) | collective-permute-done | bytes 135200 | tf_op jit(solution)/shard_map/ppermute | solution.py:28
  90.3 0.9 shard_map.75
  92.3 0.7 copy-done.2
  (51 shorter events, 3.4 us)
Async XLA Ops:
  1.8 1.5 %collective-permute-start = (bf16[1,608,128]{2,1,0:T(8,128)(2,1)S(1)}, bf16[1,608,128]{2,1,0:T(8,128)(2,1)S(1)}, u32[]{:S(2)}, u32[]{:S(2)}) collective-permute-start(bf16[1,608,128]{2,1,0:T(8,128)(2,1)S(1)} %shard_map.66), channel_id=1, source_target_pairs={{0,8},{8,0},{1,9},{9,1},{2,10},{10,2},{3,11},{11,3},{4,12},{12,4},... | collective-permute-start | bytes 466952 | tf_op jit(solution)/shard_map/ppermute | solution.py:28
  3.3 11.4 %collective-permute-start.1 = (bf16[2,608,128]{2,1,0:T(8,128)(2,1)S(1)}, bf16[2,608,128]{2,1,0:T(8,128)(2,1)S(1)}, u32[]{:S(2)}, u32[]{:S(2)}) collective-permute-start(bf16[2,608,128]{2,1,0:T(8,128)(2,1)S(1)} %pad_maximum_fusion.refs_3_), channel_id=1, source_target_pairs={{0,16},{16,32},{32,48},{48,64},{64,80},{80,96},{96,112},{112,0},{8... | collective-permute-start | bytes 933896 | tf_op jit(solution)/shard_map/ppermute | solution.py:375
  5.3 6.7 %collective-permute-start.7 = (bf16[1,608,128]{2,1,0:T(8,128)(2,1)S(1)}, bf16[1,608,128]{2,1,0:T(8,128)(2,1)S(1)}, u32[]{:S(2)}, u32[]{:S(2)}) collective-permute-start(bf16[1,608,128]{2,1,0:T(8,128)(2,1)S(1)} %shard_map.66), channel_id=1, source_target_pairs={{0,128},{128,0},{1,129},{129,1},{2,130},{130,2},{3,131},{131,3},{4... | collective-permute-start | bytes 466952 | tf_op jit(solution)/shard_map/ppermute | solution.py:28
  12.0 3.7 %collective-permute-start.8 = (bf16[1,608,128]{2,1,0:T(8,128)(2,1)S(1)}, bf16[1,608,128]{2,1,0:T(8,128)(2,1)S(1)}, u32[]{:S(2)}, u32[]{:S(2)}) collective-permute-start(bf16[1,608,128]{2,1,0:T(8,128)(2,1)S(1)} %collective-permute-done.7), channel_id=1, source_target_pairs={{0,8},{8,0},{1,9},{9,1},{2,10},{10,2},{3,11},{11,3},{4,12},{12,4},... | collective-permute-start | bytes 466952 | tf_op jit(solution)/shard_map/ppermute | solution.py:28
  14.7 8.1 %collective-permute-start.2 = (bf16[2,608,128]{2,1,0:T(8,128)(2,1)S(1)}, bf16[2,608,128]{2,1,0:T(8,128)(2,1)S(1)}, u32[]{:S(2)}, u32[]{:S(2)}) collective-permute-start(bf16[2,608,128]{2,1,0:T(8,128)(2,1)S(1)} %collective-permute-done.1), channel_id=1, source_target_pairs={{0,16},{16,32},{32,48},{48,64},{64,80},{80,96},{96,112},{112,0},{8... | collective-permute-start | bytes 933896 | tf_op jit(solution)/shard_map/ppermute | solution.py:375
  15.7 10.4 %collective-permute-start.9 = (bf16[2,608,128]{2,1,0:T(8,128)(2,1)S(1)}, bf16[2,608,128]{2,1,0:T(8,128)(2,1)S(1)}, u32[]{:S(2)}, u32[]{:S(2)}) collective-permute-start(bf16[2,608,128]{2,1,0:T(8,128)(2,1)S(1)} %constant_dynamic-update-slice_fusion.4.refs_3_), channel_id=1, source_target_pairs={{0,16},{16,32},{32,48},{48,64},{64,80},{80,96},{96,112},{112,0},{8... | collective-permute-start | bytes 933896 | tf_op jit(solution)/shard_map/ppermute | solution.py:375
  22.8 8.1 %collective-permute-start.4 = (bf16[2,608,128]{2,1,0:T(8,128)(2,1)S(1)}, bf16[2,608,128]{2,1,0:T(8,128)(2,1)S(1)}, u32[]{:S(2)}, u32[]{:S(2)}) collective-permute-start(bf16[2,608,128]{2,1,0:T(8,128)(2,1)S(1)} %collective-permute-done.2), channel_id=1, source_target_pairs={{0,16},{16,32},{32,48},{48,64},{64,80},{80,96},{96,112},{112,0},{8... | collective-permute-start | bytes 933896 | tf_op jit(solution)/shard_map/ppermute | solution.py:375
  26.1 8.1 %collective-permute-start.10 = (bf16[2,608,128]{2,1,0:T(8,128)(2,1)S(1)}, bf16[2,608,128]{2,1,0:T(8,128)(2,1)S(1)}, u32[]{:S(2)}, u32[]{:S(2)}) collective-permute-start(bf16[2,608,128]{2,1,0:T(8,128)(2,1)S(1)} %collective-permute-done.9), channel_id=1, source_target_pairs={{0,16},{16,32},{32,48},{48,64},{64,80},{80,96},{96,112},{112,0},{8... | collective-permute-start | bytes 933896 | tf_op jit(solution)/shard_map/ppermute | solution.py:375
  30.9 6.5 %collective-permute-start.5 = (bf16[1,608,128]{2,1,0:T(8,128)(2,1)S(1)}, bf16[1,608,128]{2,1,0:T(8,128)(2,1)S(1)}, u32[]{:S(2)}, u32[]{:S(2)}) collective-permute-start(bf16[1,608,128]{2,1,0:T(8,128)(2,1)S(1)} %slice.8), channel_id=1, source_target_pairs={{0,16},{16,32},{32,48},{48,64},{64,80},{80,96},{96,112},{112,0},{8... | collective-permute-start | bytes 466952 | tf_op jit(solution)/shard_map/ppermute | solution.py:375
  31.1 11.6 %collective-permute-start.3 = (bf16[4,608,128]{2,1,0:T(8,128)(2,1)S(1)}, bf16[4,608,128]{2,1,0:T(8,128)(2,1)S(1)}, u32[]{:S(2)}, u32[]{:S(2)}) collective-permute-start(bf16[4,608,128]{2,1,0:T(8,128)(2,1)S(1)} %constant_dynamic-update-slice_fusion.refs_4_), channel_id=1, source_target_pairs={{0,8},{8,0},{1,9},{9,1},{2,10},{10,2},{3,11},{11,3},{4,12},{12,4},... | collective-permute-start | bytes 1867784 | tf_op jit(solution)/shard_map/ppermute | solution.py:28
  34.2 8.1 %collective-permute-start.11 = (bf16[2,608,128]{2,1,0:T(8,128)(2,1)S(1)}, bf16[2,608,128]{2,1,0:T(8,128)(2,1)S(1)}, u32[]{:S(2)}, u32[]{:S(2)}) collective-permute-start(bf16[2,608,128]{2,1,0:T(8,128)(2,1)S(1)} %collective-permute-done.10), channel_id=1, source_target_pairs={{0,16},{16,32},{32,48},{48,64},{64,80},{80,96},{96,112},{112,0},{8... | collective-permute-start | bytes 933896 | tf_op jit(solution)/shard_map/ppermute | solution.py:375
  37.5 5.2 %collective-permute-start.6 = (bf16[3,608,128]{2,1,0:T(8,128)(2,1)S(1)}, bf16[3,608,128]{2,1,0:T(8,128)(2,1)S(1)}, u32[]{:S(2)}, u32[]{:S(2)}) collective-permute-start(bf16[3,608,128]{2,1,0:T(8,128)(2,1)S(1)} %constant_dynamic-update-slice_fusion.2.refs_6_), channel_id=1, source_target_pairs={{0,8},{8,0},{1,9},{9,1},{2,10},{10,2},{3,11},{11,3},{4,12},{12,4},... | collective-permute-start | bytes 1400840 | tf_op jit(solution)/shard_map/ppermute | solution.py:28
  38.3 19.0 %collective-permute-start.16 = (bf16[4,608,128]{2,1,0:T(8,128)(2,1)S(1)}, bf16[4,608,128]{2,1,0:T(8,128)(2,1)S(1)}, u32[]{:S(2)}, u32[]{:S(2)}) collective-permute-start(bf16[4,608,128]{2,1,0:T(8,128)(2,1)S(1)} %constant_dynamic-update-slice_fusion.6.refs_4_), channel_id=1, source_target_pairs={{0,8},{8,0},{1,9},{9,1},{2,10},{10,2},{3,11},{11,3},{4,12},{12,4},... | collective-permute-start | bytes 1867784 | tf_op jit(solution)/shard_map/ppermute | solution.py:28
  42.4 11.9 %collective-permute-start.12 = (bf16[1,608,128]{2,1,0:T(8,128)(2,1)S(1)}, bf16[1,608,128]{2,1,0:T(8,128)(2,1)S(1)}, u32[]{:S(2)}, u32[]{:S(2)}) collective-permute-start(bf16[1,608,128]{2,1,0:T(8,128)(2,1)S(1)} %slice.9), channel_id=1, source_target_pairs={{0,16},{16,32},{32,48},{48,64},{64,80},{80,96},{96,112},{112,0},{8... | collective-permute-start | bytes 466952 | tf_op jit(solution)/shard_map/ppermute | solution.py:375
  54.3 3.0 %collective-permute-start.17 = (bf16[3,608,128]{2,1,0:T(8,128)(2,1)S(1)}, bf16[3,608,128]{2,1,0:T(8,128)(2,1)S(1)}, u32[]{:S(2)}, u32[]{:S(2)}) collective-permute-start(bf16[3,608,128]{2,1,0:T(8,128)(2,1)S(1)} %constant_dynamic-update-slice_fusion.8.refs_6_), channel_id=1, source_target_pairs={{0,8},{8,0},{1,9},{9,1},{2,10},{10,2},{3,11},{11,3},{4,12},{12,4},... | collective-permute-start | bytes 1400840 | tf_op jit(solution)/shard_map/ppermute | solution.py:28
  54.4 13.3 %collective-permute-start.13 = (s16[1040,128]{1,0:T(8,128)(2,1)S(1)}, s16[1040,128]{1,0:T(8,128)(2,1)S(1)}, u32[]{:S(2)}, u32[]{:S(2)}) collective-permute-start(s16[1040,128]{1,0:T(8,128)(2,1)S(1)} %get-tuple-element.51), channel_id=1, source_target_pairs={{0,1},{1,2},{2,3},{3,0},{4,5},{5,6},{6,7},{7,4},{8,9},{9,10},{10,1... | collective-permute-start | bytes 798728 | tf_op jit(solution)/shard_map/ppermute | solution.py:380
  54.8 19.2 %collective-permute-start.14 = (s16[1040,128]{1,0:T(8,128)(2,1)S(1)}, s16[1040,128]{1,0:T(8,128)(2,1)S(1)}, u32[]{:S(2)}, u32[]{:S(2)}) collective-permute-start(s16[1040,128]{1,0:T(8,128)(2,1)S(1)} %get-tuple-element.52), channel_id=1, source_target_pairs={{0,2},{1,3},{2,0},{3,1},{4,6},{5,7},{6,4},{7,5},{8,10},{9,11},{10,... | collective-permute-start | bytes 798728 | tf_op jit(solution)/shard_map/ppermute | solution.py:380
  57.3 18.3 %collective-permute-start.15 = (s16[1040,128]{1,0:T(8,128)(2,1)S(1)}, s16[1040,128]{1,0:T(8,128)(2,1)S(1)}, u32[]{:S(2)}, u32[]{:S(2)}) collective-permute-start(s16[1040,128]{1,0:T(8,128)(2,1)S(1)} %get-tuple-element.53), channel_id=1, source_target_pairs={{0,3},{1,0},{2,1},{3,2},{4,7},{5,4},{6,5},{7,6},{8,11},{9,8},{10,9... | collective-permute-start | bytes 798728 | tf_op jit(solution)/shard_map/ppermute | solution.py:380
  64.2 13.6 %collective-permute-start.18 = (s16[528,128]{1,0:T(8,128)(2,1)S(1)}, s16[528,128]{1,0:T(8,128)(2,1)S(1)}, u32[]{:S(2)}, u32[]{:S(2)}) collective-permute-start(s16[528,128]{1,0:T(8,128)(2,1)S(1)} %get-tuple-element.59), channel_id=1, source_target_pairs={{0,1},{1,2},{2,3},{3,0},{4,5},{5,6},{6,7},{7,4},{8,9},{9,10},{10,1... | collective-permute-start | bytes 405512 | tf_op jit(solution)/shard_map/ppermute | solution.py:380
  67.5 11.7 %collective-permute-start.19 = (s16[528,128]{1,0:T(8,128)(2,1)S(1)}, s16[528,128]{1,0:T(8,128)(2,1)S(1)}, u32[]{:S(2)}, u32[]{:S(2)}) collective-permute-start(s16[528,128]{1,0:T(8,128)(2,1)S(1)} %get-tuple-element.60), channel_id=1, source_target_pairs={{0,2},{1,3},{2,0},{3,1},{4,6},{5,7},{6,4},{7,5},{8,10},{9,11},{10,... | collective-permute-start | bytes 405512 | tf_op jit(solution)/shard_map/ppermute | solution.py:380
  67.7 11.5 %collective-permute-start.20 = (s16[528,128]{1,0:T(8,128)(2,1)S(1)}, s16[528,128]{1,0:T(8,128)(2,1)S(1)}, u32[]{:S(2)}, u32[]{:S(2)}) collective-permute-start(s16[528,128]{1,0:T(8,128)(2,1)S(1)} %get-tuple-element.61), channel_id=1, source_target_pairs={{0,3},{1,0},{2,1},{3,2},{4,7},{5,4},{6,5},{7,6},{8,11},{9,8},{10,9... | collective-permute-start | bytes 405512 | tf_op jit(solution)/shard_map/ppermute | solution.py:380
  69.3 22.6 %copy-start = (s32[32,32]{1,0:T(8,128)S(1)}, s32[32,32]{1,0:T(8,128)}, u32[]{:S(2)}) copy-start(s32[32,32]{1,0:T(8,128)} %mask_ref.1) | copy-start | bytes 12292
  69.3 22.6 %copy-start.1 = (s32[8,32]{1,0:T(8,128)S(1)}, s32[8,32]{1,0:T(8,128)}, u32[]{:S(2)}) copy-start(s32[8,32]{1,0:T(8,128)} %refs_1_.1) | copy-start | bytes 3076
  73.9 7.8 %collective-permute-start.21 = (s16[528,128]{1,0:T(8,128)(2,1)S(1)}, s16[528,128]{1,0:T(8,128)(2,1)S(1)}, u32[]{:S(2)}, u32[]{:S(2)}) collective-permute-start(s16[528,128]{1,0:T(8,128)(2,1)S(1)} %get-tuple-element.65), channel_id=1, source_target_pairs={{0,1},{1,2},{2,3},{3,0},{4,5},{5,6},{6,7},{7,4},{8,9},{9,10},{10,1... | collective-permute-start | bytes 405512 | tf_op jit(solution)/shard_map/ppermute | solution.py:380
  75.6 7.2 %collective-permute-start.22 = (s16[528,128]{1,0:T(8,128)(2,1)S(1)}, s16[528,128]{1,0:T(8,128)(2,1)S(1)}, u32[]{:S(2)}, u32[]{:S(2)}) collective-permute-start(s16[528,128]{1,0:T(8,128)(2,1)S(1)} %get-tuple-element.66), channel_id=1, source_target_pairs={{0,2},{1,3},{2,0},{3,1},{4,6},{5,7},{6,4},{7,5},{8,10},{9,11},{10,... | collective-permute-start | bytes 405512 | tf_op jit(solution)/shard_map/ppermute | solution.py:380
  77.8 6.5 %collective-permute-start.23 = (s16[528,128]{1,0:T(8,128)(2,1)S(1)}, s16[528,128]{1,0:T(8,128)(2,1)S(1)}, u32[]{:S(2)}, u32[]{:S(2)}) collective-permute-start(s16[528,128]{1,0:T(8,128)(2,1)S(1)} %get-tuple-element.67), channel_id=1, source_target_pairs={{0,3},{1,0},{2,1},{3,2},{4,7},{5,4},{6,5},{7,6},{8,11},{9,8},{10,9... | collective-permute-start | bytes 405512 | tf_op jit(solution)/shard_map/ppermute | solution.py:380
  80.2 6.6 %collective-permute-start.24 = (s16[528,128]{1,0:T(8,128)(2,1)S(1)}, s16[528,128]{1,0:T(8,128)(2,1)S(1)}, u32[]{:S(2)}, u32[]{:S(2)}) collective-permute-start(s16[528,128]{1,0:T(8,128)(2,1)S(1)} %shard_map.74), channel_id=1, source_target_pairs={{0,4},{4,0},{1,5},{5,1},{2,6},{6,2},{3,7},{7,3},{8,12},{12,8},{9,1... | collective-permute-start | bytes 405512 | tf_op jit(solution)/shard_map/ppermute | solution.py:28
  85.2 5.1 %collective-permute-start.25 = (s16[528,128]{1,0:T(8,128)(2,1)S(1)}, s16[528,128]{1,0:T(8,128)(2,1)S(1)}, u32[]{:S(2)}, u32[]{:S(2)}) collective-permute-start(s16[528,128]{1,0:T(8,128)(2,1)S(1)} %shard_map.73.sent_ref), channel_id=1, source_target_pairs={{0,4},{4,0},{1,5},{5,1},{2,6},{6,2},{3,7},{7,3},{8,12},{12,8},{9,1... | collective-permute-start | bytes 405512 | tf_op jit(solution)/shard_map/ppermute | solution.py:28
  92.2 0.7 copy-start.2

commit v8 on v7

--- a/solution.py
+++ b/solution.py
@@ -368,11 +368,20 @@
     rows = (((far >> 1) - y) & 3) * 4 + (far & 1) * 2 + (core ^ jnp.asarray(OTHER, I32))
 
     own = pack(amplitudes, amp_mask)
-    across = swap(own, "xh")
-    blocks = [[jnp.concatenate([message, swap(message, "core")], axis=0)] for message in (own, across)]
-    for hop in range(1, 5):
-        for chain in blocks:
-            chain.append(lax.ppermute(chain[-1] if hop < 4 else chain[-1][:1], ("z", "core"), RING))
+
+    def with_sibling(message):
+        return jnp.concatenate([message, swap(message, "core")], axis=0)
+
+    def hop(block):
+        return lax.ppermute(block, ("z", "core"), RING)
+
+    pair = with_sibling(own)
+    first, far_pair = lax.optimization_barrier((hop(pair), with_sibling(swap(own, "xh"))))
+    blocks = [[pair, first], [far_pair]]
+    for chain in blocks:
+        while len(chain) < 4:
+            chain.append(hop(chain[-1]))
+        chain.append(hop(chain[-1][:1]))
     two = [jnp.concatenate(chain[1:3], axis=0) for chain in blocks]
     rest = jnp.concatenate(blocks[0][3:], axis=0)
 

time: 93.6 us -> 95.3 us (1.018)
  waiting for transfers between devices: 36 us -> 41.5 us
  starting transfers between devices: 25 us -> 20.6 us
    ppermute x8, waiting for transfers between devices: 23.8 us -> 29.8 us  [hop(): return lax.ppermute(block, ('z', 'core'), RING)]
    ppermute x9, starting transfers between devices: 10.5 us -> 6.42 us  [swap(): return lax.ppermute(x, axis, [(0, 1), (1, 0)])]
    ppermute x9, waiting for transfers between devices: 9.61 us -> 8.26 us  [swap(): return lax.ppermute(x, axis, [(0, 1), (1, 0)])]
where the time goes in v8:
time: 95.3 us; the launch traced here: 94.1 us
  waiting for transfers between devices  41.5 us (44%)
  Pallas kernels  29 us (30%)
  starting transfers between devices  20.6 us (22%)
    ppermute x8, waiting for transfers between devices, hop(): return lax.ppermute(block, ('z', 'core'), RING)  29.8 us
    ppermute x9, starting transfers between devices, spread(): lax.ppermute(part, 'y', [(i, (i + d + 1) % 4) for i in range(4)])  11.8 us
    pallas_call x1, Pallas kernels, first_chunk(): pl.pallas_call(lambda *refs: first_kernel(sizes, *refs), in_specs=[SMEM,...  11.6 us
    ppermute x9, waiting for transfers between devices, swap(): return lax.ppermute(x, axis, [(0, 1), (1, 0)])  8.26 us
    pallas_call x1, Pallas kernels, second_chunk(): pl.pallas_call(lambda *refs: second_kernel(sizes, *refs), in_specs=[SMEM,...  6.84 us
    ppermute x9, starting transfers between devices, swap(): return lax.ppermute(x, axis, [(0, 1), (1, 0)])  6.42 us
    pallas_call x1, Pallas kernels, second_half(): pl.pallas_call(third_kernel, in_specs=[VMEM, ANYWHERE, VMEM], out_specs=[...  4.58 us
    ppermute x9, waiting for transfers between devices, spread(): lax.ppermute(part, 'y', [(i, (i + d + 1) % 4) for i in range(4)])  3.47 us
  transfers between devices with their start and end apart: 26, of which 12 were waited for; matrix products, arithmetic and copies ran while one was open for 1% of the time, Pallas kernels for 28%

profile of v8, /device:TPU:24, one launch (start us, length us, event | category | flops | bytes accessed | tf_op | source)
XLA Modules:
  0.0 94.1 jit_solution(8859708881851210946)
XLA Ops:
  0.0 1.8 %shard_map.66 = bf16[1,608,128]{2,1,0:T(8,128)(2,1)S(1)} custom-call(bf16[32,4096]{1,0:T(8,128)(2,1)} %amps_ref.1, s32[32,32]{1,0:T(8,128)} %mask_ref.1), custom_call_target="tpu_custom_call" | custom-call | tf_op jit(solution)/shard_map/pallas_call | solution.py:68
  1.9 3.1 %collective-permute-start.2 = (bf16[1,608,128]{2,1,0:T(8,128)(2,1)S(1)}, bf16[1,608,128]{2,1,0:T(8,128)(2,1)S(1)}, u32[]{:S(2)}, u32[]{:S(2)}) collective-permute-start(bf16[1,608,128]{2,1,0:T(8,128)(2,1)S(1)} %shard_map.66), channel_id=1, source_target_pairs={{0,128},{128,0},{1,129},{129,1},{2,130},{130,2},{3,131},{131,3},{4... | collective-permute-start | bytes 466952 | tf_op jit(solution)/shard_map/ppermute | solution.py:28
  5.0 2.0 %collective-permute-start.1 = (bf16[2,608,128]{2,1,0:T(8,128)(2,1)S(1)}, bf16[2,608,128]{2,1,0:T(8,128)(2,1)S(1)}, u32[]{:S(2)}, u32[]{:S(2)}) collective-permute-start(bf16[2,608,128]{2,1,0:T(8,128)(2,1)S(1)} %pad_maximum_fusion.refs_3_), channel_id=1, source_target_pairs={{0,16},{16,32},{32,48},{48,64},{64,80},{80,96},{96,112},{112,0},{8... | collective-permute-start | bytes 933896 | tf_op jit(solution)/shard_map/ppermute | solution.py:376
  7.0 2.8 %collective-permute-done.2 = bf16[1,608,128]{2,1,0:T(8,128)(2,1)S(1)} collective-permute-done((bf16[1,608,128]{2,1,0:T(8,128)(2,1)S(1)}, bf16[1,608,128]{2,1,0:T(8,128)(2,1)S(1)}, u32[]{:S(2)}, u32[]{:S(2)}) %collective-permute-start.2) | collective-permute-done | bytes 155680 | tf_op jit(solution)/shard_map/ppermute | solution.py:28
  9.8 1.0 %collective-permute-start.3 = (bf16[1,608,128]{2,1,0:T(8,128)(2,1)S(1)}, bf16[1,608,128]{2,1,0:T(8,128)(2,1)S(1)}, u32[]{:S(2)}, u32[]{:S(2)}) collective-permute-start(bf16[1,608,128]{2,1,0:T(8,128)(2,1)S(1)} %collective-permute-done.2), channel_id=1, source_target_pairs={{0,8},{8,0},{1,9},{9,1},{2,10},{10,2},{3,11},{11,3},{4,12},{12,4},... | collective-permute-start | bytes 466952 | tf_op jit(solution)/shard_map/ppermute | solution.py:28
  10.9 1.0 %collective-permute-done.3 = bf16[1,608,128]{2,1,0:T(8,128)(2,1)S(1)} collective-permute-done((bf16[1,608,128]{2,1,0:T(8,128)(2,1)S(1)}, bf16[1,608,128]{2,1,0:T(8,128)(2,1)S(1)}, u32[]{:S(2)}, u32[]{:S(2)}) %collective-permute-start.3) | collective-permute-done | bytes 155680 | tf_op jit(solution)/shard_map/ppermute | solution.py:28
  11.9 4.0 %collective-permute-done.1 = bf16[2,608,128]{2,1,0:T(8,128)(2,1)S(1)} collective-permute-done((bf16[2,608,128]{2,1,0:T(8,128)(2,1)S(1)}, bf16[2,608,128]{2,1,0:T(8,128)(2,1)S(1)}, u32[]{:S(2)}, u32[]{:S(2)}) %collective-permute-start.1) | collective-permute-done | bytes 311328 | tf_op jit(solution)/shard_map/ppermute | solution.py:376
  15.9 8.1 %collective-permute-done.4 = bf16[2,608,128]{2,1,0:T(8,128)(2,1)S(1)} collective-permute-done((bf16[2,608,128]{2,1,0:T(8,128)(2,1)S(1)}, bf16[2,608,128]{2,1,0:T(8,128)(2,1)S(1)}, u32[]{:S(2)}, u32[]{:S(2)}) %collective-permute-start.4) | collective-permute-done | bytes 311328 | tf_op jit(solution)/shard_map/ppermute | solution.py:376
  24.0 3.3 %collective-permute-done.9 = bf16[2,608,128]{2,1,0:T(8,128)(2,1)S(1)} collective-permute-done((bf16[2,608,128]{2,1,0:T(8,128)(2,1)S(1)}, bf16[2,608,128]{2,1,0:T(8,128)(2,1)S(1)}, u32[]{:S(2)}, u32[]{:S(2)}) %collective-permute-start.9) | collective-permute-done | bytes 311328 | tf_op jit(solution)/shard_map/ppermute | solution.py:376
  27.3 4.7 %collective-permute-done.6 = bf16[2,608,128]{2,1,0:T(8,128)(2,1)S(1)} collective-permute-done((bf16[2,608,128]{2,1,0:T(8,128)(2,1)S(1)}, bf16[2,608,128]{2,1,0:T(8,128)(2,1)S(1)}, u32[]{:S(2)}, u32[]{:S(2)}) %collective-permute-start.6) | collective-permute-done | bytes 311328 | tf_op jit(solution)/shard_map/ppermute | solution.py:376
  32.3 3.1 %collective-permute-done.10 = bf16[2,608,128]{2,1,0:T(8,128)(2,1)S(1)} collective-permute-done((bf16[2,608,128]{2,1,0:T(8,128)(2,1)S(1)}, bf16[2,608,128]{2,1,0:T(8,128)(2,1)S(1)}, u32[]{:S(2)}, u32[]{:S(2)}) %collective-permute-start.10) | collective-permute-done | bytes 311328 | tf_op jit(solution)/shard_map/ppermute | solution.py:376
  35.4 3.2 %collective-permute-done.7 = bf16[1,608,128]{2,1,0:T(8,128)(2,1)S(1)} collective-permute-done((bf16[1,608,128]{2,1,0:T(8,128)(2,1)S(1)}, bf16[1,608,128]{2,1,0:T(8,128)(2,1)S(1)}, u32[]{:S(2)}, u32[]{:S(2)}) %collective-permute-start.7) | collective-permute-done | bytes 155680 | tf_op jit(solution)/shard_map/ppermute | solution.py:376
  38.7 0.7 xor_add_fusion.refs_0_
  40.1 3.4 %collective-permute-done.11 = bf16[2,608,128]{2,1,0:T(8,128)(2,1)S(1)} collective-permute-done((bf16[2,608,128]{2,1,0:T(8,128)(2,1)S(1)}, bf16[2,608,128]{2,1,0:T(8,128)(2,1)S(1)}, u32[]{:S(2)}, u32[]{:S(2)}) %collective-permute-start.11) | collective-permute-done | bytes 311328 | tf_op jit(solution)/shard_map/ppermute | solution.py:376
  43.9 11.6 %shard_map.67 = (f32[8,128,128]{2,1,0:T(8,128)S(1)}, s16[1040,128]{1,0:T(8,128)(2,1)S(1)}, s16[1040,128]{1,0:T(8,128)(2,1)S(1)}, s16[1040,128]{1,0:T(8,128)(2,1)...) custom-call(s32[16]{0:T(128)S(1)} %xor_add_fusion.refs_0_, s32[8,32]{1,0:T(8,128)} %refs_1_.1, ...), custom_call_target="tpu_custom_call" | custom-call | flops 10000000000 | bytes 16777216 | tf_op jit(solution)/shard_map/pallas_call | solution.py:226
  55.9 2.6 %collective-permute-start.14 = (s16[1040,128]{1,0:T(8,128)(2,1)S(1)}, s16[1040,128]{1,0:T(8,128)(2,1)S(1)}, u32[]{:S(2)}, u32[]{:S(2)}) collective-permute-start(s16[1040,128]{1,0:T(8,128)(2,1)S(1)} %get-tuple-element.56), channel_id=1, source_target_pairs={{0,2},{1,3},{2,0},{3,1},{4,6},{5,7},{6,4},{7,5},{8,10},{9,11},{10,... | collective-permute-start | bytes 798728 | tf_op jit(solution)/shard_map/ppermute | solution.py:389
  58.5 6.8 %shard_map.69 = (f32[4,128,128]{2,1,0:T(8,128)S(1)}, s16[528,128]{1,0:T(8,128)(2,1)S(1)}, s16[528,128]{1,0:T(8,128)(2,1)S(1)}, s16[528,128]{1,0:T(8,128)(2,1)S(1...) custom-call(s32[16]{0:T(128)S(1)} %xor_add_fusion.refs_0_, s32[16,128]{1,0:T(8,128)S(1)} %get-tuple-element.53.over_ref.refs_1_, ...), custom_call_target="tpu_custom_call" | custom-call | flops 5000000000 | bytes 8388608 | tf_op jit(solution)/shard_map/pallas_call | solution.py:244
  65.4 3.3 %collective-permute-start.18 = (s16[528,128]{1,0:T(8,128)(2,1)S(1)}, s16[528,128]{1,0:T(8,128)(2,1)S(1)}, u32[]{:S(2)}, u32[]{:S(2)}) collective-permute-start(s16[528,128]{1,0:T(8,128)(2,1)S(1)} %get-tuple-element.63), channel_id=1, source_target_pairs={{0,1},{1,2},{2,3},{3,0},{4,5},{5,6},{6,7},{7,4},{8,9},{9,10},{10,1... | collective-permute-start | bytes 405512 | tf_op jit(solution)/shard_map/ppermute | solution.py:389
  68.9 1.6 %collective-permute-start.20 = (s16[528,128]{1,0:T(8,128)(2,1)S(1)}, s16[528,128]{1,0:T(8,128)(2,1)S(1)}, u32[]{:S(2)}, u32[]{:S(2)}) collective-permute-start(s16[528,128]{1,0:T(8,128)(2,1)S(1)} %get-tuple-element.65), channel_id=1, source_target_pairs={{0,3},{1,0},{2,1},{3,2},{4,7},{5,4},{6,5},{7,6},{8,11},{9,8},{10,9... | collective-permute-start | bytes 405512 | tf_op jit(solution)/shard_map/ppermute | solution.py:389
  70.5 4.6 %shard_map.71 = (f32[4,128,128]{2,1,0:T(8,128)S(1)}, s16[528,128]{1,0:T(8,128)(2,1)S(1)}, s16[528,128]{1,0:T(8,128)(2,1)S(1)}, s16[528,128]{1,0:T(8,128)(2,1)S(1)}) custom-call(s32[16,128]{1,0:T(8,128)S(1)} %get-tuple-element.61.over_ref, bf16[1024,4096]{1,0:T(8,128)(2,1)} %get-tuple-element.59.refs_2_.ints_ref, bf16[512,4096]{1,0:T(8,128)(2,1)S(1)} %get-tuple-element.67.amps), custom_call_target="tpu_custom_call" | custom-call | flops 5000000000 | bytes 8388608 | tf_op jit(solution)/shard_map/pallas_call | solution.py:259
  75.1 1.7 %collective-permute-start.21 = (s16[528,128]{1,0:T(8,128)(2,1)S(1)}, s16[528,128]{1,0:T(8,128)(2,1)S(1)}, u32[]{:S(2)}, u32[]{:S(2)}) collective-permute-start(s16[528,128]{1,0:T(8,128)(2,1)S(1)} %get-tuple-element.69), channel_id=1, source_target_pairs={{0,1},{1,2},{2,3},{3,0},{4,5},{5,6},{6,7},{7,4},{8,9},{9,10},{10,1... | collective-permute-start | bytes 405512 | tf_op jit(solution)/shard_map/ppermute | solution.py:389
  76.8 2.1 %collective-permute-start.22 = (s16[528,128]{1,0:T(8,128)(2,1)S(1)}, s16[528,128]{1,0:T(8,128)(2,1)S(1)}, u32[]{:S(2)}, u32[]{:S(2)}) collective-permute-start(s16[528,128]{1,0:T(8,128)(2,1)S(1)} %get-tuple-element.70), channel_id=1, source_target_pairs={{0,2},{1,3},{2,0},{3,1},{4,6},{5,7},{6,4},{7,5},{8,10},{9,11},{10,... | collective-permute-start | bytes 405512 | tf_op jit(solution)/shard_map/ppermute | solution.py:389
  78.9 1.5 %shard_map.68 = (f32[8,128,128]{2,1,0:T(8,128)S(1)}, s16[528,128]{1,0:T(8,128)(2,1)S(1)}, s16[528,128]{1,0:T(8,128)(2,1)S(1)}) custom-call(s32[16,128]{1,0:T(8,128)S(1)} %get-tuple-element.53.over_ref.refs_1_, f32[8,128,128]{2,1,0:T(8,128)S(1)} %get-tuple-element.54.own_ref, s16[1040,128]{1,0:T(8,128)(2,1)S(1)} %collective-permute-done.13.a_ref, ...), custom_call_target="tpu_custom_call" | custom-call | tf_op jit(solution)/shard_map/pallas_call | solution.py:292
  80.4 0.9 shard_map.70
  81.3 0.7 collective-permute-start.24
  82.0 2.0 %collective-permute-done.22.b_ref = s16[528,128]{1,0:T(8,128)(2,1)S(1)} collective-permute-done((s16[528,128]{1,0:T(8,128)(2,1)S(1)}, s16[528,128]{1,0:T(8,128)(2,1)S(1)}, u32[]{:S(2)}, u32[]{:S(2)}) %collective-permute-start.22) | collective-permute-done | bytes 135200 | tf_op jit(solution)/shard_map/ppermute | solution.py:389
  84.1 1.4 %collective-permute-done.23.c_ref = s16[528,128]{1,0:T(8,128)(2,1)S(1)} collective-permute-done((s16[528,128]{1,0:T(8,128)(2,1)S(1)}, s16[528,128]{1,0:T(8,128)(2,1)S(1)}, u32[]{:S(2)}, u32[]{:S(2)}) %collective-permute-start.23) | collective-permute-done | bytes 135200 | tf_op jit(solution)/shard_map/ppermute | solution.py:389
  85.5 0.9 shard_map.72
  86.4 0.7 collective-permute-start.25
  87.1 4.4 %collective-permute-done.25.got_b = s16[528,128]{1,0:T(8,128)(2,1)S(1)} collective-permute-done((s16[528,128]{1,0:T(8,128)(2,1)S(1)}, s16[528,128]{1,0:T(8,128)(2,1)S(1)}, u32[]{:S(2)}, u32[]{:S(2)}) %collective-permute-start.25) | collective-permute-done | bytes 135200 | tf_op jit(solution)/shard_map/ppermute | solution.py:28
  91.5 0.9 shard_map.75
  93.4 0.7 copy-done.2
  (50 shorter events, 2.6 us)
Async XLA Ops:
  1.8 3.2 %collective-permute-start = (bf16[1,608,128]{2,1,0:T(8,128)(2,1)S(1)}, bf16[1,608,128]{2,1,0:T(8,128)(2,1)S(1)}, u32[]{:S(2)}, u32[]{:S(2)}) collective-permute-start(bf16[1,608,128]{2,1,0:T(8,128)(2,1)S(1)} %shard_map.66), channel_id=1, source_target_pairs={{0,8},{8,0},{1,9},{9,1},{2,10},{10,2},{3,11},{11,3},{4,12},{12,4},... | collective-permute-start | bytes 466952 | tf_op jit(solution)/shard_map/ppermute | solution.py:28
  1.9 7.9 %collective-permute-start.2 = (bf16[1,608,128]{2,1,0:T(8,128)(2,1)S(1)}, bf16[1,608,128]{2,1,0:T(8,128)(2,1)S(1)}, u32[]{:S(2)}, u32[]{:S(2)}) collective-permute-start(bf16[1,608,128]{2,1,0:T(8,128)(2,1)S(1)} %shard_map.66), channel_id=1, source_target_pairs={{0,128},{128,0},{1,129},{129,1},{2,130},{130,2},{3,131},{131,3},{4... | collective-permute-start | bytes 466952 | tf_op jit(solution)/shard_map/ppermute | solution.py:28
  5.0 10.8 %collective-permute-start.1 = (bf16[2,608,128]{2,1,0:T(8,128)(2,1)S(1)}, bf16[2,608,128]{2,1,0:T(8,128)(2,1)S(1)}, u32[]{:S(2)}, u32[]{:S(2)}) collective-permute-start(bf16[2,608,128]{2,1,0:T(8,128)(2,1)S(1)} %pad_maximum_fusion.refs_3_), channel_id=1, source_target_pairs={{0,16},{16,32},{32,48},{48,64},{64,80},{80,96},{96,112},{112,0},{8... | collective-permute-start | bytes 933896 | tf_op jit(solution)/shard_map/ppermute | solution.py:376
  9.8 2.0 %collective-permute-start.3 = (bf16[1,608,128]{2,1,0:T(8,128)(2,1)S(1)}, bf16[1,608,128]{2,1,0:T(8,128)(2,1)S(1)}, u32[]{:S(2)}, u32[]{:S(2)}) collective-permute-start(bf16[1,608,128]{2,1,0:T(8,128)(2,1)S(1)} %collective-permute-done.2), channel_id=1, source_target_pairs={{0,8},{8,0},{1,9},{9,1},{2,10},{10,2},{3,11},{11,3},{4,12},{12,4},... | collective-permute-start | bytes 466952 | tf_op jit(solution)/shard_map/ppermute | solution.py:28
  15.9 8.1 %collective-permute-start.4 = (bf16[2,608,128]{2,1,0:T(8,128)(2,1)S(1)}, bf16[2,608,128]{2,1,0:T(8,128)(2,1)S(1)}, u32[]{:S(2)}, u32[]{:S(2)}) collective-permute-start(bf16[2,608,128]{2,1,0:T(8,128)(2,1)S(1)} %collective-permute-done.1), channel_id=1, source_target_pairs={{0,16},{16,32},{32,48},{48,64},{64,80},{80,96},{96,112},{112,0},{8... | collective-permute-start | bytes 933896 | tf_op jit(solution)/shard_map/ppermute | solution.py:376
  15.9 11.4 %collective-permute-start.9 = (bf16[2,608,128]{2,1,0:T(8,128)(2,1)S(1)}, bf16[2,608,128]{2,1,0:T(8,128)(2,1)S(1)}, u32[]{:S(2)}, u32[]{:S(2)}) collective-permute-start(bf16[2,608,128]{2,1,0:T(8,128)(2,1)S(1)} %pad_maximum_fusion.1.refs_3_), channel_id=1, source_target_pairs={{0,16},{16,32},{32,48},{48,64},{64,80},{80,96},{96,112},{112,0},{8... | collective-permute-start | bytes 933896 | tf_op jit(solution)/shard_map/ppermute | solution.py:376
  24.0 8.1 %collective-permute-start.6 = (bf16[2,608,128]{2,1,0:T(8,128)(2,1)S(1)}, bf16[2,608,128]{2,1,0:T(8,128)(2,1)S(1)}, u32[]{:S(2)}, u32[]{:S(2)}) collective-permute-start(bf16[2,608,128]{2,1,0:T(8,128)(2,1)S(1)} %collective-permute-done.4), channel_id=1, source_target_pairs={{0,16},{16,32},{32,48},{48,64},{64,80},{80,96},{96,112},{112,0},{8... | collective-permute-start | bytes 933896 | tf_op jit(solution)/shard_map/ppermute | solution.py:376
  27.3 8.1 %collective-permute-start.10 = (bf16[2,608,128]{2,1,0:T(8,128)(2,1)S(1)}, bf16[2,608,128]{2,1,0:T(8,128)(2,1)S(1)}, u32[]{:S(2)}, u32[]{:S(2)}) collective-permute-start(bf16[2,608,128]{2,1,0:T(8,128)(2,1)S(1)} %collective-permute-done.9), channel_id=1, source_target_pairs={{0,16},{16,32},{32,48},{48,64},{64,80},{80,96},{96,112},{112,0},{8... | collective-permute-start | bytes 933896 | tf_op jit(solution)/shard_map/ppermute | solution.py:376
  32.1 6.5 %collective-permute-start.7 = (bf16[1,608,128]{2,1,0:T(8,128)(2,1)S(1)}, bf16[1,608,128]{2,1,0:T(8,128)(2,1)S(1)}, u32[]{:S(2)}, u32[]{:S(2)}) collective-permute-start(bf16[1,608,128]{2,1,0:T(8,128)(2,1)S(1)} %slice.8), channel_id=1, source_target_pairs={{0,16},{16,32},{32,48},{48,64},{64,80},{80,96},{96,112},{112,0},{8... | collective-permute-start | bytes 466952 | tf_op jit(solution)/shard_map/ppermute | solution.py:376
  32.2 11.6 %collective-permute-start.5 = (bf16[4,608,128]{2,1,0:T(8,128)(2,1)S(1)}, bf16[4,608,128]{2,1,0:T(8,128)(2,1)S(1)}, u32[]{:S(2)}, u32[]{:S(2)}) collective-permute-start(bf16[4,608,128]{2,1,0:T(8,128)(2,1)S(1)} %constant_dynamic-update-slice_fusion.refs_4_), channel_id=1, source_target_pairs={{0,8},{8,0},{1,9},{9,1},{2,10},{10,2},{3,11},{11,3},{4,12},{12,4},... | collective-permute-start | bytes 1867784 | tf_op jit(solution)/shard_map/ppermute | solution.py:28
  35.4 8.1 %collective-permute-start.11 = (bf16[2,608,128]{2,1,0:T(8,128)(2,1)S(1)}, bf16[2,608,128]{2,1,0:T(8,128)(2,1)S(1)}, u32[]{:S(2)}, u32[]{:S(2)}) collective-permute-start(bf16[2,608,128]{2,1,0:T(8,128)(2,1)S(1)} %collective-permute-done.10), channel_id=1, source_target_pairs={{0,16},{16,32},{32,48},{48,64},{64,80},{80,96},{96,112},{112,0},{8... | collective-permute-start | bytes 933896 | tf_op jit(solution)/shard_map/ppermute | solution.py:376
  38.6 5.2 %collective-permute-start.8 = (bf16[3,608,128]{2,1,0:T(8,128)(2,1)S(1)}, bf16[3,608,128]{2,1,0:T(8,128)(2,1)S(1)}, u32[]{:S(2)}, u32[]{:S(2)}) collective-permute-start(bf16[3,608,128]{2,1,0:T(8,128)(2,1)S(1)} %constant_dynamic-update-slice_fusion.2.refs_6_), channel_id=1, source_target_pairs={{0,8},{8,0},{1,9},{9,1},{2,10},{10,2},{3,11},{11,3},{4,12},{12,4},... | collective-permute-start | bytes 1400840 | tf_op jit(solution)/shard_map/ppermute | solution.py:28
  39.5 19.0 %collective-permute-start.16 = (bf16[4,608,128]{2,1,0:T(8,128)(2,1)S(1)}, bf16[4,608,128]{2,1,0:T(8,128)(2,1)S(1)}, u32[]{:S(2)}, u32[]{:S(2)}) collective-permute-start(bf16[4,608,128]{2,1,0:T(8,128)(2,1)S(1)} %constant_dynamic-update-slice_fusion.4.refs_4_), channel_id=1, source_target_pairs={{0,8},{8,0},{1,9},{9,1},{2,10},{10,2},{3,11},{11,3},{4,12},{12,4},... | collective-permute-start | bytes 1867784 | tf_op jit(solution)/shard_map/ppermute | solution.py:28
  43.5 11.9 %collective-permute-start.12 = (bf16[1,608,128]{2,1,0:T(8,128)(2,1)S(1)}, bf16[1,608,128]{2,1,0:T(8,128)(2,1)S(1)}, u32[]{:S(2)}, u32[]{:S(2)}) collective-permute-start(bf16[1,608,128]{2,1,0:T(8,128)(2,1)S(1)} %slice.9), channel_id=1, source_target_pairs={{0,16},{16,32},{32,48},{48,64},{64,80},{80,96},{96,112},{112,0},{8... | collective-permute-start | bytes 466952 | tf_op jit(solution)/shard_map/ppermute | solution.py:376
  55.5 3.0 %collective-permute-start.17 = (bf16[3,608,128]{2,1,0:T(8,128)(2,1)S(1)}, bf16[3,608,128]{2,1,0:T(8,128)(2,1)S(1)}, u32[]{:S(2)}, u32[]{:S(2)}) collective-permute-start(bf16[3,608,128]{2,1,0:T(8,128)(2,1)S(1)} %constant_dynamic-update-slice_fusion.6.refs_6_), channel_id=1, source_target_pairs={{0,8},{8,0},{1,9},{9,1},{2,10},{10,2},{3,11},{11,3},{4,12},{12,4},... | collective-permute-start | bytes 1400840 | tf_op jit(solution)/shard_map/ppermute | solution.py:28
  55.6 13.3 %collective-permute-start.13 = (s16[1040,128]{1,0:T(8,128)(2,1)S(1)}, s16[1040,128]{1,0:T(8,128)(2,1)S(1)}, u32[]{:S(2)}, u32[]{:S(2)}) collective-permute-start(s16[1040,128]{1,0:T(8,128)(2,1)S(1)} %get-tuple-element.55), channel_id=1, source_target_pairs={{0,1},{1,2},{2,3},{3,0},{4,5},{5,6},{6,7},{7,4},{8,9},{9,10},{10,1... | collective-permute-start | bytes 798728 | tf_op jit(solution)/shard_map/ppermute | solution.py:389
  55.9 19.2 %collective-permute-start.14 = (s16[1040,128]{1,0:T(8,128)(2,1)S(1)}, s16[1040,128]{1,0:T(8,128)(2,1)S(1)}, u32[]{:S(2)}, u32[]{:S(2)}) collective-permute-start(s16[1040,128]{1,0:T(8,128)(2,1)S(1)} %get-tuple-element.56), channel_id=1, source_target_pairs={{0,2},{1,3},{2,0},{3,1},{4,6},{5,7},{6,4},{7,5},{8,10},{9,11},{10,... | collective-permute-start | bytes 798728 | tf_op jit(solution)/shard_map/ppermute | solution.py:389
  58.5 18.3 %collective-permute-start.15 = (s16[1040,128]{1,0:T(8,128)(2,1)S(1)}, s16[1040,128]{1,0:T(8,128)(2,1)S(1)}, u32[]{:S(2)}, u32[]{:S(2)}) collective-permute-start(s16[1040,128]{1,0:T(8,128)(2,1)S(1)} %get-tuple-element.57), channel_id=1, source_target_pairs={{0,3},{1,0},{2,1},{3,2},{4,7},{5,4},{6,5},{7,6},{8,11},{9,8},{10,9... | collective-permute-start | bytes 798728 | tf_op jit(solution)/shard_map/ppermute | solution.py:389
  65.4 13.6 %collective-permute-start.18 = (s16[528,128]{1,0:T(8,128)(2,1)S(1)}, s16[528,128]{1,0:T(8,128)(2,1)S(1)}, u32[]{:S(2)}, u32[]{:S(2)}) collective-permute-start(s16[528,128]{1,0:T(8,128)(2,1)S(1)} %get-tuple-element.63), channel_id=1, source_target_pairs={{0,1},{1,2},{2,3},{3,0},{4,5},{5,6},{6,7},{7,4},{8,9},{9,10},{10,1... | collective-permute-start | bytes 405512 | tf_op jit(solution)/shard_map/ppermute | solution.py:389
  68.7 11.7 %collective-permute-start.19 = (s16[528,128]{1,0:T(8,128)(2,1)S(1)}, s16[528,128]{1,0:T(8,128)(2,1)S(1)}, u32[]{:S(2)}, u32[]{:S(2)}) collective-permute-start(s16[528,128]{1,0:T(8,128)(2,1)S(1)} %get-tuple-element.64), channel_id=1, source_target_pairs={{0,2},{1,3},{2,0},{3,1},{4,6},{5,7},{6,4},{7,5},{8,10},{9,11},{10,... | collective-permute-start | bytes 405512 | tf_op jit(solution)/shard_map/ppermute | solution.py:389
  68.9 11.5 %collective-permute-start.20 = (s16[528,128]{1,0:T(8,128)(2,1)S(1)}, s16[528,128]{1,0:T(8,128)(2,1)S(1)}, u32[]{:S(2)}, u32[]{:S(2)}) collective-permute-start(s16[528,128]{1,0:T(8,128)(2,1)S(1)} %get-tuple-element.65), channel_id=1, source_target_pairs={{0,3},{1,0},{2,1},{3,2},{4,7},{5,4},{6,5},{7,6},{8,11},{9,8},{10,9... | collective-permute-start | bytes 405512 | tf_op jit(solution)/shard_map/ppermute | solution.py:389
  70.5 22.6 %copy-start = (s32[32,32]{1,0:T(8,128)S(1)}, s32[32,32]{1,0:T(8,128)}, u32[]{:S(2)}) copy-start(s32[32,32]{1,0:T(8,128)} %mask_ref.1) | copy-start | bytes 12292
  70.5 22.6 %copy-start.1 = (s32[8,32]{1,0:T(8,128)S(1)}, s32[8,32]{1,0:T(8,128)}, u32[]{:S(2)}) copy-start(s32[8,32]{1,0:T(8,128)} %refs_1_.1) | copy-start | bytes 3076
  75.1 6.9 %collective-permute-start.21 = (s16[528,128]{1,0:T(8,128)(2,1)S(1)}, s16[528,128]{1,0:T(8,128)(2,1)S(1)}, u32[]{:S(2)}, u32[]{:S(2)}) collective-permute-start(s16[528,128]{1,0:T(8,128)(2,1)S(1)} %get-tuple-element.69), channel_id=1, source_target_pairs={{0,1},{1,2},{2,3},{3,0},{4,5},{5,6},{6,7},{7,4},{8,9},{9,10},{10,1... | collective-permute-start | bytes 405512 | tf_op jit(solution)/shard_map/ppermute | solution.py:389
  76.8 7.2 %collective-permute-start.22 = (s16[528,128]{1,0:T(8,128)(2,1)S(1)}, s16[528,128]{1,0:T(8,128)(2,1)S(1)}, u32[]{:S(2)}, u32[]{:S(2)}) collective-permute-start(s16[528,128]{1,0:T(8,128)(2,1)S(1)} %get-tuple-element.70), channel_id=1, source_target_pairs={{0,2},{1,3},{2,0},{3,1},{4,6},{5,7},{6,4},{7,5},{8,10},{9,11},{10,... | collective-permute-start | bytes 405512 | tf_op jit(solution)/shard_map/ppermute | solution.py:389
  78.9 6.5 %collective-permute-start.23 = (s16[528,128]{1,0:T(8,128)(2,1)S(1)}, s16[528,128]{1,0:T(8,128)(2,1)S(1)}, u32[]{:S(2)}, u32[]{:S(2)}) collective-permute-start(s16[528,128]{1,0:T(8,128)(2,1)S(1)} %get-tuple-element.71), channel_id=1, source_target_pairs={{0,3},{1,0},{2,1},{3,2},{4,7},{5,4},{6,5},{7,6},{8,11},{9,8},{10,9... | collective-permute-start | bytes 405512 | tf_op jit(solution)/shard_map/ppermute | solution.py:389
  81.3 5.7 %collective-permute-start.24 = (s16[528,128]{1,0:T(8,128)(2,1)S(1)}, s16[528,128]{1,0:T(8,128)(2,1)S(1)}, u32[]{:S(2)}, u32[]{:S(2)}) collective-permute-start(s16[528,128]{1,0:T(8,128)(2,1)S(1)} %shard_map.74), channel_id=1, source_target_pairs={{0,4},{4,0},{1,5},{5,1},{2,6},{6,2},{3,7},{7,3},{8,12},{12,8},{9,1... | collective-permute-start | bytes 405512 | tf_op jit(solution)/shard_map/ppermute | solution.py:28
  86.4 5.1 %collective-permute-start.25 = (s16[528,128]{1,0:T(8,128)(2,1)S(1)}, s16[528,128]{1,0:T(8,128)(2,1)S(1)}, u32[]{:S(2)}, u32[]{:S(2)}) collective-permute-start(s16[528,128]{1,0:T(8,128)(2,1)S(1)} %shard_map.73.sent_ref), channel_id=1, source_target_pairs={{0,4},{4,0},{1,5},{5,1},{2,6},{6,2},{3,7},{7,3},{8,12},{12,8},{9,1... | collective-permute-start | bytes 405512 | tf_op jit(solution)/shard_map/ppermute | solution.py:28
  93.4 0.7 copy-start.2
